TPU v7x, 32 devices: a whole 2x2x4 slice. The times are simulated.
32 devices in a mesh: rep: 4 (over z), shard: 4 (over x, core), tp: 2 (over y).
Axes of the slice: x: 2, y: 2, z: 4, core: 2. Of those that a mesh axis runs over, the one named last changes fastest.
Arguments:
- delta_inputs: bfloat16 [4, 2, 768, 2304], P('rep', None, 'shard', 'tp'), may hold values from -6 to 6
- delta_mixing: bfloat16 [4, 2, 768, 768], P('rep', None, 'shard', 'tp'), may hold values from -6 to 6
- delta_expand: bfloat16 [4, 2, 768, 3072], P('rep', None, 'shard', 'tp'), may hold values from -6 to 6
- delta_reduce: bfloat16 [4, 2, 3072, 768], P('rep', None, 'shard', 'tp'), may hold values from -6 to 6
- owner_weights: float32 [4, 4, 2, 442368], P('rep', 'shard', 'tp'), may hold values from -6 to 6
- owner_momentum: float32 [4, 4, 2, 442368], P('rep', 'shard', 'tp'), may hold values from -6 to 6
- delta_embed: bfloat16 [4, 50304, 768], P('rep', 'shard', 'tp'), may hold values from -6 to 6
- embed_owner: float32 [4, 4, 3144, 768], P('shard', 'rep', None, 'tp'), may hold values from -6 to 6
- embed_momentum: float32 [4, 4, 3144, 64], P('shard', 'rep'), may hold values from -6 to 6
- basis: float32 [768, 64], P('tp'), may hold values from -0.21875 to 0.21875
Outputs:
- fresh_inputs: bfloat16 [2, 768, 2304], P(None, 'shard', 'tp')
- fresh_mixing: bfloat16 [2, 768, 768], P(None, 'shard', 'tp')
- fresh_expand: bfloat16 [2, 768, 3072], P(None, 'shard', 'tp')
- fresh_reduce: bfloat16 [2, 3072, 768], P(None, 'shard', 'tp')
- next_weights: float32 [4, 4, 2, 442368], P('rep', 'shard', 'tp')
- next_momentum: float32 [4, 4, 2, 442368], P('rep', 'shard', 'tp')
- fresh_embed: bfloat16 [50304, 768], P('shard', 'tp')
- next_embed: float32 [4, 4, 3144, 768], P('shard', 'rep', None, 'tp')
- next_embed_momentum: float32 [4, 4, 3144, 64], P('shard', 'rep')
All inputs are finite; a program needn't handle non-finite values.
Results may differ from a plain program's by a relative error of at most 0.0085.
Values may be sent and summed in bfloat16 or wider, within the bound.
No kernel may reach another device: no remote copies, remote signals or barrier semaphores. Data moves between devices by JAX's collectives and lax.ppermute only.
A program may use at most 128 MiB of HBM per device.

v0:
```python
import jax
import jax.numpy as jnp
from jax import lax
from jax.sharding import PartitionSpec as P

MOMENTUM = 0.5
OUTER_RATE = 0.7


def local(
    delta_inputs,
    delta_mixing,
    delta_expand,
    delta_reduce,
    owner_weights,
    owner_momentum,
    delta_embed,
    embed_owner,
    embed_momentum,
    basis,
):
    groups = lax.axis_size("rep")
    deltas = (delta_inputs, delta_mixing, delta_expand, delta_reduce)
    blocks = []
    for delta in deltas:
        layers, rows, cols = (delta.shape[1], delta.shape[2], delta.shape[3])
        blocks.append(delta.reshape(layers, groups, rows // groups, cols))
    moved = (
        lax.all_to_all(
            lax.all_to_all(blocks[0], "rep", split_axis=1, concat_axis=1, tiled=True),
            "shard",
            split_axis=3,
            concat_axis=3,
            tiled=True,
        ),
        lax.all_to_all(
            lax.all_to_all(blocks[1], "rep", split_axis=1, concat_axis=1, tiled=True),
            "shard",
            split_axis=3,
            concat_axis=3,
            tiled=True,
        ),
        lax.all_to_all(
            lax.all_to_all(blocks[2], "rep", split_axis=1, concat_axis=1, tiled=True),
            "shard",
            split_axis=3,
            concat_axis=3,
            tiled=True,
        ),
        lax.all_to_all(
            lax.all_to_all(blocks[3], "rep", split_axis=1, concat_axis=1, tiled=True),
            "shard",
            split_axis=3,
            concat_axis=3,
            tiled=True,
        ),
    )
    means = [jnp.sum(part, axis=1, dtype=jnp.float32) / groups for part in moved]
    gradient = jnp.concatenate([part.reshape(-1) for part in means]).reshape(owner_weights.shape)
    next_momentum = MOMENTUM * owner_momentum + gradient
    next_weights = owner_weights - OUTER_RATE * (gradient + MOMENTUM * next_momentum)
    copies = next_weights.astype(jnp.bfloat16).reshape(-1)
    parts = []
    offset = 0
    for delta in deltas:
        layers, rows, cols = (delta.shape[1], delta.shape[2], delta.shape[3])
        count = layers * (rows // groups) * cols
        parts.append(copies[offset : offset + count].reshape(layers, 1, rows // groups, cols))
        offset = offset + count
    placed_back = (
        lax.all_to_all(parts[0], "shard", split_axis=3, concat_axis=3, tiled=True),
        lax.all_to_all(parts[1], "shard", split_axis=3, concat_axis=3, tiled=True),
        lax.all_to_all(parts[2], "shard", split_axis=3, concat_axis=3, tiled=True),
        lax.all_to_all(parts[3], "shard", split_axis=3, concat_axis=3, tiled=True),
    )
    whole = (
        lax.all_gather(placed_back[0], "rep", axis=1, tiled=True),
        lax.all_gather(placed_back[1], "rep", axis=1, tiled=True),
        lax.all_gather(placed_back[2], "rep", axis=1, tiled=True),
        lax.all_gather(placed_back[3], "rep", axis=1, tiled=True),
    )
    fresh = [
        part.reshape(part.shape[0], part.shape[1] * part.shape[2], part.shape[3]) for part in whole
    ]
    vocab_rows, width_half = (delta_embed.shape[1], delta_embed.shape[2])
    owned_rows = vocab_rows // groups
    embed_block = delta_embed.reshape(groups, owned_rows, width_half).astype(jnp.float32)
    embed_summed = lax.psum_scatter(
        embed_block.astype(jnp.bfloat16), "rep", scatter_dimension=0, tiled=True
    ).astype(jnp.float32)
    partial_value = jnp.dot(
        embed_summed[0], basis, precision=lax.Precision.HIGHEST, preferred_element_type=jnp.float32
    )
    coefficients = lax.psum(partial_value.astype(jnp.bfloat16), "tp").astype(jnp.float32) / groups
    next_embed_momentum = MOMENTUM * embed_momentum + coefficients[None, None]
    direction = coefficients + MOMENTUM * next_embed_momentum[0, 0]
    update = jnp.dot(
        direction, basis.T, precision=lax.Precision.HIGHEST, preferred_element_type=jnp.float32
    )
    next_embed = embed_owner - OUTER_RATE * update[None, None]
    fresh_embed = lax.all_gather(next_embed[0, 0].astype(jnp.bfloat16), "rep", axis=0, tiled=True)
    return (
        fresh[0],
        fresh[1],
        fresh[2],
        fresh[3],
        next_weights,
        next_momentum,
        fresh_embed,
        next_embed,
        next_embed_momentum,
    )


def solution(mesh):
    in_specs = (
        P("rep", None, "shard", "tp"),
        P("rep", None, "shard", "tp"),
        P("rep", None, "shard", "tp"),
        P("rep", None, "shard", "tp"),
        P("rep", "shard", "tp", None),
        P("rep", "shard", "tp", None),
        P("rep", "shard", "tp"),
        P("shard", "rep", None, "tp"),
        P("shard", "rep", None, None),
        P("tp", None),
    )
    out_specs = (
        P(None, "shard", "tp"),
        P(None, "shard", "tp"),
        P(None, "shard", "tp"),
        P(None, "shard", "tp"),
        P("rep", "shard", "tp", None),
        P("rep", "shard", "tp", None),
        P("shard", "tp"),
        P("shard", "rep", None, "tp"),
        P("shard", "rep", None, None),
    )
    return jax.shard_map(local, mesh=mesh, in_specs=in_specs, out_specs=out_specs, check_vma=False)
```

profile of v0, /device:TPU:0, one launch (start us, length us, event | category | flops | bytes accessed | tf_op | source)
XLA Modules:
  0.0 614.2 jit_solution(2067487020716261676)
XLA Ops:
  8.2 15.8 %all_to_all.60 = bf16[2,4,48,384]{3,2,0,1:T(8,128)(2,1)S(1)} all-to-all(bf16[2,4,48,384]{3,2,0,1:T(8,128)(2,1)S(1)} %copy.98), channel_id=1, replica_groups=mesh['rep'=4,'shard'=4,'tp'=2] {'rep'}, dimensions={1} | all-to-all | bytes 589824 | tf_op jit(solution)/shard_map/all_to_all | solution.py:37
  31.3 5.4 all-to-all-done.3
  41.3 21.1 %all-to-all-done = bf16[2,4,48,1152]{3,2,0,1:T(8,128)(2,1)S(1)} async-done(((bf16[2,4,48,1152]{3,2,0,1:T(8,128)(2,1)}), bf16[2,4,48,1152]{3,2,0,1:T(8,128)(2,1)S(1)}, u32[]{:S(2)}, u32[]{:S(2)}) %all-to-all-start) | async-done | bytes 884768 | tf_op jit(solution)/shard_map/all_to_all | solution.py:30
  62.4 3.5 all-to-all-start.4
  67.1 26.9 %all-to-all-done.4 = bf16[2,4,48,1536]{3,2,0,1:T(8,128)(2,1)S(1)} async-done(((bf16[2,4,48,1536]{3,2,0,1:T(8,128)(2,1)}), bf16[2,4,48,1536]{3,2,0,1:T(8,128)(2,1)S(1)}, u32[]{:S(2)}, u32[]{:S(2)}) %all-to-all-start.4) | async-done | bytes 1179680 | tf_op jit(solution)/shard_map/all_to_all | solution.py:44
  95.0 4.3 all-to-all-start.6
  101.8 4.6 reshape.113
  106.4 20.9 %all-to-all-done.6 = bf16[2,4,192,384]{3,2,0,1:T(8,128)(2,1)} async-done(((bf16[2,4,192,384]{3,2,0,1:T(8,128)(2,1)}), bf16[2,4,192,384]{3,2,0,1:T(8,128)(2,1)}, u32[]{:S(2)}, u32[]{:S(2)}) %all-to-all-start.6) | async-done | bytes 1179680 | tf_op jit(solution)/shard_map/all_to_all | solution.py:51
  130.8 3.8 copy.105
  134.6 8.9 %all-to-all-done.1 = bf16[4,2,55296]{2,1,0:T(2,128)(2,1)S(1)} async-done(((bf16[4,2,55296]{2,1,0:T(2,128)(2,1)}), bf16[4,2,55296]{2,1,0:T(2,128)(2,1)S(1)}, u32[]{:S(2)}, u32[]{:S(2)}) %all-to-all-start.1) | async-done | bytes 884768 | tf_op jit(solution)/shard_map/all_to_all | solution.py:29
  143.5 4.4 all-to-all-start.7
  151.7 4.2 copy.102
  155.8 6.0 reshape.109
  161.9 3.6 reshape.114
  165.4 4.9 convert_reduce_fusion.1
  172.0 4.3 all-to-all-start.5
  177.3 4.0 convert_reduce_fusion.2
  183.1 9.2 %all-to-all-done.5 = bf16[4,2,73728]{2,1,0:T(2,128)(2,1)} async-done(((bf16[4,2,73728]{2,1,0:T(2,128)(2,1)}), bf16[4,2,73728]{2,1,0:T(2,128)(2,1)}, u32[]{:S(2)}, u32[]{:S(2)}) %all-to-all-start.5) | async-done | bytes 1179680 | tf_op jit(solution)/shard_map/all_to_all | solution.py:43
  192.2 4.2 reshape.110
  196.4 6.4 %convert_reduce_fusion = f32[2,48,1536]{1,0,2:T(2,128)} fusion(bf16[1536,2,4,48]{3,2,1,0:T(4,128)(2,1)S(1)} %reshape.110), kind=kLoop, calls=%fused_computation | loop fusion | flops 1032192 | bytes 1769472 | tf_op jit(solution)/shard_map/reduce_sum | solution.py:58
  207.4 5.8 fusion.8
  213.3 102.6 %reduce-scatter.4.cloned.1.call-done = bf16[1,3144,384]{2,1,0:T(8,128)(2,1)} async-done(((bf16[4,3144,384]{2,1,0:T(8,128)(2,1)}), bf16[1,3144,384]{2,1,0:T(8,128)(2,1)}) %reduce-scatter.4.cloned.1.call-update) | async-done | bytes 2414608
  315.9 4.8 convolution_convert_fusion
  321.0 6.3 %slice_reduce_fusion = (bf16[147456]{0:T(1024)(128)(2,1)S(1)}, bf16[147456]{0:T(1024)(128)(2,1)S(1)}) fusion(bf16[1,1,1,442368]{3,2,1,0:T(2,128)(2,1)S(1)} %get-tuple-element.11), kind=kLoop, calls=%fused_computation.16 | loop fusion | bytes 1179648 | tf_op jit(solution)/shard_map/slice | solution.py:68
  328.2 10.0 %all_to_all.61 = bf16[2,1,192,384]{2,0,1,3:T(2,128)(2,1)S(1)} all-to-all(bf16[2,1,192,384]{2,0,1,3:T(2,128)(2,1)S(1)} %copy.116), channel_id=1, replica_groups=mesh['rep'=4,'shard'=4,'tp'=2] {'shard'}, dimensions={3} | all-to-all | bytes 589824 | tf_op jit(solution)/shard_map/all_to_all | solution.py:74
  341.7 8.8 %all_to_all.62 = bf16[4,2,18432]{2,1,0:T(2,128)(2,1)S(1)} all-to-all(bf16[4,2,18432]{2,1,0:T(2,128)(2,1)S(1)} %reshape.119), channel_id=1, replica_groups=mesh['rep'=4,'shard'=4,'tp'=2] {'shard'}, dimensions={0} | all-to-all | bytes 589824 | tf_op jit(solution)/shard_map/all_to_all | solution.py:73
  354.2 8.6 %fusion.9 = (bf16[1,1,3144,384]{3,2,1,0:T(8,128)(2,1)}, f32[1,1,3144,384]{3,2,1,0:T(8,128)}) fusion(f32[1,1,3144,384]{3,2,1,0:T(8,128)} %param.17, f32[384,64]{0,1:T(8,128)S(1)} %copy-done, f32[1,1,3144,64]{2,3,1,0:T(8,128)S(1)} %bitcast_add_fusion.2, bf16[3144,64]{0,1:T(8,128)(2,1)S(1)} %copy-done.8), kind=kOutput, calls=%fused_computation.29 | convolution fusion | flops 931630080 | bytes 13378560 | tf_op jit(solution)/shard_map/dot_general | solution.py:97
  364.4 3.5 all-to-all-start.9
  375.8 15.1 %all_gather.16 = bf16[2,4,48,384]{3,2,0,1:T(8,128)(2,1)S(1)} all-gather(bf16[2,1,48,384]{3,2,0,1:T(8,128)(2,1)S(1)} %copy.111), channel_id=1, replica_groups=mesh['rep'=4,'shard'=4,'tp'=2] {'rep'}, dimensions={1}, use_global_device_ids=true | all-gather | bytes 368640 | tf_op jit(solution)/shard_map/all_gather | solution.py:78
  392.9 32.5 %all_gather.15 = bf16[2,4,48,1152]{3,2,0,1:T(8,128)(2,1)S(1)} all-gather(bf16[2,1,48,1152]{3,2,0,1:T(8,128)(2,1)S(1)} %copy.108), channel_id=1, replica_groups=mesh['rep'=4,'shard'=4,'tp'=2] {'rep'}, dimensions={1}, use_global_device_ids=true | all-gather | bytes 1105920 | tf_op jit(solution)/shard_map/all_gather | solution.py:77
  431.1 166.8 %all-gather.9.cloned.1.call-done = bf16[1,1,12576,384]{3,2,1,0:T(8,128)(2,1)} async-done(((bf16[1,1,3144,384]{3,2,1,0:T(8,128)(2,1)}), bf16[1,1,12576,384]{3,2,1,0:T(8,128)(2,1)}) %all-gather.9.cloned.1.call-update) | async-done | bytes 9658384 | tf_op jit(solution)/shard_map/all_gather | solution.py:101
  597.9 9.4 %copy.121 = bf16[12576,384]{1,0:T(8,128)(2,1)} copy(bf16[12576,384]{1,0:T(8,128)(2,1)} %bitcast.45) | data formatting | bytes 19316736
  (97 shorter events, 59.2 us)
Async XLA Ops:
  7.2 308.7 %copy-start = (f32[384,64]{0,1:T(8,128)S(1)}, f32[384,64]{0,1:T(8,128)}, u32[]{:S(2)}) copy-start(f32[384,64]{0,1:T(8,128)} %param.19) | copy-start | bytes 294916
  8.2 22.1 %copy-start.13 = (bf16[1,2,192,1152]{3,2,1,0:T(8,128)(2,1)S(1)}, bf16[1,2,192,1152]{3,2,1,0:T(8,128)(2,1)}, u32[]{:S(2)}) copy-start(bf16[1,2,192,1152]{3,2,1,0:T(8,128)(2,1)} %param.10) | copy-start | bytes 2654212
  26.8 9.8 %all-to-all-start.3 = ((bf16[4,2,18432]{2,1,0:T(2,128)(2,1)}), bf16[4,2,18432]{2,1,0:T(2,128)(2,1)S(1)}, u32[]{:S(2)}, u32[]{:S(2)}) async-start(bf16[4,2,18432]{2,1,0:T(2,128)(2,1)} %reshape.111), calls=%async_computation.3 | async-start | bytes 589824 | tf_op jit(solution)/shard_map/all_to_all | solution.py:36
  30.3 9.9 %copy-start.9 = (bf16[1,2,192,1536]{3,2,1,0:T(8,128)(2,1)S(1)}, bf16[1,2,192,1536]{3,2,1,0:T(8,128)(2,1)}, u32[]{:S(2)}) copy-start(bf16[1,2,192,1536]{3,2,1,0:T(8,128)(2,1)} %param.12) | copy-start | bytes 3538948
  36.6 3.5 copy-start.11
  36.6 25.8 %all-to-all-start = ((bf16[2,4,48,1152]{3,2,0,1:T(8,128)(2,1)}), bf16[2,4,48,1152]{3,2,0,1:T(8,128)(2,1)S(1)}, u32[]{:S(2)}, u32[]{:S(2)}) async-start(bf16[2,4,48,1152]{3,2,0,1:T(8,128)(2,1)} %copy.95), calls=%async_computation | async-start | bytes 1769472 | tf_op jit(solution)/shard_map/all_to_all | solution.py:30
  41.3 24.7 %copy-start.10 = (bf16[1,2,768,384]{3,2,1,0:T(8,128)(2,1)S(1)}, bf16[1,2,768,384]{3,2,1,0:T(8,128)(2,1)}, u32[]{:S(2)}) copy-start(bf16[1,2,768,384]{3,2,1,0:T(8,128)(2,1)} %param.13) | copy-start | bytes 3538948
  62.4 31.5 %all-to-all-start.4 = ((bf16[2,4,48,1536]{3,2,0,1:T(8,128)(2,1)}), bf16[2,4,48,1536]{3,2,0,1:T(8,128)(2,1)S(1)}, u32[]{:S(2)}, u32[]{:S(2)}) async-start(bf16[2,4,48,1536]{3,2,0,1:T(8,128)(2,1)} %copy.101), calls=%async_computation.4 | async-start | bytes 2359296 | tf_op jit(solution)/shard_map/all_to_all | solution.py:44
  94.0 1.0 copy-start.1
  95.0 32.4 %all-to-all-start.6 = ((bf16[2,4,192,384]{3,2,0,1:T(8,128)(2,1)}), bf16[2,4,192,384]{3,2,0,1:T(8,128)(2,1)}, u32[]{:S(2)}, u32[]{:S(2)}) async-start(bf16[2,4,192,384]{3,2,0,1:T(8,128)(2,1)} %copy.104), calls=%async_computation.6 | async-start | bytes 2359296 | tf_op jit(solution)/shard_map/all_to_all | solution.py:51
  127.3 16.2 %all-to-all-start.1 = ((bf16[4,2,55296]{2,1,0:T(2,128)(2,1)}), bf16[4,2,55296]{2,1,0:T(2,128)(2,1)S(1)}, u32[]{:S(2)}, u32[]{:S(2)}) async-start(bf16[4,2,55296]{2,1,0:T(2,128)(2,1)} %reshape.113), calls=%async_computation.1 | async-start | bytes 1769472 | tf_op jit(solution)/shard_map/all_to_all | solution.py:29
  143.5 5.1 copy-start.2
  143.5 28.5 %all-to-all-start.7 = ((bf16[2,4,192,384]{2,1,0,3:T(4,128)(2,1)}), bf16[2,4,192,384]{2,1,0,3:T(4,128)(2,1)}, u32[]{:S(2)}, u32[]{:S(2)}) async-start(bf16[2,4,192,384]{2,1,0,3:T(4,128)(2,1)} %copy.105), calls=%async_computation.7 | async-start | bytes 3145728 | tf_op jit(solution)/shard_map/all_to_all | solution.py:50
  147.9 168.0 %reduce-scatter.4.cloned.1.call-start = ((), (), s32[]{:S(2)}) async-start(), calls=%async_computation.17 | async-start | bytes 12072960
  148.5 1.0 copy-start.12
  172.0 20.2 %all-to-all-start.5 = ((bf16[4,2,73728]{2,1,0:T(2,128)(2,1)}), bf16[4,2,73728]{2,1,0:T(2,128)(2,1)}, u32[]{:S(2)}, u32[]{:S(2)}) async-start(bf16[4,2,73728]{2,1,0:T(2,128)(2,1)} %reshape.109), calls=%async_computation.5 | async-start | bytes 2359296 | tf_op jit(solution)/shard_map/all_to_all | solution.py:43
  176.3 176.7 %all-reduce.3.cloned.1.call-start = ((), (), s32[]{:S(2)}) async-start(), calls=%async_computation.15 | async-start | bytes 819200 | tf_op jit(solution)/shard_map/psum | solution.py:94
  202.8 2.6 copy-start.4
  202.8 2.7 copy-start.5
  205.4 1.5 copy-start.6
  205.4 2.0 copy-start.7
  320.7 105.7 %all-gather.7.cloned.1.call-start = ((), (), s32[]{:S(2)}) async-start(), calls=%async_computation.14 | async-start | bytes 1474560 | tf_op jit(solution)/shard_map/all_gather | solution.py:80
  339.4 89.4 %all-gather.5.cloned.1.call-start = ((), (), s32[]{:S(2)}) async-start(), calls=%async_computation.13 | async-start | bytes 1474560 | tf_op jit(solution)/shard_map/all_gather | solution.py:79
  351.2 1.7 copy-start.14
  352.9 245.0 %all-gather.9.cloned.1.call-start = ((), (), s32[]{:S(2)}) async-start(), calls=%async_computation.16 | async-start | bytes 12072960 | tf_op jit(solution)/shard_map/all_gather | solution.py:101
  353.0 1.2 copy-start.8
  354.2 8.6 %copy-start.3 = (f32[1,1,3144,64]{2,3,1,0:T(8,128)}, f32[1,1,3144,64]{2,3,1,0:T(8,128)S(1)}, u32[]{:S(2)}) copy-start(f32[1,1,3144,64]{2,3,1,0:T(8,128)S(1)} %bitcast_add_fusion.2) | copy-start | bytes 2414596
  364.4 7.7 %all-to-all-start.9 = ((bf16[4,2,4608]{2,1,0:T(2,128)(2,1)}), bf16[4,2,4608]{2,1,0:T(2,128)(2,1)S(1)}, u32[]{:S(2)}, u32[]{:S(2)}) async-start(bf16[4,2,4608]{2,1,0:T(2,128)(2,1)} %reshape.117), calls=%async_computation.9 | async-start | bytes 147456 | tf_op jit(solution)/shard_map/all_to_all | solution.py:72
  372.1 19.6 %all-to-all-start.8 = ((bf16[4,2,13824]{2,1,0:T(2,128)(2,1)}), bf16[4,2,13824]{2,1,0:T(2,128)(2,1)S(1)}, u32[]{:S(2)}, u32[]{:S(2)}) async-start(bf16[4,2,13824]{2,1,0:T(2,128)(2,1)} %reshape.115), calls=%async_computation.8 | async-start | bytes 442368 | tf_op jit(solution)/shard_map/all_to_all | solution.py:71
Sparse Core Ops, SparseCore 0:
  151.1 164.6 reduce-scatter.3
  320.8 26.8 all-reduce.2
  350.0 30.4 all-gather.6
  382.5 43.8 all-gather.4
  428.4 169.4 all-gather.8
where the time goes:
time: 620 us; the launch traced here: 614 us
  waiting for transfers between devices  362 us (58%)
  local copies, waits for them, and re-layouts  83.1 us (13%)
  blocking collectives  82.1 us (13%)
  starting transfers between devices  34.9 us (6%)
  other arithmetic  23.9 us (4%)
  between operations  14.6 us (2%)
  matrix products  13.4 us (2%)
    all_gather x1, waiting for transfers between devices, local(): lax.all_gather(next_embed[0, 0].astype(jnp.bfloat16), 'rep', axis=0, tile...  167 us
    unnamed x6, waiting for transfers between devices  103 us
    unnamed x43, local copies, waits for them, and re-layouts  39.8 us
    all_gather x1, blocking collectives, local(): lax.all_gather(placed_back[0], 'rep', axis=1, tiled=True)  32.5 us
    all_to_all x1, waiting for transfers between devices, local(): lax.all_to_all(blocks[2], 'rep', split_axis=1, concat_axis=1, tiled=True)  26.9 us
    all_to_all x1, waiting for transfers between devices, local(): lax.all_to_all(blocks[0], 'rep', split_axis=1, concat_axis=1, tiled=True)  21.1 us
    all_to_all x1, waiting for transfers between devices, local(): lax.all_to_all(blocks[3], 'rep', split_axis=1, concat_axis=1, tiled=True)  20.9 us
    reduce_sum x4, other arithmetic, local(): jnp.sum(part, axis=1, dtype=jnp.float32) / groups  16.6 us
  transfers between devices with their start and end apart: 14, of which 9 were waited for; matrix products, arithmetic and copies ran while one was open for 16% of the time, Pallas kernels for 0%

commit v1 on v0

v1 whole, which is shorter than its diff:
```python
import jax
import jax.numpy as jnp
from jax import lax
from jax.sharding import PartitionSpec as P

MOMENTUM = 0.5
OUTER_RATE = 0.7

OUT_IN = [(0, 1), (3, 2)]
MIDDLE = [(1, 2), (2, 1)]
IN_OUT = [(1, 0), (2, 3)]


def permute(value, pairs):
    return lax.ppermute(value, "rep", pairs)


def block_of(place):
    rank = lax.axis_index("rep")
    return jnp.where(rank >= 2, 3 - place, place)


def line_sum(own):
    wide = lambda value: value.astype(jnp.float32)
    add = lambda one, two: (wide(one) + wide(two)).astype(one.dtype)
    far, middle, near, last = (own(block_of(place)) for place in (3, 2, 1, 0))
    far_in = permute(far, OUT_IN)
    middle_in = permute(middle, OUT_IN)
    near_in = permute(near, OUT_IN)
    far_across = permute(add(far, far_in), MIDDLE)
    middle_across = permute(add(middle, middle_in), MIDDLE)
    last_out = permute(add(last, far_across), IN_OUT)
    rank = lax.axis_index("rep")
    mine = jnp.where((rank == 0) | (rank == 3), last, near)
    return wide(mine) + wide(near_in) + wide(middle_across) + wide(last_out)


def line_gather(mine):
    rank = lax.axis_index("rep")
    end = (rank == 0) | (rank == 3)
    to_end = permute(mine, IN_OUT)
    across = permute(mine, MIDDLE)
    to_inner = permute(mine, OUT_IN)
    to_end_2 = permute(across, IN_OUT)
    across_2 = permute(to_inner, MIDDLE)
    to_end_3 = permute(across_2, IN_OUT)
    return [
        (rank, mine),
        (block_of(jnp.where(end, 1, 0)), jnp.where(end, to_end, to_inner)),
        (block_of(2), jnp.where(end, to_end_2, across)),
        (block_of(3), jnp.where(end, to_end_3, across_2)),
    ]


def local(
    delta_inputs,
    delta_mixing,
    delta_expand,
    delta_reduce,
    owner_weights,
    owner_momentum,
    delta_embed,
    embed_owner,
    embed_momentum,
    basis,
):
    groups = lax.axis_size("rep")
    shards = lax.axis_size("shard")
    deltas = (delta_inputs, delta_mixing, delta_expand, delta_reduce)
    layers = delta_inputs.shape[1]
    width = min(delta.shape[3] for delta in deltas)
    sub = min(delta.shape[2] for delta in deltas) // groups

    rows = embed_owner.shape[2]
    half_rank = basis.shape[1] // 2
    sent_rows = embed_owner[0, 0].astype(jnp.bfloat16)
    all_rows = lax.all_gather(sent_rows, "rep", axis=0, tiled=False)

    terms = lax.dot_general(
        basis,
        delta_embed[0].astype(jnp.float32),
        (((0,), (1,)), ((), ())),
        precision=lax.Precision.HIGH,
        preferred_element_type=jnp.float32,
    ).astype(jnp.bfloat16)
    side = lax.axis_index("tp")
    keep = lax.dynamic_slice_in_dim(terms, side * half_rank, half_rank, 0)
    give = lax.dynamic_slice_in_dim(terms, (1 - side) * half_rank, half_rank, 0)
    swap = [(0, 1), (1, 0)]
    taken = lax.ppermute(give, "tp", swap)
    kept = (keep.astype(jnp.float32) + taken.astype(jnp.float32)).astype(jnp.bfloat16)

    def dense_block(block):
        panels = []
        for delta in deltas:
            count = delta.shape[2] // groups
            part = lax.dynamic_slice_in_dim(delta[0], block * count, count, 1)
            part = part.reshape(layers, count // sub, sub, part.shape[2] // width, width)
            part = part.transpose(1, 3, 0, 2, 4)
            panels.append(part.reshape(-1, layers, sub, width))
        return jnp.concatenate(panels)

    def pieces(block):
        parts = []
        at = 0
        for delta in deltas:
            over = delta.shape[2] // groups // sub
            across = delta.shape[3] // width
            part = block[at : at + over * across].reshape(over, across, layers, sub, width)
            part = part.transpose(2, 0, 3, 1, 4).reshape(layers, over, sub, across * width)
            parts.append(part)
            at = at + over * across
        return parts

    summed = line_sum(dense_block).astype(jnp.bfloat16)
    sending = []
    for part in pieces(summed):
        over, cols = part.shape[1], part.shape[3]
        part = part.reshape(layers, over, sub, shards, cols // shards).transpose(3, 0, 2, 1, 4)
        sending.append(part.reshape(shards, layers, sub, over * cols // shards))
    moved = lax.all_to_all(jnp.concatenate(sending, axis=3), "shard", split_axis=0, concat_axis=0, tiled=True)
    at = 0
    flats = []
    for delta in deltas:
        over = delta.shape[2] // groups // sub
        piece = delta.shape[3] // shards
        part = moved[..., at : at + over * piece].reshape(shards, layers, sub, over, piece)
        flats.append(part.transpose(1, 3, 2, 0, 4).reshape(-1))
        at = at + over * piece
    gradient = (jnp.concatenate(flats).astype(jnp.float32) / groups).reshape(owner_weights.shape)
    next_momentum = MOMENTUM * owner_momentum + gradient
    next_weights = owner_weights - OUTER_RATE * (gradient + MOMENTUM * next_momentum)
    copies = next_weights.astype(jnp.bfloat16).reshape(-1)
    returning = []
    offset = 0
    for delta in deltas:
        over = delta.shape[2] // groups // sub
        piece = delta.shape[3] // shards
        count = layers * over * sub * shards * piece
        part = copies[offset : offset + count].reshape(layers, over, sub, shards, piece)
        returning.append(part.transpose(3, 0, 2, 1, 4).reshape(shards, layers, sub, over * piece))
        offset = offset + count
    back = lax.all_to_all(jnp.concatenate(returning, axis=3), "shard", split_axis=0, concat_axis=0, tiled=True)
    at = 0
    panels = []
    for delta in deltas:
        over = delta.shape[2] // groups // sub
        piece = delta.shape[3] // shards
        part = back[..., at : at + over * piece].reshape(shards, layers, sub, over, piece)
        part = part.transpose(3, 1, 2, 0, 4).reshape(over, layers, sub, -1, width)
        panels.append(part.transpose(0, 3, 1, 2, 4).reshape(-1, layers, sub, width))
        at = at + over * piece
    fresh = [jnp.zeros(delta.shape[1:], jnp.bfloat16) for delta in deltas]
    for block, whole in line_gather(jnp.concatenate(panels)):
        for kind, part in enumerate(pieces(whole)):
            part = part.reshape(layers, -1, part.shape[3])
            fresh[kind] = lax.dynamic_update_slice_in_dim(fresh[kind], part, block * part.shape[1], 1)

    mine = line_sum(lambda block: lax.dynamic_slice_in_dim(kept, block * rows, rows, 1)) / groups
    sent = mine.astype(jnp.bfloat16)
    other = lax.ppermute(sent, "tp", swap)

    def both(one, two):
        return jnp.where(side == 0, jnp.concatenate([one, two]), jnp.concatenate([two, one]))

    coefficients = both(sent, other).astype(jnp.float32)
    next_embed_momentum = MOMENTUM * embed_momentum[0, 0].T + coefficients
    direction = coefficients + MOMENTUM * next_embed_momentum

    def update(toward, precision):
        return OUTER_RATE * lax.dot_general(
            toward, basis, (((0,), (1,)), ((), ())), precision=precision, preferred_element_type=jnp.float32
        )

    next_embed = embed_owner[0, 0] - update(direction, lax.Precision.HIGHEST)
    half = lax.dynamic_slice_in_dim(direction, side * half_rank, half_rank, 0).astype(jnp.bfloat16)
    gathered = line_gather(half)
    here = jnp.concatenate([part for _, part in gathered[1:]])
    there = lax.ppermute(here, "tp", swap)
    fresh_embed = jnp.zeros((groups * rows, embed_owner.shape[3]), jnp.bfloat16)
    fresh_embed = lax.dynamic_update_slice_in_dim(
        fresh_embed, next_embed.astype(jnp.bfloat16), gathered[0][0] * rows, 0
    )
    for place, (block, part) in enumerate(gathered[1:]):
        toward = both(part, there[place * half_rank : (place + 1) * half_rank]).astype(jnp.float32)
        old = lax.dynamic_index_in_dim(all_rows, block, 0, False)
        new = old.astype(jnp.float32) - update(toward, lax.Precision.DEFAULT)
        fresh_embed = lax.dynamic_update_slice_in_dim(fresh_embed, new.astype(jnp.bfloat16), block * rows, 0)
    return (
        fresh[0],
        fresh[1],
        fresh[2],
        fresh[3],
        next_weights,
        next_momentum,
        fresh_embed,
        next_embed[None, None],
        next_embed_momentum.T[None, None],
    )


def solution(mesh):
    in_specs = (
        P("rep", None, "shard", "tp"),
        P("rep", None, "shard", "tp"),
        P("rep", None, "shard", "tp"),
        P("rep", None, "shard", "tp"),
        P("rep", "shard", "tp", None),
        P("rep", "shard", "tp", None),
        P("rep", "shard", "tp"),
        P("shard", "rep", None, "tp"),
        P("shard", "rep", None, None),
        P("tp", None),
    )
    out_specs = (
        P(None, "shard", "tp"),
        P(None, "shard", "tp"),
        P(None, "shard", "tp"),
        P(None, "shard", "tp"),
        P("rep", "shard", "tp", None),
        P("rep", "shard", "tp", None),
        P("shard", "tp"),
        P("shard", "rep", None, "tp"),
        P("shard", "rep", None, None),
    )
    return jax.shard_map(local, mesh=mesh, in_specs=in_specs, out_specs=out_specs, check_vma=False)
```

time: 620 us -> 504 us (0.81)
  waiting for transfers between devices: 362 us -> 249 us
  blocking collectives: 82.1 us -> 0 us
  starting transfers between devices: 34.9 us -> 75.2 us
  other arithmetic: 23.9 us -> 44.5 us
  matrix products: 13.4 us -> 30.7 us
    ppermute x0 -> x27, waiting for transfers between devices: none -> 228 us  [the longest x24 225 us: permute(): return lax.ppermute(value, 'rep', pairs)]
    all_gather x3 -> x1, waiting for transfers between devices: 167 us -> 0.01 us  [local(): all_rows = lax.all_gather(sent_rows, 'rep', axis=0, tiled=False)]
    unnamed x6 -> x1, waiting for transfers between devices: 103 us -> 0.02 us
    all_to_all x9 -> x2, waiting for transfers between devices: 92.5 us -> 21.3 us  [the longest x1 11.9 us: local(): lax.all_to_all(jnp.concatenate(sending, axis=3), 'shard', split_axis=0, c...]
    ppermute x0 -> x27, starting transfers between devices: none -> 67.9 us  [the longest x24 57.5 us: permute(): return lax.ppermute(value, 'rep', pairs)]
    all_gather x2 -> x0, blocking collectives: 47.6 us -> none  [the longest x1 32.5 us: local(): lax.all_gather(placed_back[0], 'rep', axis=1, tiled=True)]
    all_to_all x3 -> x0, blocking collectives: 34.5 us -> none  [the longest x1 15.8 us: local(): lax.all_to_all(blocks[1], 'rep', split_axis=1, concat_axis=1, tiled=True)]
    unnamed x43 -> x98, local copies, waits for them, and re-layouts: 39.8 us -> 8.52 us
  transfers between devices with their start and end apart: 14 -> 30, of which waited for: 9 -> 12; matrix products, arithmetic and copies ran while one was open for 16% -> 25% of each run, Pallas kernels for 0% -> 0%
where the time goes in v1:
time: 504 us; the launch traced here: 496 us
  waiting for transfers between devices  249 us (49%)
  local copies, waits for them, and re-layouts  80.3 us (16%)
  starting transfers between devices  75.2 us (15%)
  other arithmetic  44.5 us (9%)
  matrix products  30.7 us (6%)
  between operations  15.9 us (3%)
    ppermute x24, waiting for transfers between devices, permute(): return lax.ppermute(value, 'rep', pairs)  225 us
    ppermute x24, starting transfers between devices, permute(): return lax.ppermute(value, 'rep', pairs)  57.5 us
    convert_element_type x1, other arithmetic, local(): copies = next_weights.astype(jnp.bfloat16).reshape(-1)  22.8 us
    dot_general x4, matrix products, update(): lax.dot_general(toward, basis, (((0,), (1,)), ((), ())), precision=precis...  20.8 us
    dynamic_update_slice x16, local copies, waits for them, and re-layouts, local(): lax.dynamic_update_slice_in_dim(fresh[kind], part, block * part.shape[1], 1)  13.3 us
    another operation x9, local copies, waits for them, and re-layouts, local(): part = part.reshape(layers, -1, part.shape[3])  12 us
    all_to_all x1, waiting for transfers between devices, local(): lax.all_to_all(jnp.concatenate(sending, axis=3), 'shard', split_axis=0, c...  11.9 us
    transpose x18, local copies, waits for them, and re-layouts, pieces(): part.transpose(2, 0, 3, 1, 4).reshape(layers, over, sub, across * width)  11.1 us
  transfers between devices with their start and end apart: 30, of which 12 were waited for; matrix products, arithmetic and copies ran while one was open for 25% of the time, Pallas kernels for 0%

profile of v1, /device:TPU:0, one launch (start us, length us, event | category | flops | bytes accessed | tf_op | source)
XLA Modules:
  0.0 495.7 jit_solution(2563561695617690420)
XLA Ops:
  8.1 9.9 %convolution_convert_fusion = bf16[64,12576]{1,0:T(8,128)(2,1)S(1)} fusion(f32[384,64]{0,1:T(8,128)S(1)} %copy-done, bf16[1,12576,384]{2,1,0:T(8,128)(2,1)} %param.16), kind=kOutput, calls=%fused_computation | convolution fusion | flops 1855211520 | bytes 11366400 | tf_op jit(solution)/shard_map/dot_general | solution.py:79
  18.9 3.0 collective-permute-start.12
  29.0 2.3 constant_dynamic-slice_fusion.12
  33.1 4.4 collective-permute-start.1
  42.7 4.5 collective-permute-start.16
  48.3 2.3 collective-permute-start.3
  52.0 2.3 collective-permute-start
  57.6 27.0 %collective-permute-done.16 = bf16[32,3144]{1,0:T(8,128)(2,1)} collective-permute-done((bf16[32,3144]{1,0:T(8,128)(2,1)}, bf16[32,3144]{1,0:T(8,128)(2,1)}, u32[]{:S(2)}, u32[]{:S(2)}) %collective-permute-start.16) | collective-permute-done | bytes 201248 | tf_op jit(solution)/shard_map/ppermute | solution.py:15
  84.6 4.4 collective-permute-start.13
  90.1 79.0 %collective-permute-done.14 = bf16[32,3144]{1,0:T(8,128)(2,1)S(1)} collective-permute-done((bf16[32,3144]{1,0:T(8,128)(2,1)S(1)}, bf16[32,3144]{1,0:T(8,128)(2,1)S(1)}, u32[]{:S(2)}, u32[]{:S(2)}) %collective-permute-start.14) | collective-permute-done | bytes 201248 | tf_op jit(solution)/shard_map/ppermute | solution.py:15
  173.7 3.8 collective-permute-done.13
  178.2 17.0 %collective-permute-done.18 = bf16[32,3144]{1,0:T(8,128)(2,1)S(1)} collective-permute-done((bf16[32,3144]{1,0:T(8,128)(2,1)S(1)}, bf16[32,3144]{1,0:T(8,128)(2,1)S(1)}, u32[]{:S(2)}, u32[]{:S(2)}) %collective-permute-start.18) | collective-permute-done | bytes 201248 | tf_op jit(solution)/shard_map/ppermute | solution.py:15
  195.5 6.1 %collective-permute-start.19 = (bf16[32,3144]{1,0:T(8,128)(2,1)S(1)}, bf16[32,3144]{1,0:T(8,128)(2,1)S(1)}, u32[]{:S(2)}, u32[]{:S(2)}) collective-permute-start(bf16[32,3144]{1,0:T(8,128)(2,1)S(1)} %multiply_convert_fusion), channel_id=1, source_target_pairs={{0,1},{1,0},{2,3},{3,2},{4,5},{5,4},{6,7},{7,6},{8,9},{9,8},{10,11... | collective-permute-start | bytes 603656 | tf_op jit(solution)/shard_map/ppermute | solution.py:161
  207.8 12.8 %collective-permute-start.21 = (bf16[32,3144]{1,0:T(8,128)(2,1)S(1)}, bf16[32,3144]{1,0:T(8,128)(2,1)S(1)}, u32[]{:S(2)}, u32[]{:S(2)}) collective-permute-start(bf16[32,3144]{1,0:T(8,128)(2,1)S(1)} %dynamic-slice_convert_fusion), channel_id=1, source_target_pairs={{0,8},{24,16},{1,9},{25,17},{2,10},{26,18},{3,11},{27,19},{4,12},{... | collective-permute-start | bytes 603656 | tf_op jit(solution)/shard_map/ppermute | solution.py:15
  221.5 8.0 %convert_dynamic-update-slice_fusion = (bf16[12576,384]{1,0:T(8,128)(2,1)S(1)}, f32[3144,384]{1,0:T(8,128)}) fusion(bf16[12576,384]{1,0:T(8,128)(2,1)S(1)} %broadcast_in_dim.25, s32[]{:T(128)S(6)} %select_n.212, f32[64,3144]{1,0:T(8,128)S(1)} %get-tuple-element.15, f32[384,64]{0,1:T(8,128)S(1)} %copy-done, f32[1,1,3144,384]{3,2,1,0:T(8,128)S(1)} %bitcast.263), kind=kOutput, calls=%fused_computation.16 | convolution fusion | flops 930825216 | bytes 12990468 | tf_op jit(solution)/shard_map/dot_general | solution.py:171
  229.5 3.8 copy-done.2
  240.4 70.7 %collective-permute-done.5 = bf16[12,2,48,384]{3,2,1,0:T(8,128)(2,1)S(1)} collective-permute-done((bf16[12,2,48,384]{3,2,1,0:T(8,128)(2,1)S(1)}, bf16[12,2,48,384]{3,2,1,0:T(8,128)(2,1)S(1)}, u32[]{:S(2)}, u32[]{:S(2)}) %collective-permute-start.5) | collective-permute-done | bytes 884768 | tf_op jit(solution)/shard_map/ppermute | solution.py:15
  315.8 3.7 all-to-all-start
  320.2 11.9 %all-to-all-done = bf16[4,2,48,1152]{3,2,1,0:T(8,128)(2,1)S(1)} async-done(((bf16[4,2,48,1152]{3,2,1,0:T(8,128)(2,1)}), bf16[4,2,48,1152]{3,2,1,0:T(8,128)(2,1)S(1)}, u32[]{:S(2)}, u32[]{:S(2)}) %all-to-all-start) | async-done | bytes 884768 | tf_op jit(solution)/shard_map/all_to_all | solution.py:121
  335.4 22.8 %fusion.37 = (bf16[1,1,1,442368]{3,2,1,0:T(2,128)(2,1)S(1)}, f32[1,1,1,442368]{3,2,1,0:T(1,128)}, f32[1,1,1,442368]{3,2,1,0:T(1,128)}) fusion(f32[1,1,1,442368]{3,2,1,0:T(1,128)} %param.14, f32[1,1,1,442368]{3,2,1,0:T(1,128)} %param.15, bf16[1,1,1,147456]{3,2,1,0:T(2,128)(2,1)S(1)} %concatenate.74, bf16[1,1,1,147456]{3,2,1,0:T(2,128)(2,1)S(1)} %concatenate.73, ...), kind=kLoop, calls=%fused_computation.147 | loop fusion | flops 7077888 | bytes 8847360 | tf_op jit(solution)/shard_map/convert_element_type | solution.py:133
  358.2 6.6 %slice_reduce_fusion = (bf16[147456]{0:T(1024)(128)(2,1)S(1)}, bf16[147456]{0:T(1024)(128)(2,1)S(1)}) fusion(bf16[1,1,1,442368]{3,2,1,0:T(2,128)(2,1)S(1)} %get-tuple-element.11), kind=kLoop, calls=%fused_computation.38 | loop fusion | bytes 1179648 | tf_op jit(solution)/shard_map/slice | solution.py:140
  370.5 3.5 all-to-all-start.1
  377.2 9.4 %all-to-all-done.1 = bf16[4,2,48,1152]{3,2,1,0:T(8,128)(2,1)S(1)} async-done(((bf16[4,2,48,1152]{3,2,1,0:T(8,128)(2,1)}), bf16[4,2,48,1152]{3,2,1,0:T(8,128)(2,1)S(1)}, u32[]{:S(2)}, u32[]{:S(2)}) %all-to-all-start.1) | async-done | bytes 884768 | tf_op jit(solution)/shard_map/all_to_all | solution.py:143
  390.9 6.4 %collective-permute-start.7 = (bf16[12,2,48,384]{3,2,1,0:T(8,128)(2,1)}, bf16[12,2,48,384]{3,2,1,0:T(8,128)(2,1)}, u32[]{:S(2)}, u32[]{:S(2)}) collective-permute-start(bf16[12,2,48,384]{3,2,1,0:T(8,128)(2,1)} %pad_maximum_fusion.4), channel_id=1, source_target_pairs={{0,8},{24,16},{1,9},{25,17},{2,10},{26,18},{3,11},{27,19},{4,12},{... | collective-permute-start | bytes 2654216 | tf_op jit(solution)/shard_map/ppermute | solution.py:15
  398.9 2.0 fusion.38
  405.7 9.5 %collective-permute-done.7 = bf16[12,2,48,384]{3,2,1,0:T(8,128)(2,1)} collective-permute-done((bf16[12,2,48,384]{3,2,1,0:T(8,128)(2,1)}, bf16[12,2,48,384]{3,2,1,0:T(8,128)(2,1)}, u32[]{:S(2)}, u32[]{:S(2)}) %collective-permute-start.7) | collective-permute-done | bytes 884768 | tf_op jit(solution)/shard_map/ppermute | solution.py:15
  431.7 7.8 %collective-permute-done.9 = bf16[12,2,48,384]{3,2,1,0:T(8,128)(2,1)} collective-permute-done((bf16[12,2,48,384]{3,2,1,0:T(8,128)(2,1)}, bf16[12,2,48,384]{3,2,1,0:T(8,128)(2,1)}, u32[]{:S(2)}, u32[]{:S(2)}) %collective-permute-start.9) | collective-permute-done | bytes 884768 | tf_op jit(solution)/shard_map/ppermute | solution.py:15
  452.9 10.5 %collective-permute-done.11 = bf16[12,2,48,384]{3,2,1,0:T(8,128)(2,1)} collective-permute-done((bf16[12,2,48,384]{3,2,1,0:T(8,128)(2,1)}, bf16[12,2,48,384]{3,2,1,0:T(8,128)(2,1)}, u32[]{:S(2)}, u32[]{:S(2)}) %collective-permute-start.11) | collective-permute-done | bytes 884768 | tf_op jit(solution)/shard_map/ppermute | solution.py:15
  473.7 1.9 constant_dynamic-update-slice_fusion.9
  475.6 4.4 fusion.10
  480.0 4.2 fusion.9
  484.2 4.1 fusion.8
  (278 shorter events, 109.7 us)
Async XLA Ops:
  7.2 468.4 %all-gather.3.cloned.1.call-start = ((), (), s32[]{:S(2)}) async-start(), calls=%async_computation.2 | async-start | bytes 12072960 | tf_op jit(solution)/shard_map/all_gather | solution.py:77
  18.9 21.3 %collective-permute-start.12 = (bf16[32,12576]{1,0:T(8,128)(2,1)}, bf16[32,12576]{1,0:T(8,128)(2,1)}, u32[]{:S(2)}, u32[]{:S(2)}) collective-permute-start(bf16[32,12576]{1,0:T(8,128)(2,1)} %constant_dynamic-slice_fusion.3), channel_id=1, source_target_pairs={{0,1},{1,0},{2,3},{3,2},{4,5},{5,4},{6,7},{7,6},{8,9},{9,8},{10,11... | collective-permute-start | bytes 2414600 | tf_op jit(solution)/shard_map/ppermute | solution.py:90
  33.1 137.8 %collective-permute-start.1 = (bf16[12,2,48,384]{3,2,1,0:T(8,128)(2,1)}, bf16[12,2,48,384]{3,2,1,0:T(8,128)(2,1)}, u32[]{:S(2)}, u32[]{:S(2)}) collective-permute-start(bf16[12,2,48,384]{3,2,1,0:T(8,128)(2,1)} %pad_maximum_fusion.2), channel_id=1, source_target_pairs={{0,8},{24,16},{1,9},{25,17},{2,10},{26,18},{3,11},{27,19},{4,12},{... | collective-permute-start | bytes 2654216 | tf_op jit(solution)/shard_map/ppermute | solution.py:15
  42.7 41.9 %collective-permute-start.16 = (bf16[32,3144]{1,0:T(8,128)(2,1)}, bf16[32,3144]{1,0:T(8,128)(2,1)}, u32[]{:S(2)}, u32[]{:S(2)}) collective-permute-start(bf16[32,3144]{1,0:T(8,128)(2,1)} %get-tuple-element.42), channel_id=1, source_target_pairs={{0,8},{24,16},{1,9},{25,17},{2,10},{26,18},{3,11},{27,19},{4,12},{... | collective-permute-start | bytes 603656 | tf_op jit(solution)/shard_map/ppermute | solution.py:15
  48.3 153.3 %collective-permute-start.3 = (bf16[12,2,48,384]{3,2,1,0:T(8,128)(2,1)}, bf16[12,2,48,384]{3,2,1,0:T(8,128)(2,1)}, u32[]{:S(2)}, u32[]{:S(2)}) collective-permute-start(bf16[12,2,48,384]{3,2,1,0:T(8,128)(2,1)} %pad_maximum_fusion.3), channel_id=1, source_target_pairs={{0,8},{24,16},{1,9},{25,17},{2,10},{26,18},{3,11},{27,19},{4,12},{... | collective-permute-start | bytes 2654216 | tf_op jit(solution)/shard_map/ppermute | solution.py:15
  52.0 188.4 %collective-permute-start = (bf16[12,2,48,384]{3,2,1,0:T(8,128)(2,1)}, bf16[12,2,48,384]{3,2,1,0:T(8,128)(2,1)}, u32[]{:S(2)}, u32[]{:S(2)}) collective-permute-start(bf16[12,2,48,384]{3,2,1,0:T(8,128)(2,1)} %pad_maximum_fusion.1), channel_id=1, source_target_pairs={{0,8},{24,16},{1,9},{25,17},{2,10},{26,18},{3,11},{27,19},{4,12},{... | collective-permute-start | bytes 2654216 | tf_op jit(solution)/shard_map/ppermute | solution.py:15
  54.5 117.8 %copy-start.6 = (bf16[2,4,48,1,384]{4,2,0,1,3:T(8,128)(2,1)S(1)}, bf16[2,4,48,1,384]{4,2,0,1,3:T(8,128)(2,1)}, u32[]{:S(2)}) copy-start(bf16[2,4,48,1,384]{4,2,0,1,3:T(8,128)(2,1)} %copy-done.5) | copy-start | bytes 884740
  54.5 117.8 %copy-start.12 = (bf16[2,1,48,3,384]{4,2,0,3,1:T(8,128)(2,1)S(1)}, bf16[2,1,48,3,384]{4,2,0,3,1:T(8,128)(2,1)}, u32[]{:S(2)}) copy-start(bf16[2,1,48,3,384]{4,2,0,3,1:T(8,128)(2,1)} %copy-done.11) | copy-start | bytes 663556
  56.3 112.8 %collective-permute-start.14 = (bf16[32,3144]{1,0:T(8,128)(2,1)S(1)}, bf16[32,3144]{1,0:T(8,128)(2,1)S(1)}, u32[]{:S(2)}, u32[]{:S(2)}) collective-permute-start(bf16[32,3144]{1,0:T(8,128)(2,1)S(1)} %copy-done.34), channel_id=1, source_target_pairs={{0,8},{24,16},{1,9},{25,17},{2,10},{26,18},{3,11},{27,19},{4,12},{... | collective-permute-start | bytes 603656 | tf_op jit(solution)/shard_map/ppermute | solution.py:15
  84.6 92.9 %collective-permute-start.13 = (bf16[32,3144]{1,0:T(8,128)(2,1)}, bf16[32,3144]{1,0:T(8,128)(2,1)S(1)}, u32[]{:S(2)}, u32[]{:S(2)}) collective-permute-start(bf16[32,3144]{1,0:T(8,128)(2,1)} %get-tuple-element.41), channel_id=1, source_target_pairs={{0,8},{24,16},{1,9},{25,17},{2,10},{26,18},{3,11},{27,19},{4,12},{... | collective-permute-start | bytes 603656 | tf_op jit(solution)/shard_map/ppermute | solution.py:15
  169.1 0.7 collective-permute-start.17
  169.9 8.4 %collective-permute-start.15 = (bf16[32,3144]{1,0:T(8,128)(2,1)S(1)}, bf16[32,3144]{1,0:T(8,128)(2,1)S(1)}, u32[]{:S(2)}, u32[]{:S(2)}) collective-permute-start(bf16[32,3144]{1,0:T(8,128)(2,1)S(1)} %add_convert_fusion.7), channel_id=1, source_target_pairs={{8,16},{16,8},{9,17},{17,9},{10,18},{18,10},{11,19},{19,11},{12,20... | collective-permute-start | bytes 603656 | tf_op jit(solution)/shard_map/ppermute | solution.py:15
  170.9 24.4 %collective-permute-start.18 = (bf16[32,3144]{1,0:T(8,128)(2,1)S(1)}, bf16[32,3144]{1,0:T(8,128)(2,1)S(1)}, u32[]{:S(2)}, u32[]{:S(2)}) collective-permute-start(bf16[32,3144]{1,0:T(8,128)(2,1)S(1)} %add_convert_fusion.5), channel_id=1, source_target_pairs={{8,0},{16,24},{9,1},{17,25},{10,2},{18,26},{11,3},{19,27},{12,4},{... | collective-permute-start | bytes 603656 | tf_op jit(solution)/shard_map/ppermute | solution.py:15
  177.5 62.9 %collective-permute-start.2 = (bf16[12,2,48,384]{3,2,1,0:T(8,128)(2,1)S(1)}, bf16[12,2,48,384]{3,2,1,0:T(8,128)(2,1)S(1)}, u32[]{:S(2)}, u32[]{:S(2)}) collective-permute-start(bf16[12,2,48,384]{3,2,1,0:T(8,128)(2,1)S(1)} %add_convert_fusion.3), channel_id=1, source_target_pairs={{8,16},{16,8},{9,17},{17,9},{10,18},{18,10},{11,19},{19,11},{12,20... | collective-permute-start | bytes 2654216 | tf_op jit(solution)/shard_map/ppermute | solution.py:15
  195.5 9.8 %collective-permute-start.19 = (bf16[32,3144]{1,0:T(8,128)(2,1)S(1)}, bf16[32,3144]{1,0:T(8,128)(2,1)S(1)}, u32[]{:S(2)}, u32[]{:S(2)}) collective-permute-start(bf16[32,3144]{1,0:T(8,128)(2,1)S(1)} %multiply_convert_fusion), channel_id=1, source_target_pairs={{0,1},{1,0},{2,3},{3,2},{4,5},{5,4},{6,7},{7,6},{8,9},{9,8},{10,11... | collective-permute-start | bytes 603656 | tf_op jit(solution)/shard_map/ppermute | solution.py:161
  202.9 30.4 %collective-permute-start.4 = (bf16[12,2,48,384]{3,2,1,0:T(8,128)(2,1)S(1)}, bf16[12,2,48,384]{3,2,1,0:T(8,128)(2,1)S(1)}, u32[]{:S(2)}, u32[]{:S(2)}) collective-permute-start(bf16[12,2,48,384]{3,2,1,0:T(8,128)(2,1)S(1)} %add_convert_fusion.2), channel_id=1, source_target_pairs={{8,16},{16,8},{9,17},{17,9},{10,18},{18,10},{11,19},{19,11},{12,20... | collective-permute-start | bytes 2654216 | tf_op jit(solution)/shard_map/ppermute | solution.py:15
  206.4 28.1 %collective-permute-start.20 = (bf16[32,3144]{1,0:T(8,128)(2,1)S(1)}, bf16[32,3144]{1,0:T(8,128)(2,1)S(1)}, u32[]{:S(2)}, u32[]{:S(2)}) collective-permute-start(bf16[32,3144]{1,0:T(8,128)(2,1)S(1)} %dynamic-slice_convert_fusion), channel_id=1, source_target_pairs={{8,0},{16,24},{9,1},{17,25},{10,2},{18,26},{11,3},{19,27},{12,4},{... | collective-permute-start | bytes 603656 | tf_op jit(solution)/shard_map/ppermute | solution.py:15
  207.8 28.0 %collective-permute-start.21 = (bf16[32,3144]{1,0:T(8,128)(2,1)S(1)}, bf16[32,3144]{1,0:T(8,128)(2,1)S(1)}, u32[]{:S(2)}, u32[]{:S(2)}) collective-permute-start(bf16[32,3144]{1,0:T(8,128)(2,1)S(1)} %dynamic-slice_convert_fusion), channel_id=1, source_target_pairs={{0,8},{24,16},{1,9},{25,17},{2,10},{26,18},{3,11},{27,19},{4,12},{... | collective-permute-start | bytes 603656 | tf_op jit(solution)/shard_map/ppermute | solution.py:15
  233.4 4.4 collective-permute-start.22
  234.4 76.7 %collective-permute-start.5 = (bf16[12,2,48,384]{3,2,1,0:T(8,128)(2,1)S(1)}, bf16[12,2,48,384]{3,2,1,0:T(8,128)(2,1)S(1)}, u32[]{:S(2)}, u32[]{:S(2)}) collective-permute-start(bf16[12,2,48,384]{3,2,1,0:T(8,128)(2,1)S(1)} %add_convert_fusion.1), channel_id=1, source_target_pairs={{8,0},{16,24},{9,1},{17,25},{10,2},{18,26},{11,3},{19,27},{12,4},{... | collective-permute-start | bytes 2654216 | tf_op jit(solution)/shard_map/ppermute | solution.py:15
  235.8 3.3 collective-permute-start.24
  237.8 81.7 %collective-permute-start.23 = (bf16[32,3144]{1,0:T(8,128)(2,1)S(1)}, bf16[32,3144]{1,0:T(8,128)(2,1)S(1)}, u32[]{:S(2)}, u32[]{:S(2)}) collective-permute-start(bf16[32,3144]{1,0:T(8,128)(2,1)S(1)} %collective-permute-done.22), channel_id=1, source_target_pairs={{8,0},{16,24},{9,1},{17,25},{10,2},{18,26},{11,3},{19,27},{12,4},{... | collective-permute-start | bytes 603656 | tf_op jit(solution)/shard_map/ppermute | solution.py:15
  239.1 134.9 %collective-permute-start.25 = (bf16[32,3144]{1,0:T(8,128)(2,1)}, bf16[32,3144]{1,0:T(8,128)(2,1)}, u32[]{:S(2)}, u32[]{:S(2)}) collective-permute-start(bf16[32,3144]{1,0:T(8,128)(2,1)} %collective-permute-done.24), channel_id=1, source_target_pairs={{8,0},{16,24},{9,1},{17,25},{10,2},{18,26},{11,3},{19,27},{12,4},{... | collective-permute-start | bytes 603656 | tf_op jit(solution)/shard_map/ppermute | solution.py:15
  315.8 16.4 %all-to-all-start = ((bf16[4,2,48,1152]{3,2,1,0:T(8,128)(2,1)}), bf16[4,2,48,1152]{3,2,1,0:T(8,128)(2,1)S(1)}, u32[]{:S(2)}, u32[]{:S(2)}) async-start(bf16[4,2,48,1152]{3,2,1,0:T(8,128)(2,1)} %concatenate.70), calls=%async_computation | async-start | bytes 1769472 | tf_op jit(solution)/shard_map/all_to_all | solution.py:121
  370.5 16.2 %all-to-all-start.1 = ((bf16[4,2,48,1152]{3,2,1,0:T(8,128)(2,1)}), bf16[4,2,48,1152]{3,2,1,0:T(8,128)(2,1)S(1)}, u32[]{:S(2)}, u32[]{:S(2)}) async-start(bf16[4,2,48,1152]{3,2,1,0:T(8,128)(2,1)} %copy.253), calls=%async_computation.1 | async-start | bytes 1769472 | tf_op jit(solution)/shard_map/all_to_all | solution.py:143
  375.9 23.0 %collective-permute-start.26 = (bf16[96,3144]{1,0:T(8,128)(2,1)}, bf16[96,3144]{1,0:T(8,128)(2,1)}, u32[]{:S(2)}, u32[]{:S(2)}) collective-permute-start(bf16[96,3144]{1,0:T(8,128)(2,1)} %pad_maximum_fusion.5), channel_id=1, source_target_pairs={{0,1},{1,0},{2,3},{3,2},{4,5},{5,4},{6,7},{7,6},{8,9},{9,8},{10,11... | collective-permute-start | bytes 1810952 | tf_op jit(solution)/shard_map/ppermute | solution.py:179
  389.6 27.2 %collective-permute-start.6 = (bf16[12,2,48,384]{3,2,1,0:T(8,128)(2,1)}, bf16[12,2,48,384]{3,2,1,0:T(8,128)(2,1)}, u32[]{:S(2)}, u32[]{:S(2)}) collective-permute-start(bf16[12,2,48,384]{3,2,1,0:T(8,128)(2,1)} %pad_maximum_fusion.4), channel_id=1, source_target_pairs={{8,0},{16,24},{9,1},{17,25},{10,2},{18,26},{11,3},{19,27},{12,4},{... | collective-permute-start | bytes 2654216 | tf_op jit(solution)/shard_map/ppermute | solution.py:15
  390.9 24.3 %collective-permute-start.7 = (bf16[12,2,48,384]{3,2,1,0:T(8,128)(2,1)}, bf16[12,2,48,384]{3,2,1,0:T(8,128)(2,1)}, u32[]{:S(2)}, u32[]{:S(2)}) collective-permute-start(bf16[12,2,48,384]{3,2,1,0:T(8,128)(2,1)} %pad_maximum_fusion.4), channel_id=1, source_target_pairs={{0,8},{24,16},{1,9},{25,17},{2,10},{26,18},{3,11},{27,19},{4,12},{... | collective-permute-start | bytes 2654216 | tf_op jit(solution)/shard_map/ppermute | solution.py:15
  397.3 7.1 %collective-permute-start.8 = (bf16[12,2,48,384]{3,2,1,0:T(8,128)(2,1)}, bf16[12,2,48,384]{3,2,1,0:T(8,128)(2,1)}, u32[]{:S(2)}, u32[]{:S(2)}) collective-permute-start(bf16[12,2,48,384]{3,2,1,0:T(8,128)(2,1)} %pad_maximum_fusion.4), channel_id=1, source_target_pairs={{8,16},{16,8},{9,17},{17,9},{10,18},{18,10},{11,19},{19,11},{12,20... | collective-permute-start | bytes 2654216 | tf_op jit(solution)/shard_map/ppermute | solution.py:15
  404.4 35.2 %collective-permute-start.9 = (bf16[12,2,48,384]{3,2,1,0:T(8,128)(2,1)}, bf16[12,2,48,384]{3,2,1,0:T(8,128)(2,1)}, u32[]{:S(2)}, u32[]{:S(2)}) collective-permute-start(bf16[12,2,48,384]{3,2,1,0:T(8,128)(2,1)} %collective-permute-done.8), channel_id=1, source_target_pairs={{8,0},{16,24},{9,1},{17,25},{10,2},{18,26},{11,3},{19,27},{12,4},{... | collective-permute-start | bytes 2654216 | tf_op jit(solution)/shard_map/ppermute | solution.py:15
  415.2 15.0 %collective-permute-start.10 = (bf16[12,2,48,384]{3,2,1,0:T(8,128)(2,1)}, bf16[12,2,48,384]{3,2,1,0:T(8,128)(2,1)}, u32[]{:S(2)}, u32[]{:S(2)}) collective-permute-start(bf16[12,2,48,384]{3,2,1,0:T(8,128)(2,1)} %collective-permute-done.7), channel_id=1, source_target_pairs={{8,16},{16,8},{9,17},{17,9},{10,18},{18,10},{11,19},{19,11},{12,20... | collective-permute-start | bytes 2654216 | tf_op jit(solution)/shard_map/ppermute | solution.py:15
  430.1 33.3 %collective-permute-start.11 = (bf16[12,2,48,384]{3,2,1,0:T(8,128)(2,1)}, bf16[12,2,48,384]{3,2,1,0:T(8,128)(2,1)}, u32[]{:S(2)}, u32[]{:S(2)}) collective-permute-start(bf16[12,2,48,384]{3,2,1,0:T(8,128)(2,1)} %collective-permute-done.10), channel_id=1, source_target_pairs={{8,0},{16,24},{9,1},{17,25},{10,2},{18,26},{11,3},{19,27},{12,4},{... | collective-permute-start | bytes 2654216 | tf_op jit(solution)/shard_map/ppermute | solution.py:15
  (47 other events, 686.3 us)
Sparse Core Ops, SparseCore 0:
  23.8 240.6 all-gather.2

commit v2 on v0

v2 whole, which is shorter than its diff:
```python
import functools

import jax
import jax.numpy as jnp
from jax import lax
from jax.experimental import pallas as pl
from jax.experimental.pallas import tpu as pltpu
from jax.sharding import PartitionSpec as P

MOMENTUM = 0.5
OUTER_RATE = 0.7
LANES = 128

OUT_IN = [(0, 1), (3, 2)]
MIDDLE = [(1, 2), (2, 1)]
IN_OUT = [(1, 0), (2, 3)]
NEAR = OUT_IN + IN_OUT
SWAP = [(0, 1), (1, 0)]


def permute(value, pairs):
    return lax.ppermute(value, "rep", pairs)


def wide(value):
    return value.astype(jnp.float32)


def add(one, two):
    return (wide(one) + wide(two)).astype(one.dtype)


def at_end():
    rank = lax.axis_index("rep")
    return (rank == 0) | (rank == 3)


def block_of(place):
    return jnp.where(lax.axis_index("rep") >= 2, 3 - place, place)


def block_at(step):
    if step == 0:
        return lax.axis_index("rep")
    return block_of(jnp.where(at_end(), 1, 0)) if step == 1 else block_of(step)


class Kind:
    def __init__(self, delta, groups, shards, sub, width, panel, column):
        self.layers, self.rows, self.cols = delta.shape[1:]
        self.count = self.rows // groups
        self.over = self.count // sub
        self.across = self.cols // width
        self.piece = self.cols // shards
        self.panel = panel
        self.column = column


def make_kinds(deltas, groups, shards):
    width = min(delta.shape[3] for delta in deltas)
    sub = min(delta.shape[2] for delta in deltas) // groups
    kinds = []
    panel = column = 0
    for delta in deltas:
        kind = Kind(delta, groups, shards, sub, width, panel, column)
        kinds.append(kind)
        panel = panel + kind.over * kind.across
        column = column + kind.over * kind.piece
    return kinds, sub, width, panel, column


def each_panel(kinds, sub, width):
    for index, kind in enumerate(kinds):
        for group in range(kind.over):
            for across in range(kind.across):
                panel = kind.panel + group * kind.across + across
                for layer in range(kind.layers):
                    yield index, layer, group * sub, across * width, panel, layer * sub


def pack_kernel(kinds, sub, width, *refs):
    deltas, blocks, sem = refs[: len(kinds)], refs[len(kinds) : -1], refs[-1]
    for order, target in enumerate(blocks):
        block = block_of(len(blocks) - 1 - order)
        for index, layer, row, column, panel, at in each_panel(kinds, sub, width):
            start = pl.multiple_of(block * kinds[index].count + row, 16)
            source = deltas[index].at[0, layer, pl.ds(start, sub), pl.ds(column, width)]
            pltpu.make_async_copy(source, target.at[panel, pl.ds(at, sub), :], sem.at[order]).start()
    for order, target in enumerate(blocks):
        pltpu.make_async_copy(target, target, sem.at[order]).wait()


def place_kernel(kinds, sub, width, step, *refs):
    one, two = refs[:2]
    fresh, sem = refs[-1 - len(kinds) : -1], refs[-1]
    block = block_at(step)

    def start(source):
        for index, layer, row, column, panel, at in each_panel(kinds, sub, width):
            first = pl.multiple_of(block * kinds[index].count + row, 16)
            target = fresh[index].at[layer, pl.ds(first, sub), pl.ds(column, width)]
            pltpu.make_async_copy(source.at[panel, pl.ds(at, sub), :], target, sem).start()

    pl.when(at_end())(lambda: start(one))
    pl.when(jnp.logical_not(at_end()))(lambda: start(two))
    pltpu.make_async_copy(one, one, sem).wait()


def split_kernel(kinds, width, shards, near, last, from_out, from_middle, from_in, *refs):
    end, pieces = at_end(), refs[-1]
    for kind in kinds:
        for group in range(kind.over):
            parts = []
            for across in range(kind.across):
                panel = kind.panel + group * kind.across + across
                mine = jnp.where(end, wide(last[panel]), wide(near[panel]))
                arrived = wide(from_out[panel]) + wide(from_middle[panel]) + wide(from_in[panel])
                parts.append(mine + arrived)
            whole = jnp.concatenate(parts, axis=1)
            column = kind.column + group * kind.piece
            for s in range(shards):
                part = whole[:, s * kind.piece : (s + 1) * kind.piece]
                pieces[s, :, column : column + kind.piece] = part.astype(pieces.dtype)


def join_kernel(kinds, width, shards, pieces, *refs):
    panels = refs[-1]
    wholes = [wide(pieces[s]) for s in range(shards)]
    for kind in kinds:
        for group in range(kind.over):
            column = kind.column + group * kind.piece
            whole = jnp.concatenate([part[:, column : column + kind.piece] for part in wholes], axis=1)
            for across in range(kind.across):
                panel = kind.panel + group * kind.across + across
                panels[panel] = whole[:, across * width : (across + 1) * width].astype(panels.dtype)


def owner_update_kernel(units, shards, groups, moved, weights, momentum, *refs):
    next_weights, next_momentum, back = refs[-3:]
    for flat, row, rows, column, piece in units:
        here = slice(row, row + rows)
        parts = [moved[s, here, :].astype(jnp.float32)[:, column : column + piece] for s in range(shards)]
        gradient = jnp.concatenate(parts, axis=1) / groups
        tiles = shards * piece // LANES
        fresh = []
        for tile in range(tiles):
            at = pl.ds(flat + tile, rows, stride=tiles)
            grad = gradient[:, tile * LANES : (tile + 1) * LANES]
            new_momentum = MOMENTUM * momentum[at, :] + grad
            new_weights = weights[at, :] - OUTER_RATE * (grad + MOMENTUM * new_momentum)
            next_momentum[at, :] = new_momentum
            next_weights[at, :] = new_weights
            fresh.append(new_weights)
        fresh = jnp.concatenate(fresh, axis=1)
        for s in range(shards):
            back[s, here, column : column + piece] = fresh[:, s * piece : (s + 1) * piece].astype(back.dtype)


def kernel_call(body, out_shape, moved_bytes, **more):
    return pl.pallas_call(
        body,
        out_shape=out_shape,
        compiler_params=pltpu.CompilerParams(vmem_limit_bytes=40 << 20),
        cost_estimate=pl.CostEstimate(flops=0, bytes_accessed=moved_bytes, transcendentals=0),
        **more,
    )


ANYWHERE = pl.BlockSpec(memory_space=pl.ANY)
IN_VMEM = pl.BlockSpec(memory_space=pltpu.VMEM)


def copy_kernel(value, *refs):
    refs[-1][...] = value[...]


def after(value, *others):
    return kernel_call(
        copy_kernel,
        jax.ShapeDtypeStruct(value.shape, value.dtype),
        2 * value.size * value.dtype.itemsize,
        in_specs=[IN_VMEM] + [ANYWHERE] * len(others),
    )(value, *others)


def hold_kernel(*refs):
    pass


def hold(value, *others):
    return kernel_call(
        hold_kernel,
        jax.ShapeDtypeStruct(value.shape, value.dtype),
        0,
        in_specs=[ANYWHERE] * (1 + len(others)),
        out_specs=ANYWHERE,
        input_output_aliases={0: 0},
    )(value, *others)


def add_kernel(count, *refs):
    for one, two, total in zip(refs[:count], refs[count : 2 * count], refs[-count:]):
        total[...] = (wide(one[...]) + wide(two[...])).astype(total.dtype)


def add_after(pairs, *others):
    count = len(pairs)
    return kernel_call(
        functools.partial(add_kernel, count),
        [jax.ShapeDtypeStruct(one.shape, one.dtype) for one, _ in pairs],
        6 * sum(one.size for one, _ in pairs),
        in_specs=[IN_VMEM] * (2 * count) + [ANYWHERE] * len(others),
    )(*[one for one, _ in pairs], *[two for _, two in pairs], *others)


def narrow_kernel(cut, wide_rows, low, high):
    low[...] = wide_rows[:cut, :].astype(low.dtype)
    high[...] = wide_rows[cut:, :].astype(high.dtype)


def narrow_rows(array, cut):
    rows, columns = array.shape[2:]
    if cut % 16 or rows % 8:
        return [part.astype(jnp.bfloat16) for part in (array[0, 0, :cut], array[0, 0, cut:])]
    return kernel_call(
        functools.partial(narrow_kernel, cut),
        [jax.ShapeDtypeStruct((count, columns), jnp.bfloat16) for count in (cut, rows - cut)],
        6 * rows * columns,
    )(array.reshape(rows, columns))


class Dense:
    def __init__(self, deltas, groups, shards):
        self.groups, self.shards = groups, shards
        self.kinds, self.sub, self.width, self.panels, self.columns = make_kinds(deltas, groups, shards)
        self.layers = deltas[0].shape[1]
        self.dtype = deltas[0].dtype
        self.block_shape = (self.panels, self.layers * self.sub, self.width)
        self.block_bytes = 2 * self.panels * self.layers * self.sub * self.width
        self.aligned = self.sub % 16 == 0 and self.width % LANES == 0
        self.aligned = self.aligned and all(shards * kind.piece % LANES == 0 for kind in self.kinds)

    def pack(self, deltas):
        if self.aligned:
            return kernel_call(
                functools.partial(pack_kernel, self.kinds, self.sub, self.width),
                [jax.ShapeDtypeStruct(self.block_shape, self.dtype)] * 4,
                8 * self.block_bytes,
                in_specs=[ANYWHERE] * len(deltas),
                out_specs=[ANYWHERE] * 4,
                scratch_shapes=[pltpu.SemaphoreType.DMA((4,))],
            )(*deltas)

        def block_panels(block):
            panels = []
            for kind, delta in zip(self.kinds, deltas):
                part = lax.dynamic_slice_in_dim(delta[0], block * kind.count, kind.count, 1)
                part = part.reshape(kind.layers, kind.over, self.sub, kind.across, self.width)
                panels.append(part.transpose(1, 3, 0, 2, 4).reshape(-1, *self.block_shape[1:]))
            return jnp.concatenate(panels)

        return [block_panels(block_of(place)) for place in (3, 2, 1, 0)]

    def as_kinds(self, block):
        parts = []
        for kind in self.kinds:
            part = block[kind.panel : kind.panel + kind.over * kind.across]
            part = part.reshape(kind.over, kind.across, kind.layers, self.sub, self.width)
            parts.append(part.transpose(2, 0, 3, 1, 4).reshape(kind.layers, kind.over, self.sub, kind.cols))
        return parts

    def split(self, near, last, from_out, from_middle, from_in, *others):
        shape = (self.shards, self.layers * self.sub, self.columns)
        if self.aligned:
            return kernel_call(
                functools.partial(split_kernel, self.kinds, self.width, self.shards),
                jax.ShapeDtypeStruct(shape, self.dtype),
                9 * self.block_bytes,
                in_specs=[IN_VMEM] * 5 + [ANYWHERE] * len(others),
            )(near, last, from_out, from_middle, from_in, *others)
        mine = jnp.where(at_end(), last, near)
        total = wide(mine) + wide(from_out) + wide(from_middle) + wide(from_in)
        pieces = []
        for kind, part in zip(self.kinds, self.as_kinds(total.astype(self.dtype))):
            part = part.reshape(kind.layers, kind.over, self.sub, self.shards, kind.piece)
            pieces.append(part.transpose(3, 0, 2, 1, 4).reshape(shape[:2] + (kind.over * kind.piece,)))
        return jnp.concatenate(pieces, axis=2)

    def join(self, pieces, *others):
        if self.aligned:
            return kernel_call(
                functools.partial(join_kernel, self.kinds, self.width, self.shards),
                jax.ShapeDtypeStruct(self.block_shape, self.dtype),
                2 * self.block_bytes,
                in_specs=[IN_VMEM] + [ANYWHERE] * len(others),
            )(pieces, *others)
        panels = []
        for kind in self.kinds:
            part = pieces[..., kind.column : kind.column + kind.over * kind.piece]
            part = part.reshape(self.shards, kind.layers, self.sub, kind.over, kind.piece)
            part = part.transpose(3, 1, 2, 0, 4).reshape(kind.over, kind.layers, self.sub, kind.across, self.width)
            panels.append(part.transpose(0, 3, 1, 2, 4).reshape(-1, *self.block_shape[1:]))
        return jnp.concatenate(panels)

    def place(self, fresh, step, one, two):
        shapes = [(kind.layers, kind.rows, kind.cols) for kind in self.kinds]
        if self.aligned:
            before = fresh or []
            return kernel_call(
                functools.partial(place_kernel, self.kinds, self.sub, self.width, step),
                [jax.ShapeDtypeStruct(shape, self.dtype) for shape in shapes],
                2 * self.block_bytes,
                in_specs=[ANYWHERE] * (2 + len(before)),
                out_specs=[ANYWHERE] * len(shapes),
                scratch_shapes=[pltpu.SemaphoreType.DMA],
                input_output_aliases={2 + index: index for index in range(len(before))},
            )(one, two, *before)
        fresh = fresh or [jnp.zeros(shape, self.dtype) for shape in shapes]
        block = jnp.where(at_end(), one, two)
        placed = []
        for kind, target, part in zip(self.kinds, fresh, self.as_kinds(block)):
            part = part.reshape(kind.layers, kind.count, kind.cols)
            placed.append(lax.dynamic_update_slice_in_dim(target, part, block_at(step) * kind.count, 1))
        return placed

    def update(self, moved, weights, momentum, *others):
        if self.aligned:
            units = []
            flat = 0
            for kind in self.kinds:
                for layer in range(kind.layers):
                    for group in range(kind.over):
                        column = kind.column + group * kind.piece
                        units.append((flat, layer * self.sub, self.sub, column, kind.piece))
                        flat = flat + self.sub * self.shards * kind.piece // LANES
            flat_shape = jax.ShapeDtypeStruct((flat, LANES), jnp.float32)
            next_weights, next_momentum, back = kernel_call(
                functools.partial(owner_update_kernel, units, self.shards, self.groups),
                (flat_shape, flat_shape, jax.ShapeDtypeStruct(moved.shape, moved.dtype)),
                10 * self.block_bytes,
                in_specs=[IN_VMEM] * 3 + [ANYWHERE] * len(others),
            )(moved, weights.reshape(flat, LANES), momentum.reshape(flat, LANES), *others)
            return next_weights.reshape(weights.shape), next_momentum.reshape(weights.shape), back
        flats = []
        for kind in self.kinds:
            part = moved[..., kind.column : kind.column + kind.over * kind.piece]
            part = part.reshape(self.shards, kind.layers, self.sub, kind.over, kind.piece)
            flats.append(part.transpose(1, 3, 2, 0, 4).reshape(-1))
        gradient = (wide(jnp.concatenate(flats)) / self.groups).reshape(weights.shape)
        next_momentum = MOMENTUM * momentum + gradient
        next_weights = weights - OUTER_RATE * (gradient + MOMENTUM * next_momentum)
        copies = next_weights.astype(moved.dtype).reshape(-1)
        returning = []
        at = 0
        for kind in self.kinds:
            count = kind.layers * kind.count * kind.cols
            part = copies[at : at + count].reshape(kind.layers, kind.over, self.sub, self.shards, kind.piece)
            returning.append(part.transpose(3, 0, 2, 1, 4).reshape(moved.shape[:2] + (kind.over * kind.piece,)))
            at = at + count
        return next_weights, next_momentum, jnp.concatenate(returning, axis=2)


def local(
    delta_inputs,
    delta_mixing,
    delta_expand,
    delta_reduce,
    owner_weights,
    owner_momentum,
    delta_embed,
    embed_owner,
    embed_momentum,
    basis,
):
    groups = lax.axis_size("rep")
    shards = lax.axis_size("shard")
    side = lax.axis_index("tp")
    end = at_end()
    deltas = (delta_inputs, delta_mixing, delta_expand, delta_reduce)
    dense = Dense(deltas, groups, shards)


    def to_end(value):
        return permute(value, IN_OUT)

    def across(value):
        return permute(value, MIDDLE)

    def to_inner(value):
        return permute(value, OUT_IN)

    rows = embed_owner.shape[2]
    half_rank = basis.shape[1] // 2
    cut = rows // 2 // LANES * LANES
    low, high = narrow_rows(embed_owner, cut)
    rows_near = [to_end(low), to_end(high)]
    rows_across = [across(low), across(high)]
    rows_far = [to_end(part) for part in rows_across]

    far, middle, near, last = dense.pack(deltas)
    far_in, middle_in, near_in = (to_inner(part) for part in (far, middle, near))
    (far_sum,) = add_after([(far, far_in)], rows_near[0], rows_across[0])
    far_across = across(far_sum)
    middle_sum, last_sum = add_after([(middle, middle_in), (last, far_across)], rows_near[1])
    middle_across = across(middle_sum)
    last_out = to_end(last_sum)
    rows_inner = [to_inner(low)]
    pieces = dense.split(
        near, last, near_in, middle_across, last_out, rows_far[0], rows_across[1], rows_inner[0]
    )
    rows_inner.append(to_inner(hold(high, pieces)))
    rows_across_2 = [across(part) for part in rows_inner]
    rows_last = [to_end(part) for part in rows_across_2]

    terms = lax.dot_general(
        after(basis, far),
        wide(delta_embed[0]),
        (((0,), (1,)), ((), ())),
        precision=lax.Precision.HIGH,
        preferred_element_type=jnp.float32,
    ).astype(jnp.bfloat16)
    keep = lax.dynamic_slice_in_dim(terms, side * half_rank, half_rank, 0)
    give = lax.dynamic_slice_in_dim(terms, (1 - side) * half_rank, half_rank, 0)
    (kept,) = add_after([(keep, lax.ppermute(give, "tp", SWAP))], pieces)

    def term(place):
        return lax.dynamic_slice_in_dim(kept, block_of(place) * rows, rows, 1)

    terms_out = to_inner(jnp.stack([term(3), term(2), term(1)]))
    terms_middle = across(jnp.stack([add(term(3), terms_out[0]), add(term(2), terms_out[1])]))
    terms_in = to_end(add(term(0), terms_middle[0]))

    moved = lax.all_to_all(pieces, "shard", split_axis=0, concat_axis=0, tiled=True)
    next_weights, next_momentum, back = dense.update(moved, owner_weights, owner_momentum, terms_out)
    back = lax.all_to_all(back, "shard", split_axis=0, concat_axis=0, tiled=True)
    new_block = dense.join(back, rows_far[1], rows_across_2[0], terms_middle)

    mine = jnp.where(end, term(0), term(1))
    total = wide(mine) + wide(terms_out[2]) + wide(terms_middle[1]) + wide(terms_in)
    sent = (total / groups).astype(jnp.bfloat16)
    other = lax.ppermute(sent, "tp", SWAP)

    def both(one, two):
        return jnp.where(side == 0, jnp.concatenate([one, two]), jnp.concatenate([two, one]))

    coefficients = wide(both(sent, other))
    next_embed_momentum = MOMENTUM * embed_momentum[0, 0].T + coefficients
    direction = coefficients + MOMENTUM * next_embed_momentum

    def update(toward, precision):
        return OUTER_RATE * lax.dot_general(
            toward, basis, (((0,), (1,)), ((), ())), precision=precision, preferred_element_type=jnp.float32
        )

    next_embed = embed_owner[0, 0] - update(direction, lax.Precision.HIGHEST)
    half = lax.dynamic_slice_in_dim(direction, side * half_rank, half_rank, 0).astype(jnp.bfloat16)

    rank = lax.axis_index("rep")
    halves = jnp.stack([permute(half, [(i, (i + step) % groups) for i in range(groups)]) for step in (1, 2, 3)])
    others = lax.ppermute(halves, "tp", SWAP)
    block_near = permute(new_block, NEAR)
    block_across = across(new_block)
    block_across = hold(block_across, rows_inner[1], rows_last[0], terms_in)
    block_far = to_end(block_across)
    block_across_2 = hold(across(block_near), rows_across_2[1], others)
    block_last = to_end(block_across_2)

    fresh = dense.place(None, 0, new_block, new_block)
    fresh = dense.place(fresh, 1, block_near, block_near)
    fresh = dense.place(fresh, 2, block_far, block_across)
    fresh = dense.place(fresh, 3, block_last, block_across_2)

    fresh_embed = jnp.zeros((groups * rows, embed_owner.shape[3]), jnp.bfloat16)

    def put(target, value, step, start):
        return lax.dynamic_update_slice_in_dim(target, value.astype(target.dtype), block_at(step) * rows + start, 0)

    fresh_embed = put(fresh_embed, next_embed, 0, 0)
    arrived = [(1, rows_near, rows_inner), (2, rows_far, rows_across), (3, rows_last, rows_across_2)]
    for step, at_ends, inside in arrived:
        back_by = (rank - block_at(step) - 1) % groups
        here, there = (lax.dynamic_index_in_dim(part, back_by, 0, False) for part in (halves, others))
        toward = both(here, there)
        for start, one, two in zip((0, cut), at_ends, inside):
            part = jnp.where(end, one, two)
            change = update(wide(toward[:, start : start + part.shape[0]]), lax.Precision.DEFAULT)
            fresh_embed = put(fresh_embed, wide(part) - change, step, start)
    return (
        fresh[0],
        fresh[1],
        fresh[2],
        fresh[3],
        next_weights,
        next_momentum,
        fresh_embed,
        next_embed[None, None],
        next_embed_momentum.T[None, None],
    )


def solution(mesh):
    in_specs = (
        P("rep", None, "shard", "tp"),
        P("rep", None, "shard", "tp"),
        P("rep", None, "shard", "tp"),
        P("rep", None, "shard", "tp"),
        P("rep", "shard", "tp", None),
        P("rep", "shard", "tp", None),
        P("rep", "shard", "tp"),
        P("shard", "rep", None, "tp"),
        P("shard", "rep", None, None),
        P("tp", None),
    )
    out_specs = (
        P(None, "shard", "tp"),
        P(None, "shard", "tp"),
        P(None, "shard", "tp"),
        P(None, "shard", "tp"),
        P("rep", "shard", "tp", None),
        P("rep", "shard", "tp", None),
        P("shard", "tp"),
        P("shard", "rep", None, "tp"),
        P("shard", "rep", None, None),
    )
    return jax.shard_map(local, mesh=mesh, in_specs=in_specs, out_specs=out_specs, check_vma=False)
```

time: 620 us -> 317 us (0.51)
  waiting for transfers between devices: 362 us -> 174 us
  blocking collectives: 82.1 us -> 0 us
  local copies, waits for them, and re-layouts: 83.1 us -> 12.6 us
  starting transfers between devices: 34.9 us -> 75.8 us
  Pallas kernels: 0 us -> 19.7 us
  other arithmetic: 23.9 us -> 5.22 us
  matrix products: 13.4 us -> 27.2 us
  between operations: 14.6 us -> 1.52 us
    ppermute x0 -> x32, waiting for transfers between devices: none -> 174 us  [the longest x29 174 us: permute(): return lax.ppermute(value, 'rep', pairs)]
    all_gather x3 -> x0, waiting for transfers between devices: 167 us -> none  [the longest x1 167 us: local(): lax.all_gather(next_embed[0, 0].astype(jnp.bfloat16), 'rep', axis=0, tile...]
    unnamed x6 -> x0, waiting for transfers between devices: 103 us -> none
    all_to_all x9 -> x2, waiting for transfers between devices: 92.5 us -> 0.01 us  [the longest x1 0.01 us: local(): lax.all_to_all(pieces, 'shard', split_axis=0, concat_axis=0, tiled=True)]
    ppermute x0 -> x32, starting transfers between devices: none -> 68.7 us  [the longest x29 65.1 us: permute(): return lax.ppermute(value, 'rep', pairs)]
    all_gather x2 -> x0, blocking collectives: 47.6 us -> none  [the longest x1 32.5 us: local(): lax.all_gather(placed_back[0], 'rep', axis=1, tiled=True)]
    all_to_all x3 -> x0, blocking collectives: 34.5 us -> none  [the longest x1 15.8 us: local(): lax.all_to_all(blocks[1], 'rep', split_axis=1, concat_axis=1, tiled=True)]
    unnamed x43 -> x47, local copies, waits for them, and re-layouts: 39.8 us -> 9.6 us
  transfers between devices with their start and end apart: 14 -> 34, of which waited for: 9 -> 15; matrix products, arithmetic and copies ran while one was open for 16% -> 11% of each run, Pallas kernels for 0% -> 5%
where the time goes in v2:
time: 317 us; the launch traced here: 316 us
  waiting for transfers between devices  174 us (55%)
  starting transfers between devices  75.8 us (24%)
  matrix products  27.2 us (9%)
  Pallas kernels  19.7 us (6%)
  local copies, waits for them, and re-layouts  12.6 us (4%)
  other arithmetic  5.22 us (2%)
    ppermute x29, waiting for transfers between devices, permute(): return lax.ppermute(value, 'rep', pairs)  174 us
    ppermute x29, starting transfers between devices, permute(): return lax.ppermute(value, 'rep', pairs)  65.1 us
    dot_general x7, matrix products, update(): lax.dot_general(toward, basis, (((0,), (1,)), ((), ())), precision=precis...  17.4 us
    dot_general x1, matrix products, local(): lax.dot_general(after(basis, far), wide(delta_embed[0]), (((0,), (1,)), (...  9.78 us
    unnamed x47, local copies, waits for them, and re-layouts  9.6 us
  transfers between devices with their start and end apart: 34, of which 15 were waited for; matrix products, arithmetic and copies ran while one was open for 11% of the time, Pallas kernels for 5%

profile of v2, /device:TPU:0, one launch (start us, length us, event | category | flops | bytes accessed | tf_op | source)
XLA Modules:
  0.0 316.0 jit_solution(13008164332263674049)
XLA Ops:
  0.7 2.4 copy-done
  9.3 6.9 %collective-permute-start.2 = (bf16[12,96,384]{2,1,0:T(8,128)(2,1)S(1)}, bf16[12,96,384]{2,1,0:T(8,128)(2,1)S(1)}, u32[]{:S(2)}, u32[]{:S(2)}) collective-permute-start(bf16[12,96,384]{2,1,0:T(8,128)(2,1)S(1)} %get-tuple-element.39.refs_0_), channel_id=1, source_target_pairs={{0,8},{24,16},{1,9},{25,17},{2,10},{26,18},{3,11},{27,19},{4,12},{... | collective-permute-start | bytes 2654216 | tf_op jit(solution)/shard_map/ppermute | solution.py:22
  17.5 6.6 %collective-permute-start.1 = (bf16[12,96,384]{2,1,0:T(8,128)(2,1)}, bf16[12,96,384]{2,1,0:T(8,128)(2,1)}, u32[]{:S(2)}, u32[]{:S(2)}) collective-permute-start(bf16[12,96,384]{2,1,0:T(8,128)(2,1)} %get-tuple-element.38.refs_0_), channel_id=1, source_target_pairs={{0,8},{24,16},{1,9},{25,17},{2,10},{26,18},{3,11},{27,19},{4,12},{... | collective-permute-start | bytes 2654216 | tf_op jit(solution)/shard_map/ppermute | solution.py:22
  24.1 12.1 %collective-permute-done.2.refs_1_ = bf16[12,96,384]{2,1,0:T(8,128)(2,1)S(1)} collective-permute-done((bf16[12,96,384]{2,1,0:T(8,128)(2,1)S(1)}, bf16[12,96,384]{2,1,0:T(8,128)(2,1)S(1)}, u32[]{:S(2)}, u32[]{:S(2)}) %collective-permute-start.2) | collective-permute-done | bytes 884768 | tf_op jit(solution)/shard_map/ppermute | solution.py:22
  36.2 2.9 collective-permute-done.3.refs_2_
  42.0 4.8 %collective-permute-start = (bf16[12,96,384]{2,1,0:T(8,128)(2,1)}, bf16[12,96,384]{2,1,0:T(8,128)(2,1)}, u32[]{:S(2)}, u32[]{:S(2)}) collective-permute-start(bf16[12,96,384]{2,1,0:T(8,128)(2,1)} %get-tuple-element.36.near), channel_id=1, source_target_pairs={{0,8},{24,16},{1,9},{25,17},{2,10},{26,18},{3,11},{27,19},{4,12},{... | collective-permute-start | bytes 2654216 | tf_op jit(solution)/shard_map/ppermute | solution.py:22
  47.7 9.8 %convolution_convert_fusion = bf16[64,12576]{1,0:T(8,128)(2,1)S(1)} fusion(f32[384,64]{1,0:T(8,128)S(1)} %shard_map.174, bf16[1,12576,384]{2,1,0:T(8,128)(2,1)} %param.16), kind=kOutput, calls=%fused_computation | convolution fusion | flops 1855211520 | bytes 11366400 | tf_op jit(solution)/shard_map/dot_general | solution.py:415
  57.5 2.2 collective-permute-start.11
  59.7 4.8 %collective-permute-done.6.refs_4_ = bf16[1608,384]{1,0:T(8,128)(2,1)} collective-permute-done((bf16[1608,384]{1,0:T(8,128)(2,1)}, bf16[1608,384]{1,0:T(8,128)(2,1)}, u32[]{:S(2)}, u32[]{:S(2)}) %collective-permute-start.6) | collective-permute-done | bytes 1234976 | tf_op jit(solution)/shard_map/ppermute | solution.py:22
  65.8 3.1 shard_map.172
  70.5 3.7 %collective-permute-done.from_out = bf16[12,96,384]{2,1,0:T(8,128)(2,1)} collective-permute-done((bf16[12,96,384]{2,1,0:T(8,128)(2,1)}, bf16[12,96,384]{2,1,0:T(8,128)(2,1)}, u32[]{:S(2)}, u32[]{:S(2)}) %collective-permute-start) | collective-permute-done | bytes 884768 | tf_op jit(solution)/shard_map/ppermute | solution.py:22
  76.6 21.3 %collective-permute-done.11.refs_2_ = bf16[1536,384]{1,0:T(8,128)(2,1)S(1)} collective-permute-done((bf16[1536,384]{1,0:T(8,128)(2,1)S(1)}, bf16[1536,384]{1,0:T(8,128)(2,1)S(1)}, u32[]{:S(2)}, u32[]{:S(2)}) %collective-permute-start.11) | collective-permute-done | bytes 1179680 | tf_op jit(solution)/shard_map/ppermute | solution.py:22
  100.5 12.0 %collective-permute-done.8.from_in = bf16[12,96,384]{2,1,0:T(8,128)(2,1)} collective-permute-done((bf16[12,96,384]{2,1,0:T(8,128)(2,1)}, bf16[12,96,384]{2,1,0:T(8,128)(2,1)}, u32[]{:S(2)}, u32[]{:S(2)}) %collective-permute-start.8) | collective-permute-done | bytes 884768 | tf_op jit(solution)/shard_map/ppermute | solution.py:22
  113.8 3.6 %shard_map.173.refs_2_.refs_1_ = bf16[4,96,1152]{2,1,0:T(8,128)(2,1)} custom-call(bf16[12,96,384]{2,1,0:T(8,128)(2,1)} %get-tuple-element.36.near, bf16[12,96,384]{2,1,0:T(8,128)(2,1)S(1)} %get-tuple-element.37.refs_1_.last, bf16[12,96,384]{2,1,0:T(8,128)(2,1)} %collective-permute-done.from_out, bf16[12,96,384]{2,1,0:T(8,128)(2,1)} %collective-permute-done.7.from_middle, ...), custom_call_target="tpu_custom_call" | custom-call | bytes 7962624 | tf_op jit(solution)/shard_map/pallas_call | solution.py:275
  119.6 4.5 %collective-permute-start.13 = (bf16[3,32,3144]{2,1,0:T(8,128)(2,1)S(1)}, bf16[3,32,3144]{2,1,0:T(8,128)(2,1)S(1)}, u32[]{:S(2)}, u32[]{:S(2)}) collective-permute-start(bf16[3,32,3144]{2,1,0:T(8,128)(2,1)S(1)} %pad_maximum_fusion), channel_id=1, source_target_pairs={{0,8},{24,16},{1,9},{25,17},{2,10},{26,18},{3,11},{27,19},{4,12},{... | collective-permute-start | bytes 1810952 | tf_op jit(solution)/shard_map/ppermute | solution.py:22
  124.1 11.0 %collective-permute-done.13.refs_0_ = bf16[3,32,3144]{2,1,0:T(8,128)(2,1)S(1)} collective-permute-done((bf16[3,32,3144]{2,1,0:T(8,128)(2,1)S(1)}, bf16[3,32,3144]{2,1,0:T(8,128)(2,1)S(1)}, u32[]{:S(2)}, u32[]{:S(2)}) %collective-permute-start.13) | collective-permute-done | bytes 603680 | tf_op jit(solution)/shard_map/ppermute | solution.py:22
  137.6 3.5 %all-to-all-start = ((bf16[4,96,1152]{2,1,0:T(8,128)(2,1)}), bf16[4,96,1152]{2,1,0:T(8,128)(2,1)S(1)}, u32[]{:S(2)}, u32[]{:S(2)}) async-start(bf16[4,96,1152]{2,1,0:T(8,128)(2,1)} %shard_map.173.refs_2_.refs_1_), calls=%async_computation | async-start | bytes 1769472 | tf_op jit(solution)/shard_map/all_to_all | solution.py:433
  141.1 12.3 %collective-permute-done.21.refs_3_ = bf16[32,3144]{1,0:T(8,128)(2,1)S(1)} collective-permute-done((bf16[32,3144]{1,0:T(8,128)(2,1)S(1)}, bf16[32,3144]{1,0:T(8,128)(2,1)S(1)}, u32[]{:S(2)}, u32[]{:S(2)}) %collective-permute-start.21) | collective-permute-done | bytes 201248 | tf_op jit(solution)/shard_map/ppermute | solution.py:22
  158.3 6.6 %collective-permute-start.19 = (bf16[1608,384]{1,0:T(8,128)(2,1)}, bf16[1608,384]{1,0:T(8,128)(2,1)}, u32[]{:S(2)}, u32[]{:S(2)}) collective-permute-start(bf16[1608,384]{1,0:T(8,128)(2,1)} %shard_map.178), channel_id=1, source_target_pairs={{0,8},{24,16},{1,9},{25,17},{2,10},{26,18},{3,11},{27,19},{4,12},{... | collective-permute-start | bytes 3704840 | tf_op jit(solution)/shard_map/ppermute | solution.py:22
  167.9 3.3 %shard_map.176 = (f32[3456,128]{1,0:T(8,128)}, f32[3456,128]{1,0:T(8,128)}, bf16[4,96,1152]{2,1,0:T(8,128)(2,1)S(1)}) custom-call(bf16[4,96,1152]{2,1,0:T(8,128)(2,1)S(1)} %all-to-all-done.moved, f32[3456,128]{1,0:T(8,128)S(1)} %bitcast.84, f32[3456,128]{1,0:T(8,128)S(1)} %bitcast.85, bf16[3,32,3144]{2,1,0:T(8,128)(2,1)S(1)} %collective-permute-done.13.refs_0_), custom_call_target="tpu_custom_call" | custom-call | bytes 8847360 | tf_op jit(solution)/shard_map/pallas_call | solution.py:337
  172.2 3.5 %all-to-all-start.1 = ((bf16[4,96,1152]{2,1,0:T(8,128)(2,1)}), bf16[4,96,1152]{2,1,0:T(8,128)(2,1)S(1)}, u32[]{:S(2)}, u32[]{:S(2)}) async-start(bf16[4,96,1152]{2,1,0:T(8,128)(2,1)} %copy-done.13), calls=%async_computation.1 | async-start | bytes 1769472 | tf_op jit(solution)/shard_map/all_to_all | solution.py:435
  175.7 2.3 fusion.8
  179.7 2.2 collective-permute-start.24
  183.8 13.0 %collective-permute-done.14.refs_0_ = bf16[1608,384]{1,0:T(8,128)(2,1)} collective-permute-done((bf16[1608,384]{1,0:T(8,128)(2,1)}, bf16[1608,384]{1,0:T(8,128)(2,1)}, u32[]{:S(2)}, u32[]{:S(2)}) %collective-permute-start.14) | collective-permute-done | bytes 1234976 | tf_op jit(solution)/shard_map/ppermute | solution.py:22
  200.1 4.9 %collective-permute-start.17 = (bf16[12,96,384]{2,1,0:T(8,128)(2,1)S(1)}, bf16[12,96,384]{2,1,0:T(8,128)(2,1)S(1)}, u32[]{:S(2)}, u32[]{:S(2)}) collective-permute-start(bf16[12,96,384]{2,1,0:T(8,128)(2,1)S(1)} %shard_map.177.refs_0_.refs_1_), channel_id=1, source_target_pairs={{0,8},{24,16},{8,0},{16,24},{1,9},{25,17},{9,1},{17,25},{2,10},{26... | collective-permute-start | bytes 2654216 | tf_op jit(solution)/shard_map/ppermute | solution.py:22
  208.6 7.9 %convert_dynamic-update-slice_fusion = (bf16[12576,384]{1,0:T(8,128)(2,1)S(1)}, f32[3144,384]{1,0:T(8,128)}) fusion(bf16[12576,384]{1,0:T(8,128)(2,1)S(1)} %broadcast_in_dim.9, s32[]{:T(128)S(6)} %select_n.176, f32[64,3144]{1,0:T(8,128)S(1)} %get-tuple-element.68, f32[384,64]{0,1:T(8,128)S(1)} %copy-done.19, f32[1,1,3144,384]{3,2,1,0:T(8,128)S(1)} %bitcast.83), kind=kOutput, calls=%fused_computation.13 | convolution fusion | flops 930825216 | bytes 12990468 | tf_op jit(solution)/shard_map/dot_general | solution.py:451
  216.6 11.3 %collective-permute-done.29.refs_2_ = bf16[1536,384]{1,0:T(8,128)(2,1)} collective-permute-done((bf16[1536,384]{1,0:T(8,128)(2,1)}, bf16[1536,384]{1,0:T(8,128)(2,1)}, u32[]{:S(2)}, u32[]{:S(2)}) %collective-permute-start.29) | collective-permute-done | bytes 1179680 | tf_op jit(solution)/shard_map/ppermute | solution.py:22
  229.2 15.7 %collective-permute-done.17.refs_0_.refs_1_ = bf16[12,96,384]{2,1,0:T(8,128)(2,1)S(1)} collective-permute-done((bf16[12,96,384]{2,1,0:T(8,128)(2,1)S(1)}, bf16[12,96,384]{2,1,0:T(8,128)(2,1)S(1)}, u32[]{:S(2)}, u32[]{:S(2)}) %collective-permute-start.17) | collective-permute-done | bytes 884768 | tf_op jit(solution)/shard_map/ppermute | solution.py:22
  254.2 2.1 fusion.3
  260.2 11.4 %collective-permute-done.30.refs_0_ = bf16[12,96,384]{2,1,0:T(8,128)(2,1)S(1)} collective-permute-done((bf16[12,96,384]{2,1,0:T(8,128)(2,1)S(1)}, bf16[12,96,384]{2,1,0:T(8,128)(2,1)S(1)}, u32[]{:S(2)}, u32[]{:S(2)}) %collective-permute-start.30) | collective-permute-done | bytes 884768 | tf_op jit(solution)/shard_map/ppermute | solution.py:22
  272.5 25.6 %collective-permute-done.31 = bf16[1608,384]{1,0:T(8,128)(2,1)S(1)} collective-permute-done((bf16[1608,384]{1,0:T(8,128)(2,1)S(1)}, bf16[1608,384]{1,0:T(8,128)(2,1)S(1)}, u32[]{:S(2)}, u32[]{:S(2)}) %collective-permute-start.31) | collective-permute-done | bytes 1234976 | tf_op jit(solution)/shard_map/ppermute | solution.py:22
  298.7 16.3 %collective-permute-done.27.refs_0_ = bf16[12,96,384]{2,1,0:T(8,128)(2,1)S(1)} collective-permute-done((bf16[12,96,384]{2,1,0:T(8,128)(2,1)S(1)}, bf16[12,96,384]{2,1,0:T(8,128)(2,1)S(1)}, u32[]{:S(2)}, u32[]{:S(2)}) %collective-permute-start.27) | collective-permute-done | bytes 884768 | tf_op jit(solution)/shard_map/ppermute | solution.py:22
  (125 shorter events, 60.8 us)
Async XLA Ops:
  4.3 31.9 %collective-permute-start.4 = (bf16[1536,384]{1,0:T(8,128)(2,1)S(1)}, bf16[1536,384]{1,0:T(8,128)(2,1)}, u32[]{:S(2)}, u32[]{:S(2)}) collective-permute-start(bf16[1536,384]{1,0:T(8,128)(2,1)S(1)} %get-tuple-element.40), channel_id=1, source_target_pairs={{8,16},{16,8},{9,17},{17,9},{10,18},{18,10},{11,19},{19,11},{12,20... | collective-permute-start | bytes 3538952 | tf_op jit(solution)/shard_map/ppermute | solution.py:22
  6.1 32.9 %collective-permute-start.3 = (bf16[1536,384]{1,0:T(8,128)(2,1)S(1)}, bf16[1536,384]{1,0:T(8,128)(2,1)S(1)}, u32[]{:S(2)}, u32[]{:S(2)}) collective-permute-start(bf16[1536,384]{1,0:T(8,128)(2,1)S(1)} %get-tuple-element.40), channel_id=1, source_target_pairs={{8,0},{16,24},{9,1},{17,25},{10,2},{18,26},{11,3},{19,27},{12,4},{... | collective-permute-start | bytes 3538952 | tf_op jit(solution)/shard_map/ppermute | solution.py:22
  9.3 26.9 %collective-permute-start.2 = (bf16[12,96,384]{2,1,0:T(8,128)(2,1)S(1)}, bf16[12,96,384]{2,1,0:T(8,128)(2,1)S(1)}, u32[]{:S(2)}, u32[]{:S(2)}) collective-permute-start(bf16[12,96,384]{2,1,0:T(8,128)(2,1)S(1)} %get-tuple-element.39.refs_0_), channel_id=1, source_target_pairs={{0,8},{24,16},{1,9},{25,17},{2,10},{26,18},{3,11},{27,19},{4,12},{... | collective-permute-start | bytes 2654216 | tf_op jit(solution)/shard_map/ppermute | solution.py:22
  16.2 48.3 %collective-permute-start.6 = (bf16[1608,384]{1,0:T(8,128)(2,1)}, bf16[1608,384]{1,0:T(8,128)(2,1)}, u32[]{:S(2)}, u32[]{:S(2)}) collective-permute-start(bf16[1608,384]{1,0:T(8,128)(2,1)} %get-tuple-element.41.refs_0_), channel_id=1, source_target_pairs={{8,0},{16,24},{9,1},{17,25},{10,2},{18,26},{11,3},{19,27},{12,4},{... | collective-permute-start | bytes 3704840 | tf_op jit(solution)/shard_map/ppermute | solution.py:22
  17.5 40.0 %collective-permute-start.1 = (bf16[12,96,384]{2,1,0:T(8,128)(2,1)}, bf16[12,96,384]{2,1,0:T(8,128)(2,1)}, u32[]{:S(2)}, u32[]{:S(2)}) collective-permute-start(bf16[12,96,384]{2,1,0:T(8,128)(2,1)} %get-tuple-element.38.refs_0_), channel_id=1, source_target_pairs={{0,8},{24,16},{1,9},{25,17},{2,10},{26,18},{3,11},{27,19},{4,12},{... | collective-permute-start | bytes 2654216 | tf_op jit(solution)/shard_map/ppermute | solution.py:22
  40.4 25.4 %collective-permute-start.5 = (bf16[12,96,384]{2,1,0:T(8,128)(2,1)}, bf16[12,96,384]{2,1,0:T(8,128)(2,1)}, u32[]{:S(2)}, u32[]{:S(2)}) collective-permute-start(bf16[12,96,384]{2,1,0:T(8,128)(2,1)} %shard_map.171), channel_id=1, source_target_pairs={{8,16},{16,8},{9,17},{17,9},{10,18},{18,10},{11,19},{19,11},{12,20... | collective-permute-start | bytes 2654216 | tf_op jit(solution)/shard_map/ppermute | solution.py:22
  42.0 32.2 %collective-permute-start = (bf16[12,96,384]{2,1,0:T(8,128)(2,1)}, bf16[12,96,384]{2,1,0:T(8,128)(2,1)}, u32[]{:S(2)}, u32[]{:S(2)}) collective-permute-start(bf16[12,96,384]{2,1,0:T(8,128)(2,1)} %get-tuple-element.36.near), channel_id=1, source_target_pairs={{0,8},{24,16},{1,9},{25,17},{2,10},{26,18},{3,11},{27,19},{4,12},{... | collective-permute-start | bytes 2654216 | tf_op jit(solution)/shard_map/ppermute | solution.py:22
  46.8 53.7 %collective-permute-start.10 = (bf16[1608,384]{1,0:T(8,128)(2,1)}, bf16[1608,384]{1,0:T(8,128)(2,1)S(1)}, u32[]{:S(2)}, u32[]{:S(2)}) collective-permute-start(bf16[1608,384]{1,0:T(8,128)(2,1)} %get-tuple-element.41.refs_0_), channel_id=1, source_target_pairs={{8,16},{16,8},{9,17},{17,9},{10,18},{18,10},{11,19},{19,11},{12,20... | collective-permute-start | bytes 3704840 | tf_op jit(solution)/shard_map/ppermute | solution.py:22
  57.5 40.4 %collective-permute-start.11 = (bf16[1536,384]{1,0:T(8,128)(2,1)S(1)}, bf16[1536,384]{1,0:T(8,128)(2,1)S(1)}, u32[]{:S(2)}, u32[]{:S(2)}) collective-permute-start(bf16[1536,384]{1,0:T(8,128)(2,1)S(1)} %copy-done.16), channel_id=1, source_target_pairs={{0,8},{24,16},{1,9},{25,17},{2,10},{26,18},{3,11},{27,19},{4,12},{... | collective-permute-start | bytes 3538952 | tf_op jit(solution)/shard_map/ppermute | solution.py:22
  64.5 36.0 %collective-permute-start.9 = (bf16[1536,384]{1,0:T(8,128)(2,1)}, bf16[1536,384]{1,0:T(8,128)(2,1)}, u32[]{:S(2)}, u32[]{:S(2)}) collective-permute-start(bf16[1536,384]{1,0:T(8,128)(2,1)} %collective-permute-done.4.refs_3_), channel_id=1, source_target_pairs={{8,0},{16,24},{9,1},{17,25},{10,2},{18,26},{11,3},{19,27},{12,4},{... | collective-permute-start | bytes 3538952 | tf_op jit(solution)/shard_map/ppermute | solution.py:22
  68.9 31.6 %collective-permute-start.7 = (bf16[12,96,384]{2,1,0:T(8,128)(2,1)}, bf16[12,96,384]{2,1,0:T(8,128)(2,1)}, u32[]{:S(2)}, u32[]{:S(2)}) collective-permute-start(bf16[12,96,384]{2,1,0:T(8,128)(2,1)} %get-tuple-element.42), channel_id=1, source_target_pairs={{8,16},{16,8},{9,17},{17,9},{10,18},{18,10},{11,19},{19,11},{12,20... | collective-permute-start | bytes 2654216 | tf_op jit(solution)/shard_map/ppermute | solution.py:22
  74.2 38.3 %collective-permute-start.8 = (bf16[12,96,384]{2,1,0:T(8,128)(2,1)}, bf16[12,96,384]{2,1,0:T(8,128)(2,1)}, u32[]{:S(2)}, u32[]{:S(2)}) collective-permute-start(bf16[12,96,384]{2,1,0:T(8,128)(2,1)} %get-tuple-element.43), channel_id=1, source_target_pairs={{8,0},{16,24},{9,1},{17,25},{10,2},{18,26},{11,3},{19,27},{12,4},{... | collective-permute-start | bytes 2654216 | tf_op jit(solution)/shard_map/ppermute | solution.py:22
  99.0 18.9 %collective-permute-start.12 = (bf16[32,12576]{1,0:T(8,128)(2,1)}, bf16[32,12576]{1,0:T(8,128)(2,1)}, u32[]{:S(2)}, u32[]{:S(2)}) collective-permute-start(bf16[32,12576]{1,0:T(8,128)(2,1)} %get-tuple-element.63), channel_id=1, source_target_pairs={{0,1},{1,0},{2,3},{3,2},{4,5},{5,4},{6,7},{7,6},{8,9},{9,8},{10,11... | collective-permute-start | bytes 2414600 | tf_op jit(solution)/shard_map/ppermute | solution.py:424
  119.6 15.6 %collective-permute-start.13 = (bf16[3,32,3144]{2,1,0:T(8,128)(2,1)S(1)}, bf16[3,32,3144]{2,1,0:T(8,128)(2,1)S(1)}, u32[]{:S(2)}, u32[]{:S(2)}) collective-permute-start(bf16[3,32,3144]{2,1,0:T(8,128)(2,1)S(1)} %pad_maximum_fusion), channel_id=1, source_target_pairs={{0,8},{24,16},{1,9},{25,17},{2,10},{26,18},{3,11},{27,19},{4,12},{... | collective-permute-start | bytes 1810952 | tf_op jit(solution)/shard_map/ppermute | solution.py:22
  136.2 17.2 %collective-permute-start.21 = (bf16[32,3144]{1,0:T(8,128)(2,1)S(1)}, bf16[32,3144]{1,0:T(8,128)(2,1)S(1)}, u32[]{:S(2)}, u32[]{:S(2)}) collective-permute-start(bf16[32,3144]{1,0:T(8,128)(2,1)S(1)} %fusion.9), channel_id=1, source_target_pairs={{8,0},{16,24},{9,1},{17,25},{10,2},{18,26},{11,3},{19,27},{12,4},{... | collective-permute-start | bytes 603656 | tf_op jit(solution)/shard_map/ppermute | solution.py:22
  137.6 27.4 %all-to-all-start = ((bf16[4,96,1152]{2,1,0:T(8,128)(2,1)}), bf16[4,96,1152]{2,1,0:T(8,128)(2,1)S(1)}, u32[]{:S(2)}, u32[]{:S(2)}) async-start(bf16[4,96,1152]{2,1,0:T(8,128)(2,1)} %shard_map.173.refs_2_.refs_1_), calls=%async_computation | async-start | bytes 1769472 | tf_op jit(solution)/shard_map/all_to_all | solution.py:433
  153.7 22.0 %collective-permute-start.22 = (bf16[32,3144]{1,0:T(8,128)(2,1)S(1)}, bf16[32,3144]{1,0:T(8,128)(2,1)S(1)}, u32[]{:S(2)}, u32[]{:S(2)}) collective-permute-start(bf16[32,3144]{1,0:T(8,128)(2,1)S(1)} %fusion.12), channel_id=1, source_target_pairs={{0,1},{1,0},{2,3},{3,2},{4,5},{5,4},{6,7},{7,6},{8,9},{9,8},{10,11... | collective-permute-start | bytes 603656 | tf_op jit(solution)/shard_map/ppermute | solution.py:441
  155.3 26.6 %collective-permute-start.15 = (bf16[1536,384]{1,0:T(8,128)(2,1)}, bf16[1536,384]{1,0:T(8,128)(2,1)}, u32[]{:S(2)}, u32[]{:S(2)}) collective-permute-start(bf16[1536,384]{1,0:T(8,128)(2,1)} %copy-done.5), channel_id=1, source_target_pairs={{8,16},{16,8},{9,17},{17,9},{10,18},{18,10},{11,19},{19,11},{12,20... | collective-permute-start | bytes 3538952 | tf_op jit(solution)/shard_map/ppermute | solution.py:22
  157.0 39.8 %collective-permute-start.14 = (bf16[1608,384]{1,0:T(8,128)(2,1)}, bf16[1608,384]{1,0:T(8,128)(2,1)}, u32[]{:S(2)}, u32[]{:S(2)}) collective-permute-start(bf16[1608,384]{1,0:T(8,128)(2,1)} %copy-done.3), channel_id=1, source_target_pairs={{8,0},{16,24},{9,1},{17,25},{10,2},{18,26},{11,3},{19,27},{12,4},{... | collective-permute-start | bytes 3704840 | tf_op jit(solution)/shard_map/ppermute | solution.py:22
  158.3 39.8 %collective-permute-start.19 = (bf16[1608,384]{1,0:T(8,128)(2,1)}, bf16[1608,384]{1,0:T(8,128)(2,1)}, u32[]{:S(2)}, u32[]{:S(2)}) collective-permute-start(bf16[1608,384]{1,0:T(8,128)(2,1)} %shard_map.178), channel_id=1, source_target_pairs={{0,8},{24,16},{1,9},{25,17},{2,10},{26,18},{3,11},{27,19},{4,12},{... | collective-permute-start | bytes 3704840 | tf_op jit(solution)/shard_map/ppermute | solution.py:22
  172.2 26.7 %all-to-all-start.1 = ((bf16[4,96,1152]{2,1,0:T(8,128)(2,1)}), bf16[4,96,1152]{2,1,0:T(8,128)(2,1)S(1)}, u32[]{:S(2)}, u32[]{:S(2)}) async-start(bf16[4,96,1152]{2,1,0:T(8,128)(2,1)} %copy-done.13), calls=%async_computation.1 | async-start | bytes 1769472 | tf_op jit(solution)/shard_map/all_to_all | solution.py:435
  178.7 21.4 %collective-permute-start.23 = (bf16[32,3144]{1,0:T(8,128)(2,1)}, bf16[32,3144]{1,0:T(8,128)(2,1)}, u32[]{:S(2)}, u32[]{:S(2)}) collective-permute-start(bf16[32,3144]{1,0:T(8,128)(2,1)} %dynamic-slice_convert_fusion), channel_id=1, source_target_pairs={{0,8},{8,16},{16,24},{24,0},{1,9},{9,17},{17,25},{25,1},{2,10},{10... | collective-permute-start | bytes 603656 | tf_op jit(solution)/shard_map/ppermute | solution.py:22
  179.7 25.3 %collective-permute-start.24 = (bf16[32,3144]{1,0:T(8,128)(2,1)}, bf16[32,3144]{1,0:T(8,128)(2,1)}, u32[]{:S(2)}, u32[]{:S(2)}) collective-permute-start(bf16[32,3144]{1,0:T(8,128)(2,1)} %dynamic-slice_convert_fusion), channel_id=1, source_target_pairs={{0,16},{8,24},{16,0},{24,8},{1,17},{9,25},{17,1},{25,9},{2,18},{10... | collective-permute-start | bytes 603656 | tf_op jit(solution)/shard_map/ppermute | solution.py:22
  181.9 23.8 %collective-permute-start.25 = (bf16[32,3144]{1,0:T(8,128)(2,1)}, bf16[32,3144]{1,0:T(8,128)(2,1)}, u32[]{:S(2)}, u32[]{:S(2)}) collective-permute-start(bf16[32,3144]{1,0:T(8,128)(2,1)} %dynamic-slice_convert_fusion), channel_id=1, source_target_pairs={{0,24},{8,0},{16,8},{24,16},{1,25},{9,1},{17,9},{25,17},{2,26},{10... | collective-permute-start | bytes 603656 | tf_op jit(solution)/shard_map/ppermute | solution.py:22
  196.8 31.1 %collective-permute-start.29 = (bf16[1536,384]{1,0:T(8,128)(2,1)}, bf16[1536,384]{1,0:T(8,128)(2,1)}, u32[]{:S(2)}, u32[]{:S(2)}) collective-permute-start(bf16[1536,384]{1,0:T(8,128)(2,1)} %collective-permute-done.15.refs_1_), channel_id=1, source_target_pairs={{8,0},{16,24},{9,1},{17,25},{10,2},{18,26},{11,3},{19,27},{12,4},{... | collective-permute-start | bytes 3538952 | tf_op jit(solution)/shard_map/ppermute | solution.py:22
  198.1 52.4 %collective-permute-start.20 = (bf16[1608,384]{1,0:T(8,128)(2,1)}, bf16[1608,384]{1,0:T(8,128)(2,1)S(1)}, u32[]{:S(2)}, u32[]{:S(2)}) collective-permute-start(bf16[1608,384]{1,0:T(8,128)(2,1)} %collective-permute-done.19.refs_1_), channel_id=1, source_target_pairs={{8,16},{16,8},{9,17},{17,9},{10,18},{18,10},{11,19},{19,11},{12,20... | collective-permute-start | bytes 3704840 | tf_op jit(solution)/shard_map/ppermute | solution.py:22
  200.1 44.8 %collective-permute-start.17 = (bf16[12,96,384]{2,1,0:T(8,128)(2,1)S(1)}, bf16[12,96,384]{2,1,0:T(8,128)(2,1)S(1)}, u32[]{:S(2)}, u32[]{:S(2)}) collective-permute-start(bf16[12,96,384]{2,1,0:T(8,128)(2,1)S(1)} %shard_map.177.refs_0_.refs_1_), channel_id=1, source_target_pairs={{0,8},{24,16},{8,0},{16,24},{1,9},{25,17},{9,1},{17,25},{2,10},{26... | collective-permute-start | bytes 2654216 | tf_op jit(solution)/shard_map/ppermute | solution.py:22
  205.0 22.9 %collective-permute-start.28 = (bf16[12,96,384]{2,1,0:T(8,128)(2,1)S(1)}, bf16[12,96,384]{2,1,0:T(8,128)(2,1)S(1)}, u32[]{:S(2)}, u32[]{:S(2)}) collective-permute-start(bf16[12,96,384]{2,1,0:T(8,128)(2,1)S(1)} %shard_map.177.refs_0_.refs_1_), channel_id=1, source_target_pairs={{8,16},{16,8},{9,17},{17,9},{10,18},{18,10},{11,19},{19,11},{12,20... | collective-permute-start | bytes 2654216 | tf_op jit(solution)/shard_map/ppermute | solution.py:22
  207.1 39.4 %collective-permute-start.26 = (bf16[3,32,3144]{2,1,0:T(8,128)(2,1)S(1)}, bf16[3,32,3144]{2,1,0:T(8,128)(2,1)S(1)}, u32[]{:S(2)}, u32[]{:S(2)}) collective-permute-start(bf16[3,32,3144]{2,1,0:T(8,128)(2,1)S(1)} %pad_maximum_fusion.1), channel_id=1, source_target_pairs={{0,1},{1,0},{2,3},{3,2},{4,5},{5,4},{6,7},{7,6},{8,9},{9,8},{10,11... | collective-permute-start | bytes 1810952 | tf_op jit(solution)/shard_map/ppermute | solution.py:460
  227.9 43.7 %collective-permute-start.30 = (bf16[12,96,384]{2,1,0:T(8,128)(2,1)S(1)}, bf16[12,96,384]{2,1,0:T(8,128)(2,1)S(1)}, u32[]{:S(2)}, u32[]{:S(2)}) collective-permute-start(bf16[12,96,384]{2,1,0:T(8,128)(2,1)S(1)} %shard_map.180.refs_1_), channel_id=1, source_target_pairs={{8,0},{16,24},{9,1},{17,25},{10,2},{18,26},{11,3},{19,27},{12,4},{... | collective-permute-start | bytes 2654216 | tf_op jit(solution)/shard_map/ppermute | solution.py:22
  250.5 47.5 %collective-permute-start.31 = (bf16[1608,384]{1,0:T(8,128)(2,1)S(1)}, bf16[1608,384]{1,0:T(8,128)(2,1)S(1)}, u32[]{:S(2)}, u32[]{:S(2)}) collective-permute-start(bf16[1608,384]{1,0:T(8,128)(2,1)S(1)} %collective-permute-done.20.refs_1_), channel_id=1, source_target_pairs={{8,0},{16,24},{9,1},{17,25},{10,2},{18,26},{11,3},{19,27},{12,4},{... | collective-permute-start | bytes 3704840 | tf_op jit(solution)/shard_map/ppermute | solution.py:22
  258.3 56.7 %collective-permute-start.27 = (bf16[12,96,384]{2,1,0:T(8,128)(2,1)S(1)}, bf16[12,96,384]{2,1,0:T(8,128)(2,1)S(1)}, u32[]{:S(2)}, u32[]{:S(2)}) collective-permute-start(bf16[12,96,384]{2,1,0:T(8,128)(2,1)S(1)} %shard_map.179.refs_1_), channel_id=1, source_target_pairs={{8,0},{16,24},{9,1},{17,25},{10,2},{18,26},{11,3},{19,27},{12,4},{... | collective-permute-start | bytes 2654216 | tf_op jit(solution)/shard_map/ppermute | solution.py:22
  (25 other events, 182.2 us)

commit v3 on v2

--- a/solution.py
+++ b/solution.py
@@ -211,6 +211,19 @@
         6 * sum(one.size for one, _ in pairs),
         in_specs=[IN_VMEM] * (2 * count) + [ANYWHERE] * len(others),
     )(*[one for one, _ in pairs], *[two for _, two in pairs], *others)
+
+
+def mean_kernel(count, groups, *refs):
+    refs[-1][...] = (sum(wide(ref[...]) for ref in refs[:count]) / groups).astype(refs[-1].dtype)
+
+
+def mean_after(groups, terms, *others):
+    return kernel_call(
+        functools.partial(mean_kernel, len(terms), groups),
+        jax.ShapeDtypeStruct(terms[0].shape, terms[0].dtype),
+        10 * terms[0].size,
+        in_specs=[IN_VMEM] * len(terms) + [ANYWHERE] * len(others),
+    )(*terms, *others)
 
 
 def narrow_kernel(cut, wide_rows, low, high):
@@ -404,14 +417,6 @@
     middle_sum, last_sum = add_after([(middle, middle_in), (last, far_across)], rows_near[1])
     middle_across = across(middle_sum)
     last_out = to_end(last_sum)
-    rows_inner = [to_inner(low)]
-    pieces = dense.split(
-        near, last, near_in, middle_across, last_out, rows_far[0], rows_across[1], rows_inner[0]
-    )
-    rows_inner.append(to_inner(hold(high, pieces)))
-    rows_across_2 = [across(part) for part in rows_inner]
-    rows_last = [to_end(part) for part in rows_across_2]
-
     terms = lax.dot_general(
         after(basis, far),
         wide(delta_embed[0]),
@@ -421,23 +426,37 @@
     ).astype(jnp.bfloat16)
     keep = lax.dynamic_slice_in_dim(terms, side * half_rank, half_rank, 0)
     give = lax.dynamic_slice_in_dim(terms, (1 - side) * half_rank, half_rank, 0)
-    (kept,) = add_after([(keep, lax.ppermute(give, "tp", SWAP))], pieces)
+    (kept,) = add_after([(keep, lax.ppermute(give, "tp", SWAP))], middle_sum)
 
     def term(place):
         return lax.dynamic_slice_in_dim(kept, block_of(place) * rows, rows, 1)
 
     terms_out = to_inner(jnp.stack([term(3), term(2), term(1)]))
-    terms_middle = across(jnp.stack([add(term(3), terms_out[0]), add(term(2), terms_out[1])]))
-    terms_in = to_end(add(term(0), terms_middle[0]))
+    rows_inner = [to_inner(low)]
+    pieces = dense.split(
+        near, last, near_in, middle_across, last_out, rows_far[0], rows_across[1], rows_inner[0]
+    )
+    rows_inner.append(to_inner(hold(high, pieces)))
+    rows_across_2 = [across(part) for part in rows_inner]
+
+    far_terms, middle_terms = add_after([(term(3), terms_out[0]), (term(2), terms_out[1])], pieces)
+    terms_middle = across(jnp.stack([far_terms, middle_terms]))
 
     moved = lax.all_to_all(pieces, "shard", split_axis=0, concat_axis=0, tiled=True)
-    next_weights, next_momentum, back = dense.update(moved, owner_weights, owner_momentum, terms_out)
-    back = lax.all_to_all(back, "shard", split_axis=0, concat_axis=0, tiled=True)
-    new_block = dense.join(back, rows_far[1], rows_across_2[0], terms_middle)
+    rows_across_2[0] = hold(rows_across_2[0], moved)
+    rows_last = [to_end(part) for part in rows_across_2]
+    next_weights, next_momentum, copies = dense.update(
+        moved, owner_weights, owner_momentum, rows_far[1], rows_across_2[0], rows_inner[1]
+    )
+    (last_terms,) = add_after([(term(0), terms_middle[0])], copies)
+    terms_in = to_end(last_terms)
+    back = lax.all_to_all(copies, "shard", split_axis=0, concat_axis=0, tiled=True)
+    new_block = dense.join(back, rows_last[0], rows_across_2[1])
+    block_near = permute(new_block, NEAR)
+    block_across = across(new_block)
 
     mine = jnp.where(end, term(0), term(1))
-    total = wide(mine) + wide(terms_out[2]) + wide(terms_middle[1]) + wide(terms_in)
-    sent = (total / groups).astype(jnp.bfloat16)
+    sent = mean_after(groups, (mine, terms_out[2], terms_middle[1], terms_in), new_block)
     other = lax.ppermute(sent, "tp", SWAP)
 
     def both(one, two):
@@ -454,15 +473,13 @@
 
     next_embed = embed_owner[0, 0] - update(direction, lax.Precision.HIGHEST)
     half = lax.dynamic_slice_in_dim(direction, side * half_rank, half_rank, 0).astype(jnp.bfloat16)
+    half = after(half, block_near, block_across)
 
     rank = lax.axis_index("rep")
     halves = jnp.stack([permute(half, [(i, (i + step) % groups) for i in range(groups)]) for step in (1, 2, 3)])
     others = lax.ppermute(halves, "tp", SWAP)
-    block_near = permute(new_block, NEAR)
-    block_across = across(new_block)
-    block_across = hold(block_across, rows_inner[1], rows_last[0], terms_in)
     block_far = to_end(block_across)
-    block_across_2 = hold(across(block_near), rows_across_2[1], others)
+    block_across_2 = hold(across(block_near), rows_last[1], others)
     block_last = to_end(block_across_2)
 
     fresh = dense.place(None, 0, new_block, new_block)

time: 317 us -> 283 us (0.89)
  waiting for transfers between devices: 174 us -> 138 us
  local copies, waits for them, and re-layouts: 12.6 us -> 15.8 us
    ppermute x29, waiting for transfers between devices: 174 us -> 135 us  [permute(): return lax.ppermute(value, 'rep', pairs)]
    ppermute x1, waiting for transfers between devices: 0.01 us -> 3.52 us  [local(): other = lax.ppermute(sent, 'tp', SWAP)]
    unnamed x47 -> x55, local copies, waits for them, and re-layouts: 9.6 us -> 11.3 us
    pallas_call x3 -> x5, Pallas kernels: 5.75 us -> 7 us  [add_after(): kernel_call(functools.partial(add_kernel, count), [jax.ShapeDtypeStruct(o...]
  transfers between devices with their start and end apart: 34 -> 34, of which waited for: 15 -> 16; matrix products, arithmetic and copies ran while one was open for 11% -> 13% of each run, Pallas kernels for 5% -> 6%
where the time goes in v3:
time: 283 us; the launch traced here: 282 us
  waiting for transfers between devices  138 us (49%)
  starting transfers between devices  73.3 us (26%)
  matrix products  26.2 us (9%)
  Pallas kernels  20.9 us (7%)
  local copies, waits for them, and re-layouts  15.8 us (6%)
  other arithmetic  5.69 us (2%)
    ppermute x29, waiting for transfers between devices, permute(): return lax.ppermute(value, 'rep', pairs)  135 us
    ppermute x29, starting transfers between devices, permute(): return lax.ppermute(value, 'rep', pairs)  62.5 us
    dot_general x7, matrix products, update(): lax.dot_general(toward, basis, (((0,), (1,)), ((), ())), precision=precis...  16.6 us
    unnamed x55, local copies, waits for them, and re-layouts  11.3 us
    dot_general x1, matrix products, local(): lax.dot_general(after(basis, far), wide(delta_embed[0]), (((0,), (1,)), (...  9.62 us
    pallas_call x5, Pallas kernels, add_after(): kernel_call(functools.partial(add_kernel, count), [jax.ShapeDtypeStruct(o...  7 us
  transfers between devices with their start and end apart: 34, of which 16 were waited for; matrix products, arithmetic and copies ran while one was open for 13% of the time, Pallas kernels for 6%

profile of v3, /device:TPU:0, one launch (start us, length us, event | category | flops | bytes accessed | tf_op | source)
XLA Modules:
  0.0 281.6 jit_solution(12846624204107866177)
XLA Ops:
  0.7 2.4 copy-done
  9.7 7.7 %collective-permute-start.2 = (bf16[12,96,384]{2,1,0:T(8,128)(2,1)S(1)}, bf16[12,96,384]{2,1,0:T(8,128)(2,1)}, u32[]{:S(2)}, u32[]{:S(2)}) collective-permute-start(bf16[12,96,384]{2,1,0:T(8,128)(2,1)S(1)} %get-tuple-element.41.refs_0_), channel_id=1, source_target_pairs={{0,8},{24,16},{1,9},{25,17},{2,10},{26,18},{3,11},{27,19},{4,12},{... | collective-permute-start | bytes 2654216 | tf_op jit(solution)/shard_map/ppermute | solution.py:22
  17.4 2.2 collective-permute-start.1
  21.1 9.6 %convolution_convert_fusion = bf16[64,12576]{1,0:T(8,128)(2,1)S(1)} fusion(f32[384,64]{1,0:T(8,128)S(1)} %shard_map.178, bf16[1,12576,384]{2,1,0:T(8,128)(2,1)} %param.16), kind=kOutput, calls=%fused_computation | convolution fusion | flops 1855211520 | bytes 11366400 | tf_op jit(solution)/shard_map/dot_general | solution.py:420
  30.7 5.8 %collective-permute-done.2.refs_1_ = bf16[12,96,384]{2,1,0:T(8,128)(2,1)} collective-permute-done((bf16[12,96,384]{2,1,0:T(8,128)(2,1)S(1)}, bf16[12,96,384]{2,1,0:T(8,128)(2,1)}, u32[]{:S(2)}, u32[]{:S(2)}) %collective-permute-start.2) | collective-permute-done | bytes 884768 | tf_op jit(solution)/shard_map/ppermute | solution.py:22
  36.6 3.1 %collective-permute-done.3.refs_2_ = bf16[1536,384]{1,0:T(8,128)(2,1)S(1)} collective-permute-done((bf16[1536,384]{1,0:T(8,128)(2,1)}, bf16[1536,384]{1,0:T(8,128)(2,1)S(1)}, u32[]{:S(2)}, u32[]{:S(2)}) %collective-permute-start.3) | collective-permute-done | bytes 1179680 | tf_op jit(solution)/shard_map/ppermute | solution.py:22
  39.7 2.7 shard_map.171
  46.6 3.9 %collective-permute-start = (bf16[12,96,384]{2,1,0:T(8,128)(2,1)}, bf16[12,96,384]{2,1,0:T(8,128)(2,1)S(1)}, u32[]{:S(2)}, u32[]{:S(2)}) collective-permute-start(bf16[12,96,384]{2,1,0:T(8,128)(2,1)} %get-tuple-element.38.near), channel_id=1, source_target_pairs={{0,8},{24,16},{1,9},{25,17},{2,10},{26,18},{3,11},{27,19},{4,12},{... | collective-permute-start | bytes 2654216 | tf_op jit(solution)/shard_map/ppermute | solution.py:22
  50.5 5.2 %collective-permute-done.1.refs_2_ = bf16[12,96,384]{2,1,0:T(8,128)(2,1)} collective-permute-done((bf16[12,96,384]{2,1,0:T(8,128)(2,1)}, bf16[12,96,384]{2,1,0:T(8,128)(2,1)}, u32[]{:S(2)}, u32[]{:S(2)}) %collective-permute-start.1) | collective-permute-done | bytes 884768 | tf_op jit(solution)/shard_map/ppermute | solution.py:22
  55.6 5.5 %collective-permute-start.11 = (bf16[1536,384]{1,0:T(8,128)(2,1)}, bf16[1536,384]{1,0:T(8,128)(2,1)}, u32[]{:S(2)}, u32[]{:S(2)}) collective-permute-start(bf16[1536,384]{1,0:T(8,128)(2,1)} %get-tuple-element.42), channel_id=1, source_target_pairs={{0,8},{24,16},{1,9},{25,17},{2,10},{26,18},{3,11},{27,19},{4,12},{... | collective-permute-start | bytes 3538952 | tf_op jit(solution)/shard_map/ppermute | solution.py:22
  61.1 3.9 %collective-permute-done.6.refs_4_ = bf16[1608,384]{1,0:T(8,128)(2,1)} collective-permute-done((bf16[1608,384]{1,0:T(8,128)(2,1)}, bf16[1608,384]{1,0:T(8,128)(2,1)}, u32[]{:S(2)}, u32[]{:S(2)}) %collective-permute-start.6) | collective-permute-done | bytes 1234976 | tf_op jit(solution)/shard_map/ppermute | solution.py:22
  76.0 22.4 %collective-permute-done.11.refs_2_ = bf16[1536,384]{1,0:T(8,128)(2,1)} collective-permute-done((bf16[1536,384]{1,0:T(8,128)(2,1)}, bf16[1536,384]{1,0:T(8,128)(2,1)}, u32[]{:S(2)}, u32[]{:S(2)}) %collective-permute-start.11) | collective-permute-done | bytes 1179680 | tf_op jit(solution)/shard_map/ppermute | solution.py:22
  98.4 4.4 %collective-permute-start.21 = (bf16[3,32,3144]{2,1,0:T(8,128)(2,1)S(1)}, bf16[3,32,3144]{2,1,0:T(8,128)(2,1)S(1)}, u32[]{:S(2)}, u32[]{:S(2)}) collective-permute-start(bf16[3,32,3144]{2,1,0:T(8,128)(2,1)S(1)} %pad_maximum_fusion), channel_id=1, source_target_pairs={{0,8},{24,16},{1,9},{25,17},{2,10},{26,18},{3,11},{27,19},{4,12},{... | collective-permute-start | bytes 1810952 | tf_op jit(solution)/shard_map/ppermute | solution.py:22
  104.9 11.9 %collective-permute-done.8.from_in = bf16[12,96,384]{2,1,0:T(8,128)(2,1)S(1)} collective-permute-done((bf16[12,96,384]{2,1,0:T(8,128)(2,1)S(1)}, bf16[12,96,384]{2,1,0:T(8,128)(2,1)S(1)}, u32[]{:S(2)}, u32[]{:S(2)}) %collective-permute-start.8) | collective-permute-done | bytes 884768 | tf_op jit(solution)/shard_map/ppermute | solution.py:22
  116.8 2.8 shard_map.173.refs_1_.refs_4_
  119.6 2.5 collective-permute-start.14
  122.8 3.5 %all-to-all-start = ((bf16[4,96,1152]{2,1,0:T(8,128)(2,1)}), bf16[4,96,1152]{2,1,0:T(8,128)(2,1)S(1)}, u32[]{:S(2)}, u32[]{:S(2)}) async-start(bf16[4,96,1152]{2,1,0:T(8,128)(2,1)} %shard_map.173.refs_1_.refs_4_), calls=%async_computation | async-start | bytes 1769472 | tf_op jit(solution)/shard_map/all_to_all | solution.py:445
  128.6 15.3 %collective-permute-done.14.refs_2_ = bf16[1608,384]{1,0:T(8,128)(2,1)} collective-permute-done((bf16[1608,384]{1,0:T(8,128)(2,1)}, bf16[1608,384]{1,0:T(8,128)(2,1)}, u32[]{:S(2)}, u32[]{:S(2)}) %collective-permute-start.14) | collective-permute-done | bytes 1234976 | tf_op jit(solution)/shard_map/ppermute | solution.py:22
  147.9 3.5 %shard_map.176 = (f32[3456,128]{1,0:T(8,128)}, f32[3456,128]{1,0:T(8,128)}, bf16[4,96,1152]{2,1,0:T(8,128)(2,1)}) custom-call(bf16[4,96,1152]{2,1,0:T(8,128)(2,1)S(1)} %all-to-all-done.refs_1_.moved, f32[3456,128]{1,0:T(8,128)S(1)} %bitcast.67, f32[3456,128]{1,0:T(8,128)S(1)} %bitcast.68, bf16[1608,384]{1,0:T(8,128)(2,1)} %collective-permute-done.12.refs_0_, ...), custom_call_target="tpu_custom_call" | custom-call | bytes 8847360 | tf_op jit(solution)/shard_map/pallas_call | solution.py:350
  151.4 3.6 %all-to-all-start.1 = ((bf16[4,96,1152]{2,1,0:T(8,128)(2,1)}), bf16[4,96,1152]{2,1,0:T(8,128)(2,1)S(1)}, u32[]{:S(2)}, u32[]{:S(2)}) async-start(bf16[4,96,1152]{2,1,0:T(8,128)(2,1)} %get-tuple-element.46.refs_2_), calls=%async_computation.1 | async-start | bytes 1769472 | tf_op jit(solution)/shard_map/all_to_all | solution.py:453
  158.8 16.3 %collective-permute-done.15.refs_0_ = bf16[1536,384]{1,0:T(8,128)(2,1)} collective-permute-done((bf16[1536,384]{1,0:T(8,128)(2,1)S(1)}, bf16[1536,384]{1,0:T(8,128)(2,1)}, u32[]{:S(2)}, u32[]{:S(2)}) %collective-permute-start.15) | collective-permute-done | bytes 1179680 | tf_op jit(solution)/shard_map/ppermute | solution.py:22
  183.0 3.5 %collective-permute-done.24 = bf16[32,3144]{1,0:T(8,128)(2,1)S(1)} collective-permute-done((bf16[32,3144]{1,0:T(8,128)(2,1)S(1)}, bf16[32,3144]{1,0:T(8,128)(2,1)S(1)}, u32[]{:S(2)}, u32[]{:S(2)}) %collective-permute-start.24) | collective-permute-done | bytes 201248 | tf_op jit(solution)/shard_map/ppermute | solution.py:460
  186.5 2.2 fusion.8
  188.7 11.8 %collective-permute-done.17.refs_0_.refs_1_ = bf16[12,96,384]{2,1,0:T(8,128)(2,1)S(1)} collective-permute-done((bf16[12,96,384]{2,1,0:T(8,128)(2,1)S(1)}, bf16[12,96,384]{2,1,0:T(8,128)(2,1)S(1)}, u32[]{:S(2)}, u32[]{:S(2)}) %collective-permute-start.17) | collective-permute-done | bytes 884768 | tf_op jit(solution)/shard_map/ppermute | solution.py:22
  201.5 10.6 %collective-permute-start.26 = (bf16[32,3144]{1,0:T(8,128)(2,1)S(1)}, bf16[32,3144]{1,0:T(8,128)(2,1)S(1)}, u32[]{:S(2)}, u32[]{:S(2)}) collective-permute-start(bf16[32,3144]{1,0:T(8,128)(2,1)S(1)} %shard_map.183), channel_id=1, source_target_pairs={{0,8},{8,16},{16,24},{24,0},{1,9},{9,17},{17,25},{25,1},{2,10},{10... | collective-permute-start | bytes 603656 | tf_op jit(solution)/shard_map/ppermute | solution.py:22
  212.0 2.4 collective-permute-start.28
  216.6 3.9 %collective-permute-done.27 = bf16[32,3144]{1,0:T(8,128)(2,1)} collective-permute-done((bf16[32,3144]{1,0:T(8,128)(2,1)S(1)}, bf16[32,3144]{1,0:T(8,128)(2,1)}, u32[]{:S(2)}, u32[]{:S(2)}) %collective-permute-start.27) | collective-permute-done | bytes 201248 | tf_op jit(solution)/shard_map/ppermute | solution.py:22
  225.4 8.0 %convert_dynamic-update-slice_fusion = (bf16[12576,384]{1,0:T(8,128)(2,1)S(1)}, f32[3144,384]{1,0:T(8,128)}) fusion(bf16[12576,384]{1,0:T(8,128)(2,1)S(1)} %broadcast_in_dim.9, s32[]{:T(128)S(6)} %select_n.176, f32[64,3144]{1,0:T(8,128)S(1)} %copy-done.22, f32[384,64]{0,1:T(8,128)S(1)} %copy-done.24, f32[1,1,3144,384]{3,2,1,0:T(8,128)S(1)} %bitcast.64), kind=kOutput, calls=%fused_computation.13 | convolution fusion | flops 930825216 | bytes 12990468 | tf_op jit(solution)/shard_map/dot_general | solution.py:470
  238.4 2.2 fusion.2
  241.4 7.3 %collective-permute-done.19.refs_1_ = bf16[1608,384]{1,0:T(8,128)(2,1)S(1)} collective-permute-done((bf16[1608,384]{1,0:T(8,128)(2,1)}, bf16[1608,384]{1,0:T(8,128)(2,1)S(1)}, u32[]{:S(2)}, u32[]{:S(2)}) %collective-permute-start.19) | collective-permute-done | bytes 1234976 | tf_op jit(solution)/shard_map/ppermute | solution.py:22
  255.0 12.7 %collective-permute-done.31.refs_0_ = bf16[12,96,384]{2,1,0:T(8,128)(2,1)S(1)} collective-permute-done((bf16[12,96,384]{2,1,0:T(8,128)(2,1)S(1)}, bf16[12,96,384]{2,1,0:T(8,128)(2,1)S(1)}, u32[]{:S(2)}, u32[]{:S(2)}) %collective-permute-start.31) | collective-permute-done | bytes 884768 | tf_op jit(solution)/shard_map/ppermute | solution.py:22
  268.6 11.9 %collective-permute-done.30.refs_0_ = bf16[12,96,384]{2,1,0:T(8,128)(2,1)S(1)} collective-permute-done((bf16[12,96,384]{2,1,0:T(8,128)(2,1)S(1)}, bf16[12,96,384]{2,1,0:T(8,128)(2,1)S(1)}, u32[]{:S(2)}, u32[]{:S(2)}) %collective-permute-start.30) | collective-permute-done | bytes 884768 | tf_op jit(solution)/shard_map/ppermute | solution.py:22
  (134 shorter events, 65.3 us)
Async XLA Ops:
  4.7 31.9 %collective-permute-start.4 = (bf16[1536,384]{1,0:T(8,128)(2,1)}, bf16[1536,384]{1,0:T(8,128)(2,1)}, u32[]{:S(2)}, u32[]{:S(2)}) collective-permute-start(bf16[1536,384]{1,0:T(8,128)(2,1)} %get-tuple-element.42), channel_id=1, source_target_pairs={{8,16},{16,8},{9,17},{17,9},{10,18},{18,10},{11,19},{19,11},{12,20... | collective-permute-start | bytes 3538952 | tf_op jit(solution)/shard_map/ppermute | solution.py:22
  6.5 33.1 %collective-permute-start.3 = (bf16[1536,384]{1,0:T(8,128)(2,1)}, bf16[1536,384]{1,0:T(8,128)(2,1)S(1)}, u32[]{:S(2)}, u32[]{:S(2)}) collective-permute-start(bf16[1536,384]{1,0:T(8,128)(2,1)} %get-tuple-element.42), channel_id=1, source_target_pairs={{8,0},{16,24},{9,1},{17,25},{10,2},{18,26},{11,3},{19,27},{12,4},{... | collective-permute-start | bytes 3538952 | tf_op jit(solution)/shard_map/ppermute | solution.py:22
  9.7 26.9 %collective-permute-start.2 = (bf16[12,96,384]{2,1,0:T(8,128)(2,1)S(1)}, bf16[12,96,384]{2,1,0:T(8,128)(2,1)}, u32[]{:S(2)}, u32[]{:S(2)}) collective-permute-start(bf16[12,96,384]{2,1,0:T(8,128)(2,1)S(1)} %get-tuple-element.41.refs_0_), channel_id=1, source_target_pairs={{0,8},{24,16},{1,9},{25,17},{2,10},{26,18},{3,11},{27,19},{4,12},{... | collective-permute-start | bytes 2654216 | tf_op jit(solution)/shard_map/ppermute | solution.py:22
  17.4 38.2 %collective-permute-start.1 = (bf16[12,96,384]{2,1,0:T(8,128)(2,1)}, bf16[12,96,384]{2,1,0:T(8,128)(2,1)}, u32[]{:S(2)}, u32[]{:S(2)}) collective-permute-start(bf16[12,96,384]{2,1,0:T(8,128)(2,1)} %get-tuple-element.40.refs_0_), channel_id=1, source_target_pairs={{0,8},{24,16},{1,9},{25,17},{2,10},{26,18},{3,11},{27,19},{4,12},{... | collective-permute-start | bytes 2654216 | tf_op jit(solution)/shard_map/ppermute | solution.py:22
  19.6 45.5 %collective-permute-start.6 = (bf16[1608,384]{1,0:T(8,128)(2,1)}, bf16[1608,384]{1,0:T(8,128)(2,1)}, u32[]{:S(2)}, u32[]{:S(2)}) collective-permute-start(bf16[1608,384]{1,0:T(8,128)(2,1)} %get-tuple-element.43.refs_0_), channel_id=1, source_target_pairs={{8,0},{16,24},{9,1},{17,25},{10,2},{18,26},{11,3},{19,27},{12,4},{... | collective-permute-start | bytes 3704840 | tf_op jit(solution)/shard_map/ppermute | solution.py:22
  42.4 24.4 %collective-permute-start.5 = (bf16[12,96,384]{2,1,0:T(8,128)(2,1)}, bf16[12,96,384]{2,1,0:T(8,128)(2,1)}, u32[]{:S(2)}, u32[]{:S(2)}) collective-permute-start(bf16[12,96,384]{2,1,0:T(8,128)(2,1)} %shard_map.171), channel_id=1, source_target_pairs={{8,16},{16,8},{9,17},{17,9},{10,18},{18,10},{11,19},{19,11},{12,20... | collective-permute-start | bytes 2654216 | tf_op jit(solution)/shard_map/ppermute | solution.py:22
  45.1 25.2 %collective-permute-start.20 = (bf16[32,12576]{1,0:T(8,128)(2,1)}, bf16[32,12576]{1,0:T(8,128)(2,1)}, u32[]{:S(2)}, u32[]{:S(2)}) collective-permute-start(bf16[32,12576]{1,0:T(8,128)(2,1)} %get-tuple-element.69), channel_id=1, source_target_pairs={{0,1},{1,0},{2,3},{3,2},{4,5},{5,4},{6,7},{7,6},{8,9},{9,8},{10,11... | collective-permute-start | bytes 2414600 | tf_op jit(solution)/shard_map/ppermute | solution.py:429
  46.6 28.0 %collective-permute-start = (bf16[12,96,384]{2,1,0:T(8,128)(2,1)}, bf16[12,96,384]{2,1,0:T(8,128)(2,1)S(1)}, u32[]{:S(2)}, u32[]{:S(2)}) collective-permute-start(bf16[12,96,384]{2,1,0:T(8,128)(2,1)} %get-tuple-element.38.near), channel_id=1, source_target_pairs={{0,8},{24,16},{1,9},{25,17},{2,10},{26,18},{3,11},{27,19},{4,12},{... | collective-permute-start | bytes 2654216 | tf_op jit(solution)/shard_map/ppermute | solution.py:22
  55.6 42.8 %collective-permute-start.11 = (bf16[1536,384]{1,0:T(8,128)(2,1)}, bf16[1536,384]{1,0:T(8,128)(2,1)}, u32[]{:S(2)}, u32[]{:S(2)}) collective-permute-start(bf16[1536,384]{1,0:T(8,128)(2,1)} %get-tuple-element.42), channel_id=1, source_target_pairs={{0,8},{24,16},{1,9},{25,17},{2,10},{26,18},{3,11},{27,19},{4,12},{... | collective-permute-start | bytes 3538952 | tf_op jit(solution)/shard_map/ppermute | solution.py:22
  65.1 37.7 %collective-permute-start.10 = (bf16[1608,384]{1,0:T(8,128)(2,1)}, bf16[1608,384]{1,0:T(8,128)(2,1)}, u32[]{:S(2)}, u32[]{:S(2)}) collective-permute-start(bf16[1608,384]{1,0:T(8,128)(2,1)} %get-tuple-element.43.refs_0_), channel_id=1, source_target_pairs={{8,16},{16,8},{9,17},{17,9},{10,18},{18,10},{11,19},{19,11},{12,20... | collective-permute-start | bytes 3704840 | tf_op jit(solution)/shard_map/ppermute | solution.py:22
  66.8 36.8 %collective-permute-start.9 = (bf16[1536,384]{1,0:T(8,128)(2,1)}, bf16[1536,384]{1,0:T(8,128)(2,1)S(1)}, u32[]{:S(2)}, u32[]{:S(2)}) collective-permute-start(bf16[1536,384]{1,0:T(8,128)(2,1)} %collective-permute-done.4.refs_3_), channel_id=1, source_target_pairs={{8,0},{16,24},{9,1},{17,25},{10,2},{18,26},{11,3},{19,27},{12,4},{... | collective-permute-start | bytes 3538952 | tf_op jit(solution)/shard_map/ppermute | solution.py:22
  70.2 34.7 %collective-permute-start.7 = (bf16[12,96,384]{2,1,0:T(8,128)(2,1)S(1)}, bf16[12,96,384]{2,1,0:T(8,128)(2,1)S(1)}, u32[]{:S(2)}, u32[]{:S(2)}) collective-permute-start(bf16[12,96,384]{2,1,0:T(8,128)(2,1)S(1)} %get-tuple-element.44.refs_2_), channel_id=1, source_target_pairs={{8,16},{16,8},{9,17},{17,9},{10,18},{18,10},{11,19},{19,11},{12,20... | collective-permute-start | bytes 2654216 | tf_op jit(solution)/shard_map/ppermute | solution.py:22
  74.6 42.2 %collective-permute-start.8 = (bf16[12,96,384]{2,1,0:T(8,128)(2,1)S(1)}, bf16[12,96,384]{2,1,0:T(8,128)(2,1)S(1)}, u32[]{:S(2)}, u32[]{:S(2)}) collective-permute-start(bf16[12,96,384]{2,1,0:T(8,128)(2,1)S(1)} %get-tuple-element.45), channel_id=1, source_target_pairs={{8,0},{16,24},{9,1},{17,25},{10,2},{18,26},{11,3},{19,27},{12,4},{... | collective-permute-start | bytes 2654216 | tf_op jit(solution)/shard_map/ppermute | solution.py:22
  98.4 23.7 %collective-permute-start.21 = (bf16[3,32,3144]{2,1,0:T(8,128)(2,1)S(1)}, bf16[3,32,3144]{2,1,0:T(8,128)(2,1)S(1)}, u32[]{:S(2)}, u32[]{:S(2)}) collective-permute-start(bf16[3,32,3144]{2,1,0:T(8,128)(2,1)S(1)} %pad_maximum_fusion), channel_id=1, source_target_pairs={{0,8},{24,16},{1,9},{25,17},{2,10},{26,18},{3,11},{27,19},{4,12},{... | collective-permute-start | bytes 1810952 | tf_op jit(solution)/shard_map/ppermute | solution.py:22
  102.8 41.9 %collective-permute-start.13 = (bf16[1536,384]{1,0:T(8,128)(2,1)}, bf16[1536,384]{1,0:T(8,128)(2,1)S(1)}, u32[]{:S(2)}, u32[]{:S(2)}) collective-permute-start(bf16[1536,384]{1,0:T(8,128)(2,1)} %collective-permute-done.11.refs_2_), channel_id=1, source_target_pairs={{8,16},{16,8},{9,17},{17,9},{10,18},{18,10},{11,19},{19,11},{12,20... | collective-permute-start | bytes 3538952 | tf_op jit(solution)/shard_map/ppermute | solution.py:22
  103.6 42.8 %collective-permute-start.12 = (bf16[1608,384]{1,0:T(8,128)(2,1)}, bf16[1608,384]{1,0:T(8,128)(2,1)}, u32[]{:S(2)}, u32[]{:S(2)}) collective-permute-start(bf16[1608,384]{1,0:T(8,128)(2,1)} %collective-permute-done.10.refs_1_), channel_id=1, source_target_pairs={{8,0},{16,24},{9,1},{17,25},{10,2},{18,26},{11,3},{19,27},{12,4},{... | collective-permute-start | bytes 3704840 | tf_op jit(solution)/shard_map/ppermute | solution.py:22
  119.6 24.4 %collective-permute-start.14 = (bf16[1608,384]{1,0:T(8,128)(2,1)}, bf16[1608,384]{1,0:T(8,128)(2,1)}, u32[]{:S(2)}, u32[]{:S(2)}) collective-permute-start(bf16[1608,384]{1,0:T(8,128)(2,1)} %shard_map.175), channel_id=1, source_target_pairs={{0,8},{24,16},{1,9},{25,17},{2,10},{26,18},{3,11},{27,19},{4,12},{... | collective-permute-start | bytes 3704840 | tf_op jit(solution)/shard_map/ppermute | solution.py:22
  122.8 21.9 %all-to-all-start = ((bf16[4,96,1152]{2,1,0:T(8,128)(2,1)}), bf16[4,96,1152]{2,1,0:T(8,128)(2,1)S(1)}, u32[]{:S(2)}, u32[]{:S(2)}) async-start(bf16[4,96,1152]{2,1,0:T(8,128)(2,1)} %shard_map.173.refs_1_.refs_4_), calls=%async_computation | async-start | bytes 1769472 | tf_op jit(solution)/shard_map/all_to_all | solution.py:445
  127.2 27.8 %collective-permute-start.22 = (bf16[2,32,3144]{2,1,0:T(8,128)(2,1)}, bf16[2,32,3144]{2,1,0:T(8,128)(2,1)}, u32[]{:S(2)}, u32[]{:S(2)}) collective-permute-start(bf16[2,32,3144]{2,1,0:T(8,128)(2,1)} %pad_maximum_fusion.2), channel_id=1, source_target_pairs={{8,16},{16,8},{9,17},{17,9},{10,18},{18,10},{11,19},{19,11},{12,20... | collective-permute-start | bytes 1207304 | tf_op jit(solution)/shard_map/ppermute | solution.py:22
  144.0 31.1 %collective-permute-start.16 = (bf16[1608,384]{1,0:T(8,128)(2,1)}, bf16[1608,384]{1,0:T(8,128)(2,1)S(1)}, u32[]{:S(2)}, u32[]{:S(2)}) collective-permute-start(bf16[1608,384]{1,0:T(8,128)(2,1)} %collective-permute-done.14.refs_2_), channel_id=1, source_target_pairs={{8,16},{16,8},{9,17},{17,9},{10,18},{18,10},{11,19},{19,11},{12,20... | collective-permute-start | bytes 3704840 | tf_op jit(solution)/shard_map/ppermute | solution.py:22
  144.8 30.4 %collective-permute-start.15 = (bf16[1536,384]{1,0:T(8,128)(2,1)S(1)}, bf16[1536,384]{1,0:T(8,128)(2,1)}, u32[]{:S(2)}, u32[]{:S(2)}) collective-permute-start(bf16[1536,384]{1,0:T(8,128)(2,1)S(1)} %shard_map.174.refs_1_), channel_id=1, source_target_pairs={{8,0},{16,24},{9,1},{17,25},{10,2},{18,26},{11,3},{19,27},{12,4},{... | collective-permute-start | bytes 3538952 | tf_op jit(solution)/shard_map/ppermute | solution.py:22
  151.4 23.7 %all-to-all-start.1 = ((bf16[4,96,1152]{2,1,0:T(8,128)(2,1)}), bf16[4,96,1152]{2,1,0:T(8,128)(2,1)S(1)}, u32[]{:S(2)}, u32[]{:S(2)}) async-start(bf16[4,96,1152]{2,1,0:T(8,128)(2,1)} %get-tuple-element.46.refs_2_), calls=%async_computation.1 | async-start | bytes 1769472 | tf_op jit(solution)/shard_map/all_to_all | solution.py:453
  157.5 20.2 %collective-permute-start.23 = (bf16[32,3144]{1,0:T(8,128)(2,1)}, bf16[32,3144]{1,0:T(8,128)(2,1)S(1)}, u32[]{:S(2)}, u32[]{:S(2)}) collective-permute-start(bf16[32,3144]{1,0:T(8,128)(2,1)} %shard_map.181), channel_id=1, source_target_pairs={{8,0},{16,24},{9,1},{17,25},{10,2},{18,26},{11,3},{19,27},{12,4},{... | collective-permute-start | bytes 603656 | tf_op jit(solution)/shard_map/ppermute | solution.py:22
  182.2 18.2 %collective-permute-start.17 = (bf16[12,96,384]{2,1,0:T(8,128)(2,1)S(1)}, bf16[12,96,384]{2,1,0:T(8,128)(2,1)S(1)}, u32[]{:S(2)}, u32[]{:S(2)}) collective-permute-start(bf16[12,96,384]{2,1,0:T(8,128)(2,1)S(1)} %shard_map.177.refs_4_.refs_0_.refs_1_), channel_id=1, source_target_pairs={{0,8},{24,16},{8,0},{16,24},{1,9},{25,17},{9,1},{17,25},{2,10},{26... | collective-permute-start | bytes 2654216 | tf_op jit(solution)/shard_map/ppermute | solution.py:22
  182.3 18.2 %collective-permute-start.25 = (bf16[12,96,384]{2,1,0:T(8,128)(2,1)S(1)}, bf16[12,96,384]{2,1,0:T(8,128)(2,1)S(1)}, u32[]{:S(2)}, u32[]{:S(2)}) collective-permute-start(bf16[12,96,384]{2,1,0:T(8,128)(2,1)S(1)} %shard_map.177.refs_4_.refs_0_.refs_1_), channel_id=1, source_target_pairs={{8,16},{16,8},{9,17},{17,9},{10,18},{18,10},{11,19},{19,11},{12,20... | collective-permute-start | bytes 2654216 | tf_op jit(solution)/shard_map/ppermute | solution.py:22
  201.5 15.2 %collective-permute-start.26 = (bf16[32,3144]{1,0:T(8,128)(2,1)S(1)}, bf16[32,3144]{1,0:T(8,128)(2,1)S(1)}, u32[]{:S(2)}, u32[]{:S(2)}) collective-permute-start(bf16[32,3144]{1,0:T(8,128)(2,1)S(1)} %shard_map.183), channel_id=1, source_target_pairs={{0,8},{8,16},{16,24},{24,0},{1,9},{9,17},{17,25},{25,1},{2,10},{10... | collective-permute-start | bytes 603656 | tf_op jit(solution)/shard_map/ppermute | solution.py:22
  212.0 10.3 %collective-permute-start.28 = (bf16[32,3144]{1,0:T(8,128)(2,1)S(1)}, bf16[32,3144]{1,0:T(8,128)(2,1)}, u32[]{:S(2)}, u32[]{:S(2)}) collective-permute-start(bf16[32,3144]{1,0:T(8,128)(2,1)S(1)} %shard_map.183), channel_id=1, source_target_pairs={{0,24},{8,0},{16,8},{24,16},{1,25},{9,1},{17,9},{25,17},{2,26},{10... | collective-permute-start | bytes 603656 | tf_op jit(solution)/shard_map/ppermute | solution.py:22
  215.3 33.4 %collective-permute-start.19 = (bf16[1608,384]{1,0:T(8,128)(2,1)}, bf16[1608,384]{1,0:T(8,128)(2,1)S(1)}, u32[]{:S(2)}, u32[]{:S(2)}) collective-permute-start(bf16[1608,384]{1,0:T(8,128)(2,1)} %copy-done.5), channel_id=1, source_target_pairs={{8,0},{16,24},{9,1},{17,25},{10,2},{18,26},{11,3},{19,27},{12,4},{... | collective-permute-start | bytes 3704840 | tf_op jit(solution)/shard_map/ppermute | solution.py:22
  223.7 12.8 %collective-permute-start.29 = (bf16[3,32,3144]{2,1,0:T(8,128)(2,1)S(1)}, bf16[3,32,3144]{2,1,0:T(8,128)(2,1)S(1)}, u32[]{:S(2)}, u32[]{:S(2)}) collective-permute-start(bf16[3,32,3144]{2,1,0:T(8,128)(2,1)S(1)} %pad_maximum_fusion.1), channel_id=1, source_target_pairs={{0,1},{1,0},{2,3},{3,2},{4,5},{5,4},{6,7},{7,6},{8,9},{9,8},{10,11... | collective-permute-start | bytes 1810952 | tf_op jit(solution)/shard_map/ppermute | solution.py:480
  233.4 34.3 %collective-permute-start.31 = (bf16[12,96,384]{2,1,0:T(8,128)(2,1)S(1)}, bf16[12,96,384]{2,1,0:T(8,128)(2,1)S(1)}, u32[]{:S(2)}, u32[]{:S(2)}) collective-permute-start(bf16[12,96,384]{2,1,0:T(8,128)(2,1)S(1)} %copy-done.2), channel_id=1, source_target_pairs={{8,0},{16,24},{9,1},{17,25},{10,2},{18,26},{11,3},{19,27},{12,4},{... | collective-permute-start | bytes 2654216 | tf_op jit(solution)/shard_map/ppermute | solution.py:22
  234.7 14.0 %collective-permute-start.18 = (bf16[12,96,384]{2,1,0:T(8,128)(2,1)S(1)}, bf16[12,96,384]{2,1,0:T(8,128)(2,1)S(1)}, u32[]{:S(2)}, u32[]{:S(2)}) collective-permute-start(bf16[12,96,384]{2,1,0:T(8,128)(2,1)S(1)} %collective-permute-done.17.refs_0_.refs_1_), channel_id=1, source_target_pairs={{8,16},{16,8},{9,17},{17,9},{10,18},{18,10},{11,19},{19,11},{12,20... | collective-permute-start | bytes 2654216 | tf_op jit(solution)/shard_map/ppermute | solution.py:22
  248.7 31.8 %collective-permute-start.30 = (bf16[12,96,384]{2,1,0:T(8,128)(2,1)S(1)}, bf16[12,96,384]{2,1,0:T(8,128)(2,1)S(1)}, u32[]{:S(2)}, u32[]{:S(2)}) collective-permute-start(bf16[12,96,384]{2,1,0:T(8,128)(2,1)S(1)} %shard_map.184.refs_1_), channel_id=1, source_target_pairs={{8,0},{16,24},{9,1},{17,25},{10,2},{18,26},{11,3},{19,27},{12,4},{... | collective-permute-start | bytes 2654216 | tf_op jit(solution)/shard_map/ppermute | solution.py:22
  (29 other events, 156.6 us)

commit v4 on v3

--- a/solution.py
+++ b/solution.py
@@ -451,12 +451,12 @@
     (last_terms,) = add_after([(term(0), terms_middle[0])], copies)
     terms_in = to_end(last_terms)
     back = lax.all_to_all(copies, "shard", split_axis=0, concat_axis=0, tiled=True)
-    new_block = dense.join(back, rows_last[0], rows_across_2[1])
+    new_block = dense.join(back)
     block_near = permute(new_block, NEAR)
     block_across = across(new_block)
 
     mine = jnp.where(end, term(0), term(1))
-    sent = mean_after(groups, (mine, terms_out[2], terms_middle[1], terms_in), new_block)
+    sent = mean_after(groups, (mine, terms_out[2], terms_middle[1], terms_in), new_block, rows_last[0], rows_across_2[1])
     other = lax.ppermute(sent, "tp", SWAP)
 
     def both(one, two):
@@ -473,7 +473,7 @@
 
     next_embed = embed_owner[0, 0] - update(direction, lax.Precision.HIGHEST)
     half = lax.dynamic_slice_in_dim(direction, side * half_rank, half_rank, 0).astype(jnp.bfloat16)
-    half = after(half, block_near, block_across)
+    half = after(half, block_near)
 
     rank = lax.axis_index("rep")
     halves = jnp.stack([permute(half, [(i, (i + step) % groups) for i in range(groups)]) for step in (1, 2, 3)])

time: 283 us -> 279 us (0.986)
  waiting for transfers between devices: 138 us -> 147 us
  starting transfers between devices: 73.3 us -> 65.2 us
  local copies, waits for them, and re-layouts: 15.8 us -> 11.1 us
    all_to_all x1, waiting for transfers between devices: 0.01 us -> 9.94 us  [local(): lax.all_to_all(copies, 'shard', split_axis=0, concat_axis=0, tiled=True)]
    ppermute x29, starting transfers between devices: 62.5 us -> 54.6 us  [permute(): return lax.ppermute(value, 'rep', pairs)]
    unnamed x55 -> x43, local copies, waits for them, and re-layouts: 11.3 us -> 8.25 us
  transfers between devices with their start and end apart: 34 -> 34, of which waited for: 16 -> 18; matrix products, arithmetic and copies ran while one was open for 13% -> 12% of each run, Pallas kernels for 6% -> 7%
where the time goes in v4:
time: 279 us; the launch traced here: 278 us
  waiting for transfers between devices  147 us (53%)
  starting transfers between devices  65.2 us (23%)
  matrix products  26.1 us (9%)
  Pallas kernels  22.5 us (8%)
  local copies, waits for them, and re-layouts  11.1 us (4%)
  other arithmetic  4.29 us (2%)
    ppermute x29, waiting for transfers between devices, permute(): return lax.ppermute(value, 'rep', pairs)  133 us
    ppermute x29, starting transfers between devices, permute(): return lax.ppermute(value, 'rep', pairs)  54.6 us
    dot_general x7, matrix products, update(): lax.dot_general(toward, basis, (((0,), (1,)), ((), ())), precision=precis...  16.5 us
    all_to_all x1, waiting for transfers between devices, local(): lax.all_to_all(copies, 'shard', split_axis=0, concat_axis=0, tiled=True)  9.94 us
    dot_general x1, matrix products, local(): lax.dot_general(after(basis, far), wide(delta_embed[0]), (((0,), (1,)), (...  9.62 us
    unnamed x43, local copies, waits for them, and re-layouts  8.25 us
    pallas_call x5, Pallas kernels, add_after(): kernel_call(functools.partial(add_kernel, count), [jax.ShapeDtypeStruct(o...  6.73 us
  transfers between devices with their start and end apart: 34, of which 18 were waited for; matrix products, arithmetic and copies ran while one was open for 12% of the time, Pallas kernels for 7%

profile of v4, /device:TPU:0, one launch (start us, length us, event | category | flops | bytes accessed | tf_op | source)
XLA Modules:
  0.0 277.5 jit_solution(14826581950438275448)
XLA Ops:
  0.7 2.4 copy-done
  9.7 7.7 %collective-permute-start.2 = (bf16[12,96,384]{2,1,0:T(8,128)(2,1)S(1)}, bf16[12,96,384]{2,1,0:T(8,128)(2,1)}, u32[]{:S(2)}, u32[]{:S(2)}) collective-permute-start(bf16[12,96,384]{2,1,0:T(8,128)(2,1)S(1)} %get-tuple-element.41.refs_0_), channel_id=1, source_target_pairs={{0,8},{24,16},{1,9},{25,17},{2,10},{26,18},{3,11},{27,19},{4,12},{... | collective-permute-start | bytes 2654216 | tf_op jit(solution)/shard_map/ppermute | solution.py:22
  17.4 2.2 collective-permute-start.1
  21.1 9.6 %convolution_convert_fusion = bf16[64,12576]{1,0:T(8,128)(2,1)S(1)} fusion(f32[384,64]{1,0:T(8,128)S(1)} %shard_map.178, bf16[1,12576,384]{2,1,0:T(8,128)(2,1)} %param.16), kind=kOutput, calls=%fused_computation | convolution fusion | flops 1855211520 | bytes 11366400 | tf_op jit(solution)/shard_map/dot_general | solution.py:420
  30.7 5.9 %collective-permute-done.2.refs_1_ = bf16[12,96,384]{2,1,0:T(8,128)(2,1)} collective-permute-done((bf16[12,96,384]{2,1,0:T(8,128)(2,1)S(1)}, bf16[12,96,384]{2,1,0:T(8,128)(2,1)}, u32[]{:S(2)}, u32[]{:S(2)}) %collective-permute-start.2) | collective-permute-done | bytes 884768 | tf_op jit(solution)/shard_map/ppermute | solution.py:22
  36.6 3.1 %collective-permute-done.3.refs_2_ = bf16[1536,384]{1,0:T(8,128)(2,1)S(1)} collective-permute-done((bf16[1536,384]{1,0:T(8,128)(2,1)}, bf16[1536,384]{1,0:T(8,128)(2,1)S(1)}, u32[]{:S(2)}, u32[]{:S(2)}) %collective-permute-start.3) | collective-permute-done | bytes 1179680 | tf_op jit(solution)/shard_map/ppermute | solution.py:22
  39.7 2.7 shard_map.171
  45.7 5.7 %collective-permute-start = (bf16[12,96,384]{2,1,0:T(8,128)(2,1)}, bf16[12,96,384]{2,1,0:T(8,128)(2,1)}, u32[]{:S(2)}, u32[]{:S(2)}) collective-permute-start(bf16[12,96,384]{2,1,0:T(8,128)(2,1)} %get-tuple-element.38.near), channel_id=1, source_target_pairs={{0,8},{24,16},{1,9},{25,17},{2,10},{26,18},{3,11},{27,19},{4,12},{... | collective-permute-start | bytes 2654216 | tf_op jit(solution)/shard_map/ppermute | solution.py:22
  51.4 4.2 %collective-permute-done.1.refs_2_ = bf16[12,96,384]{2,1,0:T(8,128)(2,1)} collective-permute-done((bf16[12,96,384]{2,1,0:T(8,128)(2,1)}, bf16[12,96,384]{2,1,0:T(8,128)(2,1)}, u32[]{:S(2)}, u32[]{:S(2)}) %collective-permute-start.1) | collective-permute-done | bytes 884768 | tf_op jit(solution)/shard_map/ppermute | solution.py:22
  55.6 5.5 %collective-permute-start.11 = (bf16[1536,384]{1,0:T(8,128)(2,1)}, bf16[1536,384]{1,0:T(8,128)(2,1)}, u32[]{:S(2)}, u32[]{:S(2)}) collective-permute-start(bf16[1536,384]{1,0:T(8,128)(2,1)} %get-tuple-element.42), channel_id=1, source_target_pairs={{0,8},{24,16},{1,9},{25,17},{2,10},{26,18},{3,11},{27,19},{4,12},{... | collective-permute-start | bytes 3538952 | tf_op jit(solution)/shard_map/ppermute | solution.py:22
  61.1 4.0 %collective-permute-done.6.refs_4_ = bf16[1608,384]{1,0:T(8,128)(2,1)} collective-permute-done((bf16[1608,384]{1,0:T(8,128)(2,1)}, bf16[1608,384]{1,0:T(8,128)(2,1)}, u32[]{:S(2)}, u32[]{:S(2)}) %collective-permute-start.6) | collective-permute-done | bytes 1234976 | tf_op jit(solution)/shard_map/ppermute | solution.py:22
  76.0 22.4 %collective-permute-done.11.refs_2_ = bf16[1536,384]{1,0:T(8,128)(2,1)} collective-permute-done((bf16[1536,384]{1,0:T(8,128)(2,1)}, bf16[1536,384]{1,0:T(8,128)(2,1)}, u32[]{:S(2)}, u32[]{:S(2)}) %collective-permute-start.11) | collective-permute-done | bytes 1179680 | tf_op jit(solution)/shard_map/ppermute | solution.py:22
  98.4 4.4 %collective-permute-start.20 = (bf16[3,32,3144]{2,1,0:T(8,128)(2,1)S(1)}, bf16[3,32,3144]{2,1,0:T(8,128)(2,1)S(1)}, u32[]{:S(2)}, u32[]{:S(2)}) collective-permute-start(bf16[3,32,3144]{2,1,0:T(8,128)(2,1)S(1)} %pad_maximum_fusion), channel_id=1, source_target_pairs={{0,8},{24,16},{1,9},{25,17},{2,10},{26,18},{3,11},{27,19},{4,12},{... | collective-permute-start | bytes 1810952 | tf_op jit(solution)/shard_map/ppermute | solution.py:22
  104.9 12.7 %collective-permute-done.8.from_in = bf16[12,96,384]{2,1,0:T(8,128)(2,1)S(1)} collective-permute-done((bf16[12,96,384]{2,1,0:T(8,128)(2,1)S(1)}, bf16[12,96,384]{2,1,0:T(8,128)(2,1)S(1)}, u32[]{:S(2)}, u32[]{:S(2)}) %collective-permute-start.8) | collective-permute-done | bytes 884768 | tf_op jit(solution)/shard_map/ppermute | solution.py:22
  117.7 3.1 %shard_map.173.refs_1_.refs_4_ = bf16[4,96,1152]{2,1,0:T(8,128)(2,1)} custom-call(bf16[12,96,384]{2,1,0:T(8,128)(2,1)} %get-tuple-element.38.near, bf16[12,96,384]{2,1,0:T(8,128)(2,1)S(1)} %get-tuple-element.39.refs_1_.last, bf16[12,96,384]{2,1,0:T(8,128)(2,1)} %collective-permute-done.from_out, bf16[12,96,384]{2,1,0:T(8,128)(2,1)S(1)} %collective-permute-done.7.from_middle, ...), custom_call_target="tpu_custom_call" | custom-call | bytes 7962624 | tf_op jit(solution)/shard_map/pallas_call | solution.py:288
  120.7 2.5 collective-permute-start.14
  123.3 3.5 %all-to-all-start = ((bf16[4,96,1152]{2,1,0:T(8,128)(2,1)}), bf16[4,96,1152]{2,1,0:T(8,128)(2,1)S(1)}, u32[]{:S(2)}, u32[]{:S(2)}) async-start(bf16[4,96,1152]{2,1,0:T(8,128)(2,1)} %shard_map.173.refs_1_.refs_4_), calls=%async_computation | async-start | bytes 1769472 | tf_op jit(solution)/shard_map/all_to_all | solution.py:445
  127.7 17.5 %collective-permute-done.14.refs_2_ = bf16[1608,384]{1,0:T(8,128)(2,1)} collective-permute-done((bf16[1608,384]{1,0:T(8,128)(2,1)}, bf16[1608,384]{1,0:T(8,128)(2,1)}, u32[]{:S(2)}, u32[]{:S(2)}) %collective-permute-start.14) | collective-permute-done | bytes 1234976 | tf_op jit(solution)/shard_map/ppermute | solution.py:22
  150.0 3.5 %shard_map.176 = (f32[3456,128]{1,0:T(8,128)}, f32[3456,128]{1,0:T(8,128)}, bf16[4,96,1152]{2,1,0:T(8,128)(2,1)}) custom-call(bf16[4,96,1152]{2,1,0:T(8,128)(2,1)S(1)} %all-to-all-done.refs_1_.moved, f32[3456,128]{1,0:T(8,128)S(1)} %bitcast.67, f32[3456,128]{1,0:T(8,128)S(1)} %bitcast.68, bf16[1608,384]{1,0:T(8,128)(2,1)} %collective-permute-done.12.refs_0_, ...), custom_call_target="tpu_custom_call" | custom-call | bytes 8847360 | tf_op jit(solution)/shard_map/pallas_call | solution.py:350
  153.5 3.5 %all-to-all-start.1 = ((bf16[4,96,1152]{2,1,0:T(8,128)(2,1)}), bf16[4,96,1152]{2,1,0:T(8,128)(2,1)S(1)}, u32[]{:S(2)}, u32[]{:S(2)}) async-start(bf16[4,96,1152]{2,1,0:T(8,128)(2,1)} %get-tuple-element.46.refs_2_), calls=%async_computation.1 | async-start | bytes 1769472 | tf_op jit(solution)/shard_map/all_to_all | solution.py:453
  159.7 9.9 %all-to-all-done.1.pieces = bf16[4,96,1152]{2,1,0:T(8,128)(2,1)S(1)} async-done(((bf16[4,96,1152]{2,1,0:T(8,128)(2,1)}), bf16[4,96,1152]{2,1,0:T(8,128)(2,1)S(1)}, u32[]{:S(2)}, u32[]{:S(2)}) %all-to-all-start.1) | async-done | bytes 884768 | tf_op jit(solution)/shard_map/all_to_all | solution.py:453
  170.0 8.5 %collective-permute-done.22.refs_3_ = bf16[32,3144]{1,0:T(8,128)(2,1)} collective-permute-done((bf16[32,3144]{1,0:T(8,128)(2,1)}, bf16[32,3144]{1,0:T(8,128)(2,1)}, u32[]{:S(2)}, u32[]{:S(2)}) %collective-permute-start.22) | collective-permute-done | bytes 201248 | tf_op jit(solution)/shard_map/ppermute | solution.py:22
  182.7 4.4 %collective-permute-done.24 = bf16[32,3144]{1,0:T(8,128)(2,1)S(1)} collective-permute-done((bf16[32,3144]{1,0:T(8,128)(2,1)}, bf16[32,3144]{1,0:T(8,128)(2,1)S(1)}, u32[]{:S(2)}, u32[]{:S(2)}) %collective-permute-start.24) | collective-permute-done | bytes 201248 | tf_op jit(solution)/shard_map/ppermute | solution.py:460
  187.1 2.3 fusion.8
  189.5 12.9 %collective-permute-done.15.refs_0_.refs_1_ = bf16[12,96,384]{2,1,0:T(8,128)(2,1)S(1)} collective-permute-done((bf16[12,96,384]{2,1,0:T(8,128)(2,1)S(1)}, bf16[12,96,384]{2,1,0:T(8,128)(2,1)S(1)}, u32[]{:S(2)}, u32[]{:S(2)}) %collective-permute-start.15) | collective-permute-done | bytes 884768 | tf_op jit(solution)/shard_map/ppermute | solution.py:22
  202.5 2.2 collective-permute-start.26
  210.2 5.8 %collective-permute-done.26 = bf16[32,3144]{1,0:T(8,128)(2,1)} collective-permute-done((bf16[32,3144]{1,0:T(8,128)(2,1)S(1)}, bf16[32,3144]{1,0:T(8,128)(2,1)}, u32[]{:S(2)}, u32[]{:S(2)}) %collective-permute-start.26) | collective-permute-done | bytes 201248 | tf_op jit(solution)/shard_map/ppermute | solution.py:22
  219.5 8.0 %convert_dynamic-update-slice_fusion = (bf16[12576,384]{1,0:T(8,128)(2,1)S(1)}, f32[3144,384]{1,0:T(8,128)}) fusion(bf16[12576,384]{1,0:T(8,128)(2,1)S(1)} %broadcast_in_dim.9, s32[]{:T(128)S(6)} %select_n.176, f32[64,3144]{1,0:T(8,128)S(1)} %copy-done.16, f32[384,64]{0,1:T(8,128)S(1)} %copy-done.18, f32[1,1,3144,384]{3,2,1,0:T(8,128)S(1)} %bitcast.64), kind=kOutput, calls=%fused_computation.13 | convolution fusion | flops 930825216 | bytes 12990468 | tf_op jit(solution)/shard_map/dot_general | solution.py:470
  232.5 2.2 fusion.2
  235.5 7.2 %collective-permute-done.18.refs_1_ = bf16[1608,384]{1,0:T(8,128)(2,1)S(1)} collective-permute-done((bf16[1608,384]{1,0:T(8,128)(2,1)}, bf16[1608,384]{1,0:T(8,128)(2,1)S(1)}, u32[]{:S(2)}, u32[]{:S(2)}) %collective-permute-start.18) | collective-permute-done | bytes 1234976 | tf_op jit(solution)/shard_map/ppermute | solution.py:22
  248.1 13.6 %collective-permute-done.31.refs_0_ = bf16[12,96,384]{2,1,0:T(8,128)(2,1)S(1)} collective-permute-done((bf16[12,96,384]{2,1,0:T(8,128)(2,1)S(1)}, bf16[12,96,384]{2,1,0:T(8,128)(2,1)S(1)}, u32[]{:S(2)}, u32[]{:S(2)}) %collective-permute-start.31) | collective-permute-done | bytes 884768 | tf_op jit(solution)/shard_map/ppermute | solution.py:22
  263.4 13.1 %collective-permute-done.29.refs_0_ = bf16[12,96,384]{2,1,0:T(8,128)(2,1)S(1)} collective-permute-done((bf16[12,96,384]{2,1,0:T(8,128)(2,1)S(1)}, bf16[12,96,384]{2,1,0:T(8,128)(2,1)S(1)}, u32[]{:S(2)}, u32[]{:S(2)}) %collective-permute-start.29) | collective-permute-done | bytes 884768 | tf_op jit(solution)/shard_map/ppermute | solution.py:22
  (122 shorter events, 59.9 us)
Async XLA Ops:
  4.7 31.9 %collective-permute-start.4 = (bf16[1536,384]{1,0:T(8,128)(2,1)}, bf16[1536,384]{1,0:T(8,128)(2,1)}, u32[]{:S(2)}, u32[]{:S(2)}) collective-permute-start(bf16[1536,384]{1,0:T(8,128)(2,1)} %get-tuple-element.42), channel_id=1, source_target_pairs={{8,16},{16,8},{9,17},{17,9},{10,18},{18,10},{11,19},{19,11},{12,20... | collective-permute-start | bytes 3538952 | tf_op jit(solution)/shard_map/ppermute | solution.py:22
  6.6 33.1 %collective-permute-start.3 = (bf16[1536,384]{1,0:T(8,128)(2,1)}, bf16[1536,384]{1,0:T(8,128)(2,1)S(1)}, u32[]{:S(2)}, u32[]{:S(2)}) collective-permute-start(bf16[1536,384]{1,0:T(8,128)(2,1)} %get-tuple-element.42), channel_id=1, source_target_pairs={{8,0},{16,24},{9,1},{17,25},{10,2},{18,26},{11,3},{19,27},{12,4},{... | collective-permute-start | bytes 3538952 | tf_op jit(solution)/shard_map/ppermute | solution.py:22
  9.7 26.8 %collective-permute-start.2 = (bf16[12,96,384]{2,1,0:T(8,128)(2,1)S(1)}, bf16[12,96,384]{2,1,0:T(8,128)(2,1)}, u32[]{:S(2)}, u32[]{:S(2)}) collective-permute-start(bf16[12,96,384]{2,1,0:T(8,128)(2,1)S(1)} %get-tuple-element.41.refs_0_), channel_id=1, source_target_pairs={{0,8},{24,16},{1,9},{25,17},{2,10},{26,18},{3,11},{27,19},{4,12},{... | collective-permute-start | bytes 2654216 | tf_op jit(solution)/shard_map/ppermute | solution.py:22
  17.4 38.2 %collective-permute-start.1 = (bf16[12,96,384]{2,1,0:T(8,128)(2,1)}, bf16[12,96,384]{2,1,0:T(8,128)(2,1)}, u32[]{:S(2)}, u32[]{:S(2)}) collective-permute-start(bf16[12,96,384]{2,1,0:T(8,128)(2,1)} %get-tuple-element.40.refs_0_), channel_id=1, source_target_pairs={{0,8},{24,16},{1,9},{25,17},{2,10},{26,18},{3,11},{27,19},{4,12},{... | collective-permute-start | bytes 2654216 | tf_op jit(solution)/shard_map/ppermute | solution.py:22
  19.6 45.5 %collective-permute-start.6 = (bf16[1608,384]{1,0:T(8,128)(2,1)}, bf16[1608,384]{1,0:T(8,128)(2,1)}, u32[]{:S(2)}, u32[]{:S(2)}) collective-permute-start(bf16[1608,384]{1,0:T(8,128)(2,1)} %get-tuple-element.43.refs_0_), channel_id=1, source_target_pairs={{8,0},{16,24},{9,1},{17,25},{10,2},{18,26},{11,3},{19,27},{12,4},{... | collective-permute-start | bytes 3704840 | tf_op jit(solution)/shard_map/ppermute | solution.py:22
  42.4 24.4 %collective-permute-start.5 = (bf16[12,96,384]{2,1,0:T(8,128)(2,1)}, bf16[12,96,384]{2,1,0:T(8,128)(2,1)S(1)}, u32[]{:S(2)}, u32[]{:S(2)}) collective-permute-start(bf16[12,96,384]{2,1,0:T(8,128)(2,1)} %shard_map.171), channel_id=1, source_target_pairs={{8,16},{16,8},{9,17},{17,9},{10,18},{18,10},{11,19},{19,11},{12,20... | collective-permute-start | bytes 2654216 | tf_op jit(solution)/shard_map/ppermute | solution.py:22
  44.2 27.8 %collective-permute-start.19 = (bf16[32,12576]{1,0:T(8,128)(2,1)}, bf16[32,12576]{1,0:T(8,128)(2,1)}, u32[]{:S(2)}, u32[]{:S(2)}) collective-permute-start(bf16[32,12576]{1,0:T(8,128)(2,1)} %get-tuple-element.69), channel_id=1, source_target_pairs={{0,1},{1,0},{2,3},{3,2},{4,5},{5,4},{6,7},{7,6},{8,9},{9,8},{10,11... | collective-permute-start | bytes 2414600 | tf_op jit(solution)/shard_map/ppermute | solution.py:429
  45.7 28.9 %collective-permute-start = (bf16[12,96,384]{2,1,0:T(8,128)(2,1)}, bf16[12,96,384]{2,1,0:T(8,128)(2,1)}, u32[]{:S(2)}, u32[]{:S(2)}) collective-permute-start(bf16[12,96,384]{2,1,0:T(8,128)(2,1)} %get-tuple-element.38.near), channel_id=1, source_target_pairs={{0,8},{24,16},{1,9},{25,17},{2,10},{26,18},{3,11},{27,19},{4,12},{... | collective-permute-start | bytes 2654216 | tf_op jit(solution)/shard_map/ppermute | solution.py:22
  55.6 42.8 %collective-permute-start.11 = (bf16[1536,384]{1,0:T(8,128)(2,1)}, bf16[1536,384]{1,0:T(8,128)(2,1)}, u32[]{:S(2)}, u32[]{:S(2)}) collective-permute-start(bf16[1536,384]{1,0:T(8,128)(2,1)} %get-tuple-element.42), channel_id=1, source_target_pairs={{0,8},{24,16},{1,9},{25,17},{2,10},{26,18},{3,11},{27,19},{4,12},{... | collective-permute-start | bytes 3538952 | tf_op jit(solution)/shard_map/ppermute | solution.py:22
  65.1 37.7 %collective-permute-start.10 = (bf16[1608,384]{1,0:T(8,128)(2,1)}, bf16[1608,384]{1,0:T(8,128)(2,1)}, u32[]{:S(2)}, u32[]{:S(2)}) collective-permute-start(bf16[1608,384]{1,0:T(8,128)(2,1)} %get-tuple-element.43.refs_0_), channel_id=1, source_target_pairs={{8,16},{16,8},{9,17},{17,9},{10,18},{18,10},{11,19},{19,11},{12,20... | collective-permute-start | bytes 3704840 | tf_op jit(solution)/shard_map/ppermute | solution.py:22
  67.7 35.9 %collective-permute-start.9 = (bf16[1536,384]{1,0:T(8,128)(2,1)}, bf16[1536,384]{1,0:T(8,128)(2,1)S(1)}, u32[]{:S(2)}, u32[]{:S(2)}) collective-permute-start(bf16[1536,384]{1,0:T(8,128)(2,1)} %collective-permute-done.4.refs_3_), channel_id=1, source_target_pairs={{8,0},{16,24},{9,1},{17,25},{10,2},{18,26},{11,3},{19,27},{12,4},{... | collective-permute-start | bytes 3538952 | tf_op jit(solution)/shard_map/ppermute | solution.py:22
  72.0 32.9 %collective-permute-start.7 = (bf16[12,96,384]{2,1,0:T(8,128)(2,1)S(1)}, bf16[12,96,384]{2,1,0:T(8,128)(2,1)S(1)}, u32[]{:S(2)}, u32[]{:S(2)}) collective-permute-start(bf16[12,96,384]{2,1,0:T(8,128)(2,1)S(1)} %get-tuple-element.44.refs_2_), channel_id=1, source_target_pairs={{8,16},{16,8},{9,17},{17,9},{10,18},{18,10},{11,19},{19,11},{12,20... | collective-permute-start | bytes 2654216 | tf_op jit(solution)/shard_map/ppermute | solution.py:22
  74.6 43.1 %collective-permute-start.8 = (bf16[12,96,384]{2,1,0:T(8,128)(2,1)S(1)}, bf16[12,96,384]{2,1,0:T(8,128)(2,1)S(1)}, u32[]{:S(2)}, u32[]{:S(2)}) collective-permute-start(bf16[12,96,384]{2,1,0:T(8,128)(2,1)S(1)} %get-tuple-element.45), channel_id=1, source_target_pairs={{8,0},{16,24},{9,1},{17,25},{10,2},{18,26},{11,3},{19,27},{12,4},{... | collective-permute-start | bytes 2654216 | tf_op jit(solution)/shard_map/ppermute | solution.py:22
  98.4 24.8 %collective-permute-start.20 = (bf16[3,32,3144]{2,1,0:T(8,128)(2,1)S(1)}, bf16[3,32,3144]{2,1,0:T(8,128)(2,1)S(1)}, u32[]{:S(2)}, u32[]{:S(2)}) collective-permute-start(bf16[3,32,3144]{2,1,0:T(8,128)(2,1)S(1)} %pad_maximum_fusion), channel_id=1, source_target_pairs={{0,8},{24,16},{1,9},{25,17},{2,10},{26,18},{3,11},{27,19},{4,12},{... | collective-permute-start | bytes 1810952 | tf_op jit(solution)/shard_map/ppermute | solution.py:22
  102.8 44.0 %collective-permute-start.13 = (bf16[1536,384]{1,0:T(8,128)(2,1)}, bf16[1536,384]{1,0:T(8,128)(2,1)S(1)}, u32[]{:S(2)}, u32[]{:S(2)}) collective-permute-start(bf16[1536,384]{1,0:T(8,128)(2,1)} %collective-permute-done.11.refs_2_), channel_id=1, source_target_pairs={{8,16},{16,8},{9,17},{17,9},{10,18},{18,10},{11,19},{19,11},{12,20... | collective-permute-start | bytes 3538952 | tf_op jit(solution)/shard_map/ppermute | solution.py:22
  103.6 44.9 %collective-permute-start.12 = (bf16[1608,384]{1,0:T(8,128)(2,1)}, bf16[1608,384]{1,0:T(8,128)(2,1)}, u32[]{:S(2)}, u32[]{:S(2)}) collective-permute-start(bf16[1608,384]{1,0:T(8,128)(2,1)} %collective-permute-done.10.refs_1_), channel_id=1, source_target_pairs={{8,0},{16,24},{9,1},{17,25},{10,2},{18,26},{11,3},{19,27},{12,4},{... | collective-permute-start | bytes 3704840 | tf_op jit(solution)/shard_map/ppermute | solution.py:22
  120.7 24.4 %collective-permute-start.14 = (bf16[1608,384]{1,0:T(8,128)(2,1)}, bf16[1608,384]{1,0:T(8,128)(2,1)}, u32[]{:S(2)}, u32[]{:S(2)}) collective-permute-start(bf16[1608,384]{1,0:T(8,128)(2,1)} %shard_map.175), channel_id=1, source_target_pairs={{0,8},{24,16},{1,9},{25,17},{2,10},{26,18},{3,11},{27,19},{4,12},{... | collective-permute-start | bytes 3704840 | tf_op jit(solution)/shard_map/ppermute | solution.py:22
  123.3 23.6 %all-to-all-start = ((bf16[4,96,1152]{2,1,0:T(8,128)(2,1)}), bf16[4,96,1152]{2,1,0:T(8,128)(2,1)S(1)}, u32[]{:S(2)}, u32[]{:S(2)}) async-start(bf16[4,96,1152]{2,1,0:T(8,128)(2,1)} %shard_map.173.refs_1_.refs_4_), calls=%async_computation | async-start | bytes 1769472 | tf_op jit(solution)/shard_map/all_to_all | solution.py:445
  127.0 30.1 %collective-permute-start.21 = (bf16[2,32,3144]{2,1,0:T(8,128)(2,1)S(1)}, bf16[2,32,3144]{2,1,0:T(8,128)(2,1)S(1)}, u32[]{:S(2)}, u32[]{:S(2)}) collective-permute-start(bf16[2,32,3144]{2,1,0:T(8,128)(2,1)S(1)} %pad_maximum_fusion.2), channel_id=1, source_target_pairs={{8,16},{16,8},{9,17},{17,9},{10,18},{18,10},{11,19},{19,11},{12,20... | collective-permute-start | bytes 1207304 | tf_op jit(solution)/shard_map/ppermute | solution.py:22
  145.1 33.4 %collective-permute-start.17 = (bf16[1608,384]{1,0:T(8,128)(2,1)}, bf16[1608,384]{1,0:T(8,128)(2,1)}, u32[]{:S(2)}, u32[]{:S(2)}) collective-permute-start(bf16[1608,384]{1,0:T(8,128)(2,1)} %collective-permute-done.14.refs_2_), channel_id=1, source_target_pairs={{8,16},{16,8},{9,17},{17,9},{10,18},{18,10},{11,19},{19,11},{12,20... | collective-permute-start | bytes 3704840 | tf_op jit(solution)/shard_map/ppermute | solution.py:22
  146.9 31.6 %collective-permute-start.23 = (bf16[1536,384]{1,0:T(8,128)(2,1)S(1)}, bf16[1536,384]{1,0:T(8,128)(2,1)}, u32[]{:S(2)}, u32[]{:S(2)}) collective-permute-start(bf16[1536,384]{1,0:T(8,128)(2,1)S(1)} %shard_map.174.refs_1_), channel_id=1, source_target_pairs={{8,0},{16,24},{9,1},{17,25},{10,2},{18,26},{11,3},{19,27},{12,4},{... | collective-permute-start | bytes 3538952 | tf_op jit(solution)/shard_map/ppermute | solution.py:22
  153.5 16.2 %all-to-all-start.1 = ((bf16[4,96,1152]{2,1,0:T(8,128)(2,1)}), bf16[4,96,1152]{2,1,0:T(8,128)(2,1)S(1)}, u32[]{:S(2)}, u32[]{:S(2)}) async-start(bf16[4,96,1152]{2,1,0:T(8,128)(2,1)} %get-tuple-element.46.refs_2_), calls=%async_computation.1 | async-start | bytes 1769472 | tf_op jit(solution)/shard_map/all_to_all | solution.py:453
  158.5 20.0 %collective-permute-start.22 = (bf16[32,3144]{1,0:T(8,128)(2,1)}, bf16[32,3144]{1,0:T(8,128)(2,1)}, u32[]{:S(2)}, u32[]{:S(2)}) collective-permute-start(bf16[32,3144]{1,0:T(8,128)(2,1)} %shard_map.181), channel_id=1, source_target_pairs={{8,0},{16,24},{9,1},{17,25},{10,2},{18,26},{11,3},{19,27},{12,4},{... | collective-permute-start | bytes 603656 | tf_op jit(solution)/shard_map/ppermute | solution.py:22
  182.7 19.7 %collective-permute-start.15 = (bf16[12,96,384]{2,1,0:T(8,128)(2,1)S(1)}, bf16[12,96,384]{2,1,0:T(8,128)(2,1)S(1)}, u32[]{:S(2)}, u32[]{:S(2)}) collective-permute-start(bf16[12,96,384]{2,1,0:T(8,128)(2,1)S(1)} %shard_map.177.refs_4_.refs_0_.refs_1_), channel_id=1, source_target_pairs={{0,8},{24,16},{8,0},{16,24},{1,9},{25,17},{9,1},{17,25},{2,10},{26... | collective-permute-start | bytes 2654216 | tf_op jit(solution)/shard_map/ppermute | solution.py:22
  202.5 13.5 %collective-permute-start.26 = (bf16[32,3144]{1,0:T(8,128)(2,1)S(1)}, bf16[32,3144]{1,0:T(8,128)(2,1)}, u32[]{:S(2)}, u32[]{:S(2)}) collective-permute-start(bf16[32,3144]{1,0:T(8,128)(2,1)S(1)} %shard_map.183), channel_id=1, source_target_pairs={{0,16},{8,24},{16,0},{24,8},{1,17},{9,25},{17,1},{25,9},{2,18},{10... | collective-permute-start | bytes 603656 | tf_op jit(solution)/shard_map/ppermute | solution.py:22
  204.7 11.8 %collective-permute-start.27 = (bf16[32,3144]{1,0:T(8,128)(2,1)S(1)}, bf16[32,3144]{1,0:T(8,128)(2,1)}, u32[]{:S(2)}, u32[]{:S(2)}) collective-permute-start(bf16[32,3144]{1,0:T(8,128)(2,1)S(1)} %shard_map.183), channel_id=1, source_target_pairs={{0,24},{8,0},{16,8},{24,16},{1,25},{9,1},{17,9},{25,17},{2,26},{10... | collective-permute-start | bytes 603656 | tf_op jit(solution)/shard_map/ppermute | solution.py:22
  207.2 21.0 %collective-permute-start.30 = (bf16[12,96,384]{2,1,0:T(8,128)(2,1)S(1)}, bf16[12,96,384]{2,1,0:T(8,128)(2,1)S(1)}, u32[]{:S(2)}, u32[]{:S(2)}) collective-permute-start(bf16[12,96,384]{2,1,0:T(8,128)(2,1)S(1)} %shard_map.177.refs_4_.refs_0_.refs_1_), channel_id=1, source_target_pairs={{8,16},{16,8},{9,17},{17,9},{10,18},{18,10},{11,19},{19,11},{12,20... | collective-permute-start | bytes 2654216 | tf_op jit(solution)/shard_map/ppermute | solution.py:22
  208.0 34.7 %collective-permute-start.18 = (bf16[1608,384]{1,0:T(8,128)(2,1)}, bf16[1608,384]{1,0:T(8,128)(2,1)S(1)}, u32[]{:S(2)}, u32[]{:S(2)}) collective-permute-start(bf16[1608,384]{1,0:T(8,128)(2,1)} %collective-permute-done.17.refs_6_), channel_id=1, source_target_pairs={{8,0},{16,24},{9,1},{17,25},{10,2},{18,26},{11,3},{19,27},{12,4},{... | collective-permute-start | bytes 3704840 | tf_op jit(solution)/shard_map/ppermute | solution.py:22
  217.8 12.7 %collective-permute-start.28 = (bf16[3,32,3144]{2,1,0:T(8,128)(2,1)S(1)}, bf16[3,32,3144]{2,1,0:T(8,128)(2,1)S(1)}, u32[]{:S(2)}, u32[]{:S(2)}) collective-permute-start(bf16[3,32,3144]{2,1,0:T(8,128)(2,1)S(1)} %pad_maximum_fusion.1), channel_id=1, source_target_pairs={{0,1},{1,0},{2,3},{3,2},{4,5},{5,4},{6,7},{7,6},{8,9},{9,8},{10,11... | collective-permute-start | bytes 1810952 | tf_op jit(solution)/shard_map/ppermute | solution.py:480
  227.5 8.0 %collective-permute-start.16 = (bf16[12,96,384]{2,1,0:T(8,128)(2,1)S(1)}, bf16[12,96,384]{2,1,0:T(8,128)(2,1)S(1)}, u32[]{:S(2)}, u32[]{:S(2)}) collective-permute-start(bf16[12,96,384]{2,1,0:T(8,128)(2,1)S(1)} %collective-permute-done.15.refs_0_.refs_1_), channel_id=1, source_target_pairs={{8,16},{16,8},{9,17},{17,9},{10,18},{18,10},{11,19},{19,11},{12,20... | collective-permute-start | bytes 2654216 | tf_op jit(solution)/shard_map/ppermute | solution.py:22
  228.2 33.4 %collective-permute-start.31 = (bf16[12,96,384]{2,1,0:T(8,128)(2,1)S(1)}, bf16[12,96,384]{2,1,0:T(8,128)(2,1)S(1)}, u32[]{:S(2)}, u32[]{:S(2)}) collective-permute-start(bf16[12,96,384]{2,1,0:T(8,128)(2,1)S(1)} %collective-permute-done.30.refs_1_), channel_id=1, source_target_pairs={{8,0},{16,24},{9,1},{17,25},{10,2},{18,26},{11,3},{19,27},{12,4},{... | collective-permute-start | bytes 2654216 | tf_op jit(solution)/shard_map/ppermute | solution.py:22
  242.7 33.8 %collective-permute-start.29 = (bf16[12,96,384]{2,1,0:T(8,128)(2,1)S(1)}, bf16[12,96,384]{2,1,0:T(8,128)(2,1)S(1)}, u32[]{:S(2)}, u32[]{:S(2)}) collective-permute-start(bf16[12,96,384]{2,1,0:T(8,128)(2,1)S(1)} %shard_map.184.refs_1_), channel_id=1, source_target_pairs={{8,0},{16,24},{9,1},{17,25},{10,2},{18,26},{11,3},{19,27},{12,4},{... | collective-permute-start | bytes 2654216 | tf_op jit(solution)/shard_map/ppermute | solution.py:22
  (23 other events, 116.1 us)

commit v5 on v4

--- a/solution.py
+++ b/solution.py
@@ -156,11 +156,11 @@
             back[s, here, column : column + piece] = fresh[:, s * piece : (s + 1) * piece].astype(back.dtype)
 
 
-def kernel_call(body, out_shape, moved_bytes, **more):
+def kernel_call(body, out_shape, moved_bytes, vmem=40, **more):
     return pl.pallas_call(
         body,
         out_shape=out_shape,
-        compiler_params=pltpu.CompilerParams(vmem_limit_bytes=40 << 20),
+        compiler_params=pltpu.CompilerParams(vmem_limit_bytes=vmem << 20),
         cost_estimate=pl.CostEstimate(flops=0, bytes_accessed=moved_bytes, transcendentals=0),
         **more,
     )
@@ -226,19 +226,24 @@
     )(*terms, *others)
 
 
-def narrow_kernel(cut, wide_rows, low, high):
-    low[...] = wide_rows[:cut, :].astype(low.dtype)
-    high[...] = wide_rows[cut:, :].astype(high.dtype)
-
-
-def narrow_rows(array, cut):
+def narrow_kernel(first, wide_rows, part, held, sem):
+    copy = pltpu.make_async_copy(wide_rows.at[pl.ds(first, part.shape[0]), :], held, sem)
+    copy.start()
+    copy.wait()
+    part[...] = held[...].astype(part.dtype)
+
+
+def narrow_rows(array, first, count):
     rows, columns = array.shape[2:]
-    if cut % 16 or rows % 8:
-        return [part.astype(jnp.bfloat16) for part in (array[0, 0, :cut], array[0, 0, cut:])]
+    if first % 8 or count % 8:
+        return array[0, 0, first : first + count].astype(jnp.bfloat16)
     return kernel_call(
-        functools.partial(narrow_kernel, cut),
-        [jax.ShapeDtypeStruct((count, columns), jnp.bfloat16) for count in (cut, rows - cut)],
-        6 * rows * columns,
+        functools.partial(narrow_kernel, first),
+        jax.ShapeDtypeStruct((count, columns), jnp.bfloat16),
+        6 * count * columns,
+        vmem=60,
+        in_specs=[ANYWHERE],
+        scratch_shapes=[pltpu.VMEM((count, columns), array.dtype), pltpu.SemaphoreType.DMA],
     )(array.reshape(rows, columns))
 
 
@@ -405,7 +410,7 @@
     rows = embed_owner.shape[2]
     half_rank = basis.shape[1] // 2
     cut = rows // 2 // LANES * LANES
-    low, high = narrow_rows(embed_owner, cut)
+    low, high = narrow_rows(embed_owner, 0, cut), narrow_rows(embed_owner, cut, rows - cut)
     rows_near = [to_end(low), to_end(high)]
     rows_across = [across(low), across(high)]
     rows_far = [to_end(part) for part in rows_across]

time: 279 us -> 278 us (level)
  waiting for transfers between devices: 147 us -> 135 us
  starting transfers between devices: 65.2 us -> 69.1 us
    ppermute x29, waiting for transfers between devices: 133 us -> 122 us  [permute(): return lax.ppermute(value, 'rep', pairs)]
    pallas_call x1 -> x2, Pallas kernels: 1.68 us -> 5.79 us  [narrow_rows(): kernel_call(functools.partial(narrow_kernel, first), jax.ShapeDtypeStruct...]
    ppermute x29, starting transfers between devices: 54.6 us -> 58.4 us  [permute(): return lax.ppermute(value, 'rep', pairs)]
    unnamed x43 -> x49, local copies, waits for them, and re-layouts: 8.25 us -> 8.06 us
  transfers between devices with their start and end apart: 34 -> 34, of which waited for: 18 -> 17; matrix products, arithmetic and copies ran while one was open for 12% -> 14% of each run, Pallas kernels for 7% -> 7%
where the time goes in v5:
time: 278 us; the launch traced here: 277 us
  waiting for transfers between devices  135 us (49%)
  starting transfers between devices  69.1 us (25%)
  matrix products  27.3 us (10%)
  Pallas kernels  25.2 us (9%)
  local copies, waits for them, and re-layouts  12.7 us (5%)
  other arithmetic  5.78 us (2%)
    ppermute x29, waiting for transfers between devices, permute(): return lax.ppermute(value, 'rep', pairs)  122 us
    ppermute x29, starting transfers between devices, permute(): return lax.ppermute(value, 'rep', pairs)  58.4 us
    dot_general x7, matrix products, update(): lax.dot_general(toward, basis, (((0,), (1,)), ((), ())), precision=precis...  17.7 us
    dot_general x1, matrix products, local(): lax.dot_general(after(basis, far), wide(delta_embed[0]), (((0,), (1,)), (...  9.62 us
    all_to_all x1, waiting for transfers between devices, local(): lax.all_to_all(copies, 'shard', split_axis=0, concat_axis=0, tiled=True)  8.83 us
    unnamed x49, local copies, waits for them, and re-layouts  8.06 us
    pallas_call x2, Pallas kernels, narrow_rows(): kernel_call(functools.partial(narrow_kernel, first), jax.ShapeDtypeStruct...  5.79 us
  transfers between devices with their start and end apart: 34, of which 17 were waited for; matrix products, arithmetic and copies ran while one was open for 14% of the time, Pallas kernels for 7%

profile of v5, /device:TPU:0, one launch (start us, length us, event | category | flops | bytes accessed | tf_op | source)
XLA Modules:
  0.0 276.5 jit_solution(6912835741437411175)
XLA Ops:
  0.7 2.9 %shard_map.170 = bf16[1536,384]{1,0:T(8,128)(2,1)} custom-call(f32[3144,384]{1,0:T(8,128)} %bitcast.68), custom_call_target="tpu_custom_call" | custom-call | bytes 3538944 | tf_op jit(solution)/shard_map/pallas_call | solution.py:240
  10.9 7.8 %collective-permute-start.2 = (bf16[12,96,384]{2,1,0:T(8,128)(2,1)S(1)}, bf16[12,96,384]{2,1,0:T(8,128)(2,1)S(1)}, u32[]{:S(2)}, u32[]{:S(2)}) collective-permute-start(bf16[12,96,384]{2,1,0:T(8,128)(2,1)S(1)} %get-tuple-element.39.refs_0_), channel_id=1, source_target_pairs={{0,8},{24,16},{1,9},{25,17},{2,10},{26,18},{3,11},{27,19},{4,12},{... | collective-permute-start | bytes 2654216 | tf_op jit(solution)/shard_map/ppermute | solution.py:22
  18.8 2.3 collective-permute-start.1
  21.1 2.9 %shard_map.172.refs_0_ = bf16[1608,384]{1,0:T(8,128)(2,1)} custom-call(f32[3144,384]{1,0:T(8,128)} %bitcast.69), custom_call_target="tpu_custom_call" | custom-call | bytes 3704832 | tf_op jit(solution)/shard_map/pallas_call | solution.py:240
  25.4 9.6 %convolution_convert_fusion = bf16[64,12576]{1,0:T(8,128)(2,1)S(1)} fusion(f32[384,64]{1,0:T(8,128)S(1)} %shard_map.179, bf16[1,12576,384]{2,1,0:T(8,128)(2,1)} %param.16), kind=kOutput, calls=%fused_computation | convolution fusion | flops 1855211520 | bytes 11366400 | tf_op jit(solution)/shard_map/dot_general | solution.py:425
  35.1 3.7 %collective-permute-done.2.refs_1_ = bf16[12,96,384]{2,1,0:T(8,128)(2,1)S(1)} collective-permute-done((bf16[12,96,384]{2,1,0:T(8,128)(2,1)S(1)}, bf16[12,96,384]{2,1,0:T(8,128)(2,1)S(1)}, u32[]{:S(2)}, u32[]{:S(2)}) %collective-permute-start.2) | collective-permute-done | bytes 884768 | tf_op jit(solution)/shard_map/ppermute | solution.py:22
  44.2 7.7 %collective-permute-start = (bf16[12,96,384]{2,1,0:T(8,128)(2,1)}, bf16[12,96,384]{2,1,0:T(8,128)(2,1)}, u32[]{:S(2)}, u32[]{:S(2)}) collective-permute-start(bf16[12,96,384]{2,1,0:T(8,128)(2,1)} %get-tuple-element.36.near), channel_id=1, source_target_pairs={{0,8},{24,16},{1,9},{25,17},{2,10},{26,18},{3,11},{27,19},{4,12},{... | collective-permute-start | bytes 2654216 | tf_op jit(solution)/shard_map/ppermute | solution.py:22
  51.9 6.0 %collective-permute-done.1.refs_2_ = bf16[12,96,384]{2,1,0:T(8,128)(2,1)} collective-permute-done((bf16[12,96,384]{2,1,0:T(8,128)(2,1)}, bf16[12,96,384]{2,1,0:T(8,128)(2,1)}, u32[]{:S(2)}, u32[]{:S(2)}) %collective-permute-start.1) | collective-permute-done | bytes 884768 | tf_op jit(solution)/shard_map/ppermute | solution.py:22
  57.8 5.4 %collective-permute-start.11 = (bf16[1536,384]{1,0:T(8,128)(2,1)}, bf16[1536,384]{1,0:T(8,128)(2,1)}, u32[]{:S(2)}, u32[]{:S(2)}) collective-permute-start(bf16[1536,384]{1,0:T(8,128)(2,1)} %shard_map.170), channel_id=1, source_target_pairs={{0,8},{24,16},{1,9},{25,17},{2,10},{26,18},{3,11},{27,19},{4,12},{... | collective-permute-start | bytes 3538952 | tf_op jit(solution)/shard_map/ppermute | solution.py:22
  66.9 2.1 shard_map.173
  72.2 4.6 %collective-permute-done.from_out = bf16[12,96,384]{2,1,0:T(8,128)(2,1)} collective-permute-done((bf16[12,96,384]{2,1,0:T(8,128)(2,1)}, bf16[12,96,384]{2,1,0:T(8,128)(2,1)}, u32[]{:S(2)}, u32[]{:S(2)}) %collective-permute-start) | collective-permute-done | bytes 884768 | tf_op jit(solution)/shard_map/ppermute | solution.py:22
  78.2 22.4 %collective-permute-done.11.refs_2_ = bf16[1536,384]{1,0:T(8,128)(2,1)} collective-permute-done((bf16[1536,384]{1,0:T(8,128)(2,1)}, bf16[1536,384]{1,0:T(8,128)(2,1)}, u32[]{:S(2)}, u32[]{:S(2)}) %collective-permute-start.11) | collective-permute-done | bytes 1179680 | tf_op jit(solution)/shard_map/ppermute | solution.py:22
  100.6 4.4 %collective-permute-start.20 = (bf16[3,32,3144]{2,1,0:T(8,128)(2,1)S(1)}, bf16[3,32,3144]{2,1,0:T(8,128)(2,1)S(1)}, u32[]{:S(2)}, u32[]{:S(2)}) collective-permute-start(bf16[3,32,3144]{2,1,0:T(8,128)(2,1)S(1)} %pad_maximum_fusion), channel_id=1, source_target_pairs={{0,8},{24,16},{1,9},{25,17},{2,10},{26,18},{3,11},{27,19},{4,12},{... | collective-permute-start | bytes 1810952 | tf_op jit(solution)/shard_map/ppermute | solution.py:22
  107.1 8.4 %collective-permute-done.8.from_in = bf16[12,96,384]{2,1,0:T(8,128)(2,1)S(1)} collective-permute-done((bf16[12,96,384]{2,1,0:T(8,128)(2,1)S(1)}, bf16[12,96,384]{2,1,0:T(8,128)(2,1)S(1)}, u32[]{:S(2)}, u32[]{:S(2)}) %collective-permute-start.8) | collective-permute-done | bytes 884768 | tf_op jit(solution)/shard_map/ppermute | solution.py:22
  115.5 3.1 %shard_map.174.refs_1_.refs_4_ = bf16[4,96,1152]{2,1,0:T(8,128)(2,1)} custom-call(bf16[12,96,384]{2,1,0:T(8,128)(2,1)} %get-tuple-element.36.near, bf16[12,96,384]{2,1,0:T(8,128)(2,1)S(1)} %get-tuple-element.37.refs_1_.last, bf16[12,96,384]{2,1,0:T(8,128)(2,1)} %collective-permute-done.from_out, bf16[12,96,384]{2,1,0:T(8,128)(2,1)S(1)} %collective-permute-done.7.from_middle, ...), custom_call_target="tpu_custom_call" | custom-call | bytes 7962624 | tf_op jit(solution)/shard_map/pallas_call | solution.py:293
  118.6 2.5 collective-permute-start.14
  121.9 3.5 %all-to-all-start = ((bf16[4,96,1152]{2,1,0:T(8,128)(2,1)}), bf16[4,96,1152]{2,1,0:T(8,128)(2,1)S(1)}, u32[]{:S(2)}, u32[]{:S(2)}) async-start(bf16[4,96,1152]{2,1,0:T(8,128)(2,1)} %shard_map.174.refs_1_.refs_4_), calls=%async_computation | async-start | bytes 1769472 | tf_op jit(solution)/shard_map/all_to_all | solution.py:450
  130.5 12.8 %collective-permute-done.14.refs_2_ = bf16[1608,384]{1,0:T(8,128)(2,1)} collective-permute-done((bf16[1608,384]{1,0:T(8,128)(2,1)S(1)}, bf16[1608,384]{1,0:T(8,128)(2,1)}, u32[]{:S(2)}, u32[]{:S(2)}) %collective-permute-start.14) | collective-permute-done | bytes 1234976 | tf_op jit(solution)/shard_map/ppermute | solution.py:22
  148.2 3.5 %shard_map.177 = (f32[3456,128]{1,0:T(8,128)}, f32[3456,128]{1,0:T(8,128)}, bf16[4,96,1152]{2,1,0:T(8,128)(2,1)}) custom-call(bf16[4,96,1152]{2,1,0:T(8,128)(2,1)S(1)} %all-to-all-done.refs_1_.moved, f32[3456,128]{1,0:T(8,128)S(1)} %bitcast.64, f32[3456,128]{1,0:T(8,128)S(1)} %bitcast.65, bf16[1608,384]{1,0:T(8,128)(2,1)} %collective-permute-done.12.refs_0_, ...), custom_call_target="tpu_custom_call" | custom-call | bytes 8847360 | tf_op jit(solution)/shard_map/pallas_call | solution.py:355
  151.7 3.6 %all-to-all-start.1 = ((bf16[4,96,1152]{2,1,0:T(8,128)(2,1)}), bf16[4,96,1152]{2,1,0:T(8,128)(2,1)S(1)}, u32[]{:S(2)}, u32[]{:S(2)}) async-start(bf16[4,96,1152]{2,1,0:T(8,128)(2,1)} %get-tuple-element.42.refs_2_), calls=%async_computation.1 | async-start | bytes 1769472 | tf_op jit(solution)/shard_map/all_to_all | solution.py:458
  159.2 8.8 %all-to-all-done.1.pieces = bf16[4,96,1152]{2,1,0:T(8,128)(2,1)S(1)} async-done(((bf16[4,96,1152]{2,1,0:T(8,128)(2,1)}), bf16[4,96,1152]{2,1,0:T(8,128)(2,1)S(1)}, u32[]{:S(2)}, u32[]{:S(2)}) %all-to-all-start.1) | async-done | bytes 884768 | tf_op jit(solution)/shard_map/all_to_all | solution.py:458
  168.3 9.2 %collective-permute-done.22.refs_3_ = bf16[32,3144]{1,0:T(8,128)(2,1)} collective-permute-done((bf16[32,3144]{1,0:T(8,128)(2,1)}, bf16[32,3144]{1,0:T(8,128)(2,1)}, u32[]{:S(2)}, u32[]{:S(2)}) %collective-permute-start.22) | collective-permute-done | bytes 201248 | tf_op jit(solution)/shard_map/ppermute | solution.py:22
  181.7 4.4 %collective-permute-done.24 = bf16[32,3144]{1,0:T(8,128)(2,1)S(1)} collective-permute-done((bf16[32,3144]{1,0:T(8,128)(2,1)}, bf16[32,3144]{1,0:T(8,128)(2,1)S(1)}, u32[]{:S(2)}, u32[]{:S(2)}) %collective-permute-start.24) | collective-permute-done | bytes 201248 | tf_op jit(solution)/shard_map/ppermute | solution.py:465
  186.1 2.3 fusion.8
  188.5 14.1 %collective-permute-done.15.refs_0_.refs_1_ = bf16[12,96,384]{2,1,0:T(8,128)(2,1)S(1)} collective-permute-done((bf16[12,96,384]{2,1,0:T(8,128)(2,1)S(1)}, bf16[12,96,384]{2,1,0:T(8,128)(2,1)S(1)}, u32[]{:S(2)}, u32[]{:S(2)}) %collective-permute-start.15) | collective-permute-done | bytes 884768 | tf_op jit(solution)/shard_map/ppermute | solution.py:22
  204.4 2.1 collective-permute-start.27
  210.4 5.8 %collective-permute-done.26 = bf16[32,3144]{1,0:T(8,128)(2,1)} collective-permute-done((bf16[32,3144]{1,0:T(8,128)(2,1)S(1)}, bf16[32,3144]{1,0:T(8,128)(2,1)}, u32[]{:S(2)}, u32[]{:S(2)}) %collective-permute-start.26) | collective-permute-done | bytes 201248 | tf_op jit(solution)/shard_map/ppermute | solution.py:22
  219.7 8.0 %convert_dynamic-update-slice_fusion = (bf16[12576,384]{1,0:T(8,128)(2,1)S(1)}, f32[3144,384]{1,0:T(8,128)}) fusion(bf16[12576,384]{1,0:T(8,128)(2,1)S(1)} %broadcast_in_dim.9, s32[]{:T(128)S(6)} %select_n.176, f32[64,3144]{1,0:T(8,128)S(1)} %copy-done.19, f32[384,64]{0,1:T(8,128)S(1)} %copy-done.21, f32[1,1,3144,384]{3,2,1,0:T(8,128)S(1)} %bitcast.71), kind=kOutput, calls=%fused_computation.13 | convolution fusion | flops 930825216 | bytes 12990468 | tf_op jit(solution)/shard_map/dot_general | solution.py:475
  232.9 2.2 fusion.2
  235.9 7.1 %collective-permute-done.18.refs_1_ = bf16[1608,384]{1,0:T(8,128)(2,1)S(1)} collective-permute-done((bf16[1608,384]{1,0:T(8,128)(2,1)}, bf16[1608,384]{1,0:T(8,128)(2,1)S(1)}, u32[]{:S(2)}, u32[]{:S(2)}) %collective-permute-start.18) | collective-permute-done | bytes 1234976 | tf_op jit(solution)/shard_map/ppermute | solution.py:22
  248.4 13.6 %collective-permute-done.31.refs_0_ = bf16[12,96,384]{2,1,0:T(8,128)(2,1)S(1)} collective-permute-done((bf16[12,96,384]{2,1,0:T(8,128)(2,1)S(1)}, bf16[12,96,384]{2,1,0:T(8,128)(2,1)S(1)}, u32[]{:S(2)}, u32[]{:S(2)}) %collective-permute-start.31) | collective-permute-done | bytes 884768 | tf_op jit(solution)/shard_map/ppermute | solution.py:22
  263.7 11.7 %collective-permute-done.29.refs_0_ = bf16[12,96,384]{2,1,0:T(8,128)(2,1)S(1)} collective-permute-done((bf16[12,96,384]{2,1,0:T(8,128)(2,1)S(1)}, bf16[12,96,384]{2,1,0:T(8,128)(2,1)S(1)}, u32[]{:S(2)}, u32[]{:S(2)}) %collective-permute-start.29) | collective-permute-done | bytes 884768 | tf_op jit(solution)/shard_map/ppermute | solution.py:22
  (129 shorter events, 66.4 us)
Async XLA Ops:
  3.6 35.2 %collective-permute-start.4 = (bf16[1536,384]{1,0:T(8,128)(2,1)}, bf16[1536,384]{1,0:T(8,128)(2,1)}, u32[]{:S(2)}, u32[]{:S(2)}) collective-permute-start(bf16[1536,384]{1,0:T(8,128)(2,1)} %shard_map.170), channel_id=1, source_target_pairs={{8,16},{16,8},{9,17},{17,9},{10,18},{18,10},{11,19},{19,11},{12,20... | collective-permute-start | bytes 3538952 | tf_op jit(solution)/shard_map/ppermute | solution.py:22
  5.3 33.4 %collective-permute-start.3 = (bf16[1536,384]{1,0:T(8,128)(2,1)}, bf16[1536,384]{1,0:T(8,128)(2,1)}, u32[]{:S(2)}, u32[]{:S(2)}) collective-permute-start(bf16[1536,384]{1,0:T(8,128)(2,1)} %shard_map.170), channel_id=1, source_target_pairs={{8,0},{16,24},{9,1},{17,25},{10,2},{18,26},{11,3},{19,27},{12,4},{... | collective-permute-start | bytes 3538952 | tf_op jit(solution)/shard_map/ppermute | solution.py:22
  10.9 27.9 %collective-permute-start.2 = (bf16[12,96,384]{2,1,0:T(8,128)(2,1)S(1)}, bf16[12,96,384]{2,1,0:T(8,128)(2,1)S(1)}, u32[]{:S(2)}, u32[]{:S(2)}) collective-permute-start(bf16[12,96,384]{2,1,0:T(8,128)(2,1)S(1)} %get-tuple-element.39.refs_0_), channel_id=1, source_target_pairs={{0,8},{24,16},{1,9},{25,17},{2,10},{26,18},{3,11},{27,19},{4,12},{... | collective-permute-start | bytes 2654216 | tf_op jit(solution)/shard_map/ppermute | solution.py:22
  18.8 39.1 %collective-permute-start.1 = (bf16[12,96,384]{2,1,0:T(8,128)(2,1)}, bf16[12,96,384]{2,1,0:T(8,128)(2,1)}, u32[]{:S(2)}, u32[]{:S(2)}) collective-permute-start(bf16[12,96,384]{2,1,0:T(8,128)(2,1)} %get-tuple-element.38.refs_0_), channel_id=1, source_target_pairs={{0,8},{24,16},{1,9},{25,17},{2,10},{26,18},{3,11},{27,19},{4,12},{... | collective-permute-start | bytes 2654216 | tf_op jit(solution)/shard_map/ppermute | solution.py:22
  24.0 39.9 %collective-permute-start.6 = (bf16[1608,384]{1,0:T(8,128)(2,1)}, bf16[1608,384]{1,0:T(8,128)(2,1)}, u32[]{:S(2)}, u32[]{:S(2)}) collective-permute-start(bf16[1608,384]{1,0:T(8,128)(2,1)} %shard_map.172.refs_0_), channel_id=1, source_target_pairs={{8,0},{16,24},{9,1},{17,25},{10,2},{18,26},{11,3},{19,27},{12,4},{... | collective-permute-start | bytes 3704840 | tf_op jit(solution)/shard_map/ppermute | solution.py:22
  39.9 25.7 %collective-permute-start.5 = (bf16[12,96,384]{2,1,0:T(8,128)(2,1)}, bf16[12,96,384]{2,1,0:T(8,128)(2,1)}, u32[]{:S(2)}, u32[]{:S(2)}) collective-permute-start(bf16[12,96,384]{2,1,0:T(8,128)(2,1)} %shard_map.171), channel_id=1, source_target_pairs={{8,16},{16,8},{9,17},{17,9},{10,18},{18,10},{11,19},{19,11},{12,20... | collective-permute-start | bytes 2654216 | tf_op jit(solution)/shard_map/ppermute | solution.py:22
  42.7 26.3 %collective-permute-start.19 = (bf16[32,12576]{1,0:T(8,128)(2,1)}, bf16[32,12576]{1,0:T(8,128)(2,1)}, u32[]{:S(2)}, u32[]{:S(2)}) collective-permute-start(bf16[32,12576]{1,0:T(8,128)(2,1)} %get-tuple-element.65), channel_id=1, source_target_pairs={{0,1},{1,0},{2,3},{3,2},{4,5},{5,4},{6,7},{7,6},{8,9},{9,8},{10,11... | collective-permute-start | bytes 2414600 | tf_op jit(solution)/shard_map/ppermute | solution.py:434
  44.2 32.6 %collective-permute-start = (bf16[12,96,384]{2,1,0:T(8,128)(2,1)}, bf16[12,96,384]{2,1,0:T(8,128)(2,1)}, u32[]{:S(2)}, u32[]{:S(2)}) collective-permute-start(bf16[12,96,384]{2,1,0:T(8,128)(2,1)} %get-tuple-element.36.near), channel_id=1, source_target_pairs={{0,8},{24,16},{1,9},{25,17},{2,10},{26,18},{3,11},{27,19},{4,12},{... | collective-permute-start | bytes 2654216 | tf_op jit(solution)/shard_map/ppermute | solution.py:22
  57.8 42.8 %collective-permute-start.11 = (bf16[1536,384]{1,0:T(8,128)(2,1)}, bf16[1536,384]{1,0:T(8,128)(2,1)}, u32[]{:S(2)}, u32[]{:S(2)}) collective-permute-start(bf16[1536,384]{1,0:T(8,128)(2,1)} %shard_map.170), channel_id=1, source_target_pairs={{0,8},{24,16},{1,9},{25,17},{2,10},{26,18},{3,11},{27,19},{4,12},{... | collective-permute-start | bytes 3538952 | tf_op jit(solution)/shard_map/ppermute | solution.py:22
  63.9 41.2 %collective-permute-start.10 = (bf16[1608,384]{1,0:T(8,128)(2,1)S(1)}, bf16[1608,384]{1,0:T(8,128)(2,1)}, u32[]{:S(2)}, u32[]{:S(2)}) collective-permute-start(bf16[1608,384]{1,0:T(8,128)(2,1)S(1)} %copy-done), channel_id=1, source_target_pairs={{8,16},{16,8},{9,17},{17,9},{10,18},{18,10},{11,19},{19,11},{12,20... | collective-permute-start | bytes 3704840 | tf_op jit(solution)/shard_map/ppermute | solution.py:22
  65.6 40.2 %collective-permute-start.9 = (bf16[1536,384]{1,0:T(8,128)(2,1)}, bf16[1536,384]{1,0:T(8,128)(2,1)S(1)}, u32[]{:S(2)}, u32[]{:S(2)}) collective-permute-start(bf16[1536,384]{1,0:T(8,128)(2,1)} %collective-permute-done.4.refs_3_), channel_id=1, source_target_pairs={{8,0},{16,24},{9,1},{17,25},{10,2},{18,26},{11,3},{19,27},{12,4},{... | collective-permute-start | bytes 3538952 | tf_op jit(solution)/shard_map/ppermute | solution.py:22
  69.0 38.1 %collective-permute-start.7 = (bf16[12,96,384]{2,1,0:T(8,128)(2,1)S(1)}, bf16[12,96,384]{2,1,0:T(8,128)(2,1)S(1)}, u32[]{:S(2)}, u32[]{:S(2)}) collective-permute-start(bf16[12,96,384]{2,1,0:T(8,128)(2,1)S(1)} %get-tuple-element.40.refs_2_), channel_id=1, source_target_pairs={{8,16},{16,8},{9,17},{17,9},{10,18},{18,10},{11,19},{19,11},{12,20... | collective-permute-start | bytes 2654216 | tf_op jit(solution)/shard_map/ppermute | solution.py:22
  76.8 38.7 %collective-permute-start.8 = (bf16[12,96,384]{2,1,0:T(8,128)(2,1)S(1)}, bf16[12,96,384]{2,1,0:T(8,128)(2,1)S(1)}, u32[]{:S(2)}, u32[]{:S(2)}) collective-permute-start(bf16[12,96,384]{2,1,0:T(8,128)(2,1)S(1)} %get-tuple-element.41), channel_id=1, source_target_pairs={{8,0},{16,24},{9,1},{17,25},{10,2},{18,26},{11,3},{19,27},{12,4},{... | collective-permute-start | bytes 2654216 | tf_op jit(solution)/shard_map/ppermute | solution.py:22
  100.6 20.5 %collective-permute-start.20 = (bf16[3,32,3144]{2,1,0:T(8,128)(2,1)S(1)}, bf16[3,32,3144]{2,1,0:T(8,128)(2,1)S(1)}, u32[]{:S(2)}, u32[]{:S(2)}) collective-permute-start(bf16[3,32,3144]{2,1,0:T(8,128)(2,1)S(1)} %pad_maximum_fusion), channel_id=1, source_target_pairs={{0,8},{24,16},{1,9},{25,17},{2,10},{26,18},{3,11},{27,19},{4,12},{... | collective-permute-start | bytes 1810952 | tf_op jit(solution)/shard_map/ppermute | solution.py:22
  105.0 40.0 %collective-permute-start.13 = (bf16[1536,384]{1,0:T(8,128)(2,1)}, bf16[1536,384]{1,0:T(8,128)(2,1)S(1)}, u32[]{:S(2)}, u32[]{:S(2)}) collective-permute-start(bf16[1536,384]{1,0:T(8,128)(2,1)} %collective-permute-done.11.refs_2_), channel_id=1, source_target_pairs={{8,16},{16,8},{9,17},{17,9},{10,18},{18,10},{11,19},{19,11},{12,20... | collective-permute-start | bytes 3538952 | tf_op jit(solution)/shard_map/ppermute | solution.py:22
  105.8 40.9 %collective-permute-start.12 = (bf16[1608,384]{1,0:T(8,128)(2,1)}, bf16[1608,384]{1,0:T(8,128)(2,1)}, u32[]{:S(2)}, u32[]{:S(2)}) collective-permute-start(bf16[1608,384]{1,0:T(8,128)(2,1)} %collective-permute-done.10.refs_1_), channel_id=1, source_target_pairs={{8,0},{16,24},{9,1},{17,25},{10,2},{18,26},{11,3},{19,27},{12,4},{... | collective-permute-start | bytes 3704840 | tf_op jit(solution)/shard_map/ppermute | solution.py:22
  118.6 24.8 %collective-permute-start.14 = (bf16[1608,384]{1,0:T(8,128)(2,1)S(1)}, bf16[1608,384]{1,0:T(8,128)(2,1)}, u32[]{:S(2)}, u32[]{:S(2)}) collective-permute-start(bf16[1608,384]{1,0:T(8,128)(2,1)S(1)} %shard_map.176), channel_id=1, source_target_pairs={{0,8},{24,16},{1,9},{25,17},{2,10},{26,18},{3,11},{27,19},{4,12},{... | collective-permute-start | bytes 3704840 | tf_op jit(solution)/shard_map/ppermute | solution.py:22
  121.9 23.2 %all-to-all-start = ((bf16[4,96,1152]{2,1,0:T(8,128)(2,1)}), bf16[4,96,1152]{2,1,0:T(8,128)(2,1)S(1)}, u32[]{:S(2)}, u32[]{:S(2)}) async-start(bf16[4,96,1152]{2,1,0:T(8,128)(2,1)} %shard_map.174.refs_1_.refs_4_), calls=%async_computation | async-start | bytes 1769472 | tf_op jit(solution)/shard_map/all_to_all | solution.py:450
  129.1 26.3 %collective-permute-start.21 = (bf16[2,32,3144]{2,1,0:T(8,128)(2,1)}, bf16[2,32,3144]{2,1,0:T(8,128)(2,1)}, u32[]{:S(2)}, u32[]{:S(2)}) collective-permute-start(bf16[2,32,3144]{2,1,0:T(8,128)(2,1)} %pad_maximum_fusion.2), channel_id=1, source_target_pairs={{8,16},{16,8},{9,17},{17,9},{10,18},{18,10},{11,19},{19,11},{12,20... | collective-permute-start | bytes 1207304 | tf_op jit(solution)/shard_map/ppermute | solution.py:22
  143.4 34.1 %collective-permute-start.17 = (bf16[1608,384]{1,0:T(8,128)(2,1)}, bf16[1608,384]{1,0:T(8,128)(2,1)}, u32[]{:S(2)}, u32[]{:S(2)}) collective-permute-start(bf16[1608,384]{1,0:T(8,128)(2,1)} %collective-permute-done.14.refs_2_), channel_id=1, source_target_pairs={{8,16},{16,8},{9,17},{17,9},{10,18},{18,10},{11,19},{19,11},{12,20... | collective-permute-start | bytes 3704840 | tf_op jit(solution)/shard_map/ppermute | solution.py:22
  145.1 32.4 %collective-permute-start.23 = (bf16[1536,384]{1,0:T(8,128)(2,1)S(1)}, bf16[1536,384]{1,0:T(8,128)(2,1)}, u32[]{:S(2)}, u32[]{:S(2)}) collective-permute-start(bf16[1536,384]{1,0:T(8,128)(2,1)S(1)} %shard_map.175.refs_1_), channel_id=1, source_target_pairs={{8,0},{16,24},{9,1},{17,25},{10,2},{18,26},{11,3},{19,27},{12,4},{... | collective-permute-start | bytes 3538952 | tf_op jit(solution)/shard_map/ppermute | solution.py:22
  151.7 16.3 %all-to-all-start.1 = ((bf16[4,96,1152]{2,1,0:T(8,128)(2,1)}), bf16[4,96,1152]{2,1,0:T(8,128)(2,1)S(1)}, u32[]{:S(2)}, u32[]{:S(2)}) async-start(bf16[4,96,1152]{2,1,0:T(8,128)(2,1)} %get-tuple-element.42.refs_2_), calls=%async_computation.1 | async-start | bytes 1769472 | tf_op jit(solution)/shard_map/all_to_all | solution.py:458
  157.9 19.6 %collective-permute-start.22 = (bf16[32,3144]{1,0:T(8,128)(2,1)}, bf16[32,3144]{1,0:T(8,128)(2,1)}, u32[]{:S(2)}, u32[]{:S(2)}) collective-permute-start(bf16[32,3144]{1,0:T(8,128)(2,1)} %shard_map.182), channel_id=1, source_target_pairs={{8,0},{16,24},{9,1},{17,25},{10,2},{18,26},{11,3},{19,27},{12,4},{... | collective-permute-start | bytes 603656 | tf_op jit(solution)/shard_map/ppermute | solution.py:22
  181.7 20.9 %collective-permute-start.15 = (bf16[12,96,384]{2,1,0:T(8,128)(2,1)S(1)}, bf16[12,96,384]{2,1,0:T(8,128)(2,1)S(1)}, u32[]{:S(2)}, u32[]{:S(2)}) collective-permute-start(bf16[12,96,384]{2,1,0:T(8,128)(2,1)S(1)} %shard_map.178.refs_4_.refs_0_.refs_1_), channel_id=1, source_target_pairs={{0,8},{24,16},{8,0},{16,24},{1,9},{25,17},{9,1},{17,25},{2,10},{26... | collective-permute-start | bytes 2654216 | tf_op jit(solution)/shard_map/ppermute | solution.py:22
  202.7 13.5 %collective-permute-start.26 = (bf16[32,3144]{1,0:T(8,128)(2,1)S(1)}, bf16[32,3144]{1,0:T(8,128)(2,1)}, u32[]{:S(2)}, u32[]{:S(2)}) collective-permute-start(bf16[32,3144]{1,0:T(8,128)(2,1)S(1)} %shard_map.184), channel_id=1, source_target_pairs={{0,16},{8,24},{16,0},{24,8},{1,17},{9,25},{17,1},{25,9},{2,18},{10... | collective-permute-start | bytes 603656 | tf_op jit(solution)/shard_map/ppermute | solution.py:22
  204.4 12.3 %collective-permute-start.27 = (bf16[32,3144]{1,0:T(8,128)(2,1)S(1)}, bf16[32,3144]{1,0:T(8,128)(2,1)}, u32[]{:S(2)}, u32[]{:S(2)}) collective-permute-start(bf16[32,3144]{1,0:T(8,128)(2,1)S(1)} %shard_map.184), channel_id=1, source_target_pairs={{0,24},{8,0},{16,8},{24,16},{1,25},{9,1},{17,9},{25,17},{2,26},{10... | collective-permute-start | bytes 603656 | tf_op jit(solution)/shard_map/ppermute | solution.py:22
  207.4 21.0 %collective-permute-start.30 = (bf16[12,96,384]{2,1,0:T(8,128)(2,1)S(1)}, bf16[12,96,384]{2,1,0:T(8,128)(2,1)S(1)}, u32[]{:S(2)}, u32[]{:S(2)}) collective-permute-start(bf16[12,96,384]{2,1,0:T(8,128)(2,1)S(1)} %shard_map.178.refs_4_.refs_0_.refs_1_), channel_id=1, source_target_pairs={{8,16},{16,8},{9,17},{17,9},{10,18},{18,10},{11,19},{19,11},{12,20... | collective-permute-start | bytes 2654216 | tf_op jit(solution)/shard_map/ppermute | solution.py:22
  208.1 34.9 %collective-permute-start.18 = (bf16[1608,384]{1,0:T(8,128)(2,1)}, bf16[1608,384]{1,0:T(8,128)(2,1)S(1)}, u32[]{:S(2)}, u32[]{:S(2)}) collective-permute-start(bf16[1608,384]{1,0:T(8,128)(2,1)} %collective-permute-done.17.refs_6_), channel_id=1, source_target_pairs={{8,0},{16,24},{9,1},{17,25},{10,2},{18,26},{11,3},{19,27},{12,4},{... | collective-permute-start | bytes 3704840 | tf_op jit(solution)/shard_map/ppermute | solution.py:22
  218.0 12.7 %collective-permute-start.28 = (bf16[3,32,3144]{2,1,0:T(8,128)(2,1)S(1)}, bf16[3,32,3144]{2,1,0:T(8,128)(2,1)S(1)}, u32[]{:S(2)}, u32[]{:S(2)}) collective-permute-start(bf16[3,32,3144]{2,1,0:T(8,128)(2,1)S(1)} %pad_maximum_fusion.1), channel_id=1, source_target_pairs={{0,1},{1,0},{2,3},{3,2},{4,5},{5,4},{6,7},{7,6},{8,9},{9,8},{10,11... | collective-permute-start | bytes 1810952 | tf_op jit(solution)/shard_map/ppermute | solution.py:485
  227.7 8.2 %collective-permute-start.16 = (bf16[12,96,384]{2,1,0:T(8,128)(2,1)S(1)}, bf16[12,96,384]{2,1,0:T(8,128)(2,1)S(1)}, u32[]{:S(2)}, u32[]{:S(2)}) collective-permute-start(bf16[12,96,384]{2,1,0:T(8,128)(2,1)S(1)} %collective-permute-done.15.refs_0_.refs_1_), channel_id=1, source_target_pairs={{8,16},{16,8},{9,17},{17,9},{10,18},{18,10},{11,19},{19,11},{12,20... | collective-permute-start | bytes 2654216 | tf_op jit(solution)/shard_map/ppermute | solution.py:22
  228.4 33.6 %collective-permute-start.31 = (bf16[12,96,384]{2,1,0:T(8,128)(2,1)S(1)}, bf16[12,96,384]{2,1,0:T(8,128)(2,1)S(1)}, u32[]{:S(2)}, u32[]{:S(2)}) collective-permute-start(bf16[12,96,384]{2,1,0:T(8,128)(2,1)S(1)} %collective-permute-done.30.refs_1_), channel_id=1, source_target_pairs={{8,0},{16,24},{9,1},{17,25},{10,2},{18,26},{11,3},{19,27},{12,4},{... | collective-permute-start | bytes 2654216 | tf_op jit(solution)/shard_map/ppermute | solution.py:22
  243.1 32.4 %collective-permute-start.29 = (bf16[12,96,384]{2,1,0:T(8,128)(2,1)S(1)}, bf16[12,96,384]{2,1,0:T(8,128)(2,1)S(1)}, u32[]{:S(2)}, u32[]{:S(2)}) collective-permute-start(bf16[12,96,384]{2,1,0:T(8,128)(2,1)S(1)} %shard_map.185.refs_1_), channel_id=1, source_target_pairs={{8,0},{16,24},{9,1},{17,25},{10,2},{18,26},{11,3},{19,27},{12,4},{... | collective-permute-start | bytes 2654216 | tf_op jit(solution)/shard_map/ppermute | solution.py:22
  (26 other events, 197.7 us)

commit v6 on v5

--- a/solution.py
+++ b/solution.py
@@ -476,7 +476,7 @@
             toward, basis, (((0,), (1,)), ((), ())), precision=precision, preferred_element_type=jnp.float32
         )
 
-    next_embed = embed_owner[0, 0] - update(direction, lax.Precision.HIGHEST)
+    next_embed = embed_owner[0, 0] - update(direction, lax.Precision.HIGH)
     half = lax.dynamic_slice_in_dim(direction, side * half_rank, half_rank, 0).astype(jnp.bfloat16)
     half = after(half, block_near)
 

time: 278 us -> 278 us (level)
  transfers between devices with their start and end apart: 34 -> 34, of which waited for: 17 -> 17; matrix products, arithmetic and copies ran while one was open for 14% -> 13% of each run, Pallas kernels for 7% -> 7%
where the time goes in v6:
time: 278 us; the launch traced here: 277 us
  waiting for transfers between devices  137 us (49%)
  starting transfers between devices  69.1 us (25%)
  Pallas kernels  25.2 us (9%)
  matrix products  24.8 us (9%)
  local copies, waits for them, and re-layouts  12.7 us (5%)
  other arithmetic  5.78 us (2%)
    ppermute x29, waiting for transfers between devices, permute(): return lax.ppermute(value, 'rep', pairs)  124 us
    ppermute x29, starting transfers between devices, permute(): return lax.ppermute(value, 'rep', pairs)  58.4 us
    dot_general x7, matrix products, update(): lax.dot_general(toward, basis, (((0,), (1,)), ((), ())), precision=precis...  15.2 us
    dot_general x1, matrix products, local(): lax.dot_general(after(basis, far), wide(delta_embed[0]), (((0,), (1,)), (...  9.62 us
    all_to_all x1, waiting for transfers between devices, local(): lax.all_to_all(copies, 'shard', split_axis=0, concat_axis=0, tiled=True)  8.83 us
    unnamed x49, local copies, waits for them, and re-layouts  8.06 us
    pallas_call x2, Pallas kernels, narrow_rows(): kernel_call(functools.partial(narrow_kernel, first), jax.ShapeDtypeStruct...  5.79 us
  transfers between devices with their start and end apart: 34, of which 17 were waited for; matrix products, arithmetic and copies ran while one was open for 13% of the time, Pallas kernels for 7%

profile of v6, /device:TPU:0, one launch (start us, length us, event | category | flops | bytes accessed | tf_op | source)
XLA Modules:
  0.0 276.5 jit_solution(8864107476434765065)
XLA Ops:
  0.7 2.9 %shard_map.170 = bf16[1536,384]{1,0:T(8,128)(2,1)} custom-call(f32[3144,384]{1,0:T(8,128)} %bitcast.68), custom_call_target="tpu_custom_call" | custom-call | bytes 3538944 | tf_op jit(solution)/shard_map/pallas_call | solution.py:240
  10.9 7.8 %collective-permute-start.2 = (bf16[12,96,384]{2,1,0:T(8,128)(2,1)S(1)}, bf16[12,96,384]{2,1,0:T(8,128)(2,1)S(1)}, u32[]{:S(2)}, u32[]{:S(2)}) collective-permute-start(bf16[12,96,384]{2,1,0:T(8,128)(2,1)S(1)} %get-tuple-element.39.refs_0_), channel_id=1, source_target_pairs={{0,8},{24,16},{1,9},{25,17},{2,10},{26,18},{3,11},{27,19},{4,12},{... | collective-permute-start | bytes 2654216 | tf_op jit(solution)/shard_map/ppermute | solution.py:22
  18.8 2.3 collective-permute-start.1
  21.1 2.9 %shard_map.172.refs_0_ = bf16[1608,384]{1,0:T(8,128)(2,1)} custom-call(f32[3144,384]{1,0:T(8,128)} %bitcast.69), custom_call_target="tpu_custom_call" | custom-call | bytes 3704832 | tf_op jit(solution)/shard_map/pallas_call | solution.py:240
  25.4 9.6 %convolution_convert_fusion = bf16[64,12576]{1,0:T(8,128)(2,1)S(1)} fusion(f32[384,64]{1,0:T(8,128)S(1)} %shard_map.179, bf16[1,12576,384]{2,1,0:T(8,128)(2,1)} %param.16), kind=kOutput, calls=%fused_computation | convolution fusion | flops 1855211520 | bytes 11366400 | tf_op jit(solution)/shard_map/dot_general | solution.py:425
  35.1 3.7 %collective-permute-done.2.refs_1_ = bf16[12,96,384]{2,1,0:T(8,128)(2,1)S(1)} collective-permute-done((bf16[12,96,384]{2,1,0:T(8,128)(2,1)S(1)}, bf16[12,96,384]{2,1,0:T(8,128)(2,1)S(1)}, u32[]{:S(2)}, u32[]{:S(2)}) %collective-permute-start.2) | collective-permute-done | bytes 884768 | tf_op jit(solution)/shard_map/ppermute | solution.py:22
  44.2 7.7 %collective-permute-start = (bf16[12,96,384]{2,1,0:T(8,128)(2,1)}, bf16[12,96,384]{2,1,0:T(8,128)(2,1)}, u32[]{:S(2)}, u32[]{:S(2)}) collective-permute-start(bf16[12,96,384]{2,1,0:T(8,128)(2,1)} %get-tuple-element.36.near), channel_id=1, source_target_pairs={{0,8},{24,16},{1,9},{25,17},{2,10},{26,18},{3,11},{27,19},{4,12},{... | collective-permute-start | bytes 2654216 | tf_op jit(solution)/shard_map/ppermute | solution.py:22
  51.9 6.0 %collective-permute-done.1.refs_2_ = bf16[12,96,384]{2,1,0:T(8,128)(2,1)} collective-permute-done((bf16[12,96,384]{2,1,0:T(8,128)(2,1)}, bf16[12,96,384]{2,1,0:T(8,128)(2,1)}, u32[]{:S(2)}, u32[]{:S(2)}) %collective-permute-start.1) | collective-permute-done | bytes 884768 | tf_op jit(solution)/shard_map/ppermute | solution.py:22
  57.8 5.4 %collective-permute-start.11 = (bf16[1536,384]{1,0:T(8,128)(2,1)}, bf16[1536,384]{1,0:T(8,128)(2,1)}, u32[]{:S(2)}, u32[]{:S(2)}) collective-permute-start(bf16[1536,384]{1,0:T(8,128)(2,1)} %shard_map.170), channel_id=1, source_target_pairs={{0,8},{24,16},{1,9},{25,17},{2,10},{26,18},{3,11},{27,19},{4,12},{... | collective-permute-start | bytes 3538952 | tf_op jit(solution)/shard_map/ppermute | solution.py:22
  66.9 2.1 shard_map.173
  72.2 4.6 %collective-permute-done.from_out = bf16[12,96,384]{2,1,0:T(8,128)(2,1)} collective-permute-done((bf16[12,96,384]{2,1,0:T(8,128)(2,1)}, bf16[12,96,384]{2,1,0:T(8,128)(2,1)}, u32[]{:S(2)}, u32[]{:S(2)}) %collective-permute-start) | collective-permute-done | bytes 884768 | tf_op jit(solution)/shard_map/ppermute | solution.py:22
  78.2 22.4 %collective-permute-done.11.refs_2_ = bf16[1536,384]{1,0:T(8,128)(2,1)} collective-permute-done((bf16[1536,384]{1,0:T(8,128)(2,1)}, bf16[1536,384]{1,0:T(8,128)(2,1)}, u32[]{:S(2)}, u32[]{:S(2)}) %collective-permute-start.11) | collective-permute-done | bytes 1179680 | tf_op jit(solution)/shard_map/ppermute | solution.py:22
  100.6 4.4 %collective-permute-start.20 = (bf16[3,32,3144]{2,1,0:T(8,128)(2,1)S(1)}, bf16[3,32,3144]{2,1,0:T(8,128)(2,1)S(1)}, u32[]{:S(2)}, u32[]{:S(2)}) collective-permute-start(bf16[3,32,3144]{2,1,0:T(8,128)(2,1)S(1)} %pad_maximum_fusion), channel_id=1, source_target_pairs={{0,8},{24,16},{1,9},{25,17},{2,10},{26,18},{3,11},{27,19},{4,12},{... | collective-permute-start | bytes 1810952 | tf_op jit(solution)/shard_map/ppermute | solution.py:22
  107.1 8.4 %collective-permute-done.8.from_in = bf16[12,96,384]{2,1,0:T(8,128)(2,1)S(1)} collective-permute-done((bf16[12,96,384]{2,1,0:T(8,128)(2,1)S(1)}, bf16[12,96,384]{2,1,0:T(8,128)(2,1)S(1)}, u32[]{:S(2)}, u32[]{:S(2)}) %collective-permute-start.8) | collective-permute-done | bytes 884768 | tf_op jit(solution)/shard_map/ppermute | solution.py:22
  115.5 3.1 %shard_map.174.refs_1_.refs_4_ = bf16[4,96,1152]{2,1,0:T(8,128)(2,1)} custom-call(bf16[12,96,384]{2,1,0:T(8,128)(2,1)} %get-tuple-element.36.near, bf16[12,96,384]{2,1,0:T(8,128)(2,1)S(1)} %get-tuple-element.37.refs_1_.last, bf16[12,96,384]{2,1,0:T(8,128)(2,1)} %collective-permute-done.from_out, bf16[12,96,384]{2,1,0:T(8,128)(2,1)S(1)} %collective-permute-done.7.from_middle, ...), custom_call_target="tpu_custom_call" | custom-call | bytes 7962624 | tf_op jit(solution)/shard_map/pallas_call | solution.py:293
  118.6 2.5 collective-permute-start.14
  121.9 3.5 %all-to-all-start = ((bf16[4,96,1152]{2,1,0:T(8,128)(2,1)}), bf16[4,96,1152]{2,1,0:T(8,128)(2,1)S(1)}, u32[]{:S(2)}, u32[]{:S(2)}) async-start(bf16[4,96,1152]{2,1,0:T(8,128)(2,1)} %shard_map.174.refs_1_.refs_4_), calls=%async_computation | async-start | bytes 1769472 | tf_op jit(solution)/shard_map/all_to_all | solution.py:450
  130.5 12.8 %collective-permute-done.14.refs_2_ = bf16[1608,384]{1,0:T(8,128)(2,1)} collective-permute-done((bf16[1608,384]{1,0:T(8,128)(2,1)S(1)}, bf16[1608,384]{1,0:T(8,128)(2,1)}, u32[]{:S(2)}, u32[]{:S(2)}) %collective-permute-start.14) | collective-permute-done | bytes 1234976 | tf_op jit(solution)/shard_map/ppermute | solution.py:22
  148.2 3.5 %shard_map.177 = (f32[3456,128]{1,0:T(8,128)}, f32[3456,128]{1,0:T(8,128)}, bf16[4,96,1152]{2,1,0:T(8,128)(2,1)}) custom-call(bf16[4,96,1152]{2,1,0:T(8,128)(2,1)S(1)} %all-to-all-done.refs_1_.moved, f32[3456,128]{1,0:T(8,128)S(1)} %bitcast.64, f32[3456,128]{1,0:T(8,128)S(1)} %bitcast.65, bf16[1608,384]{1,0:T(8,128)(2,1)} %collective-permute-done.12.refs_0_, ...), custom_call_target="tpu_custom_call" | custom-call | bytes 8847360 | tf_op jit(solution)/shard_map/pallas_call | solution.py:355
  151.7 3.6 %all-to-all-start.1 = ((bf16[4,96,1152]{2,1,0:T(8,128)(2,1)}), bf16[4,96,1152]{2,1,0:T(8,128)(2,1)S(1)}, u32[]{:S(2)}, u32[]{:S(2)}) async-start(bf16[4,96,1152]{2,1,0:T(8,128)(2,1)} %get-tuple-element.42.refs_2_), calls=%async_computation.1 | async-start | bytes 1769472 | tf_op jit(solution)/shard_map/all_to_all | solution.py:458
  159.2 8.8 %all-to-all-done.1.pieces = bf16[4,96,1152]{2,1,0:T(8,128)(2,1)S(1)} async-done(((bf16[4,96,1152]{2,1,0:T(8,128)(2,1)}), bf16[4,96,1152]{2,1,0:T(8,128)(2,1)S(1)}, u32[]{:S(2)}, u32[]{:S(2)}) %all-to-all-start.1) | async-done | bytes 884768 | tf_op jit(solution)/shard_map/all_to_all | solution.py:458
  168.3 9.2 %collective-permute-done.22.refs_3_ = bf16[32,3144]{1,0:T(8,128)(2,1)} collective-permute-done((bf16[32,3144]{1,0:T(8,128)(2,1)}, bf16[32,3144]{1,0:T(8,128)(2,1)}, u32[]{:S(2)}, u32[]{:S(2)}) %collective-permute-start.22) | collective-permute-done | bytes 201248 | tf_op jit(solution)/shard_map/ppermute | solution.py:22
  181.7 4.4 %collective-permute-done.24 = bf16[32,3144]{1,0:T(8,128)(2,1)S(1)} collective-permute-done((bf16[32,3144]{1,0:T(8,128)(2,1)}, bf16[32,3144]{1,0:T(8,128)(2,1)S(1)}, u32[]{:S(2)}, u32[]{:S(2)}) %collective-permute-start.24) | collective-permute-done | bytes 201248 | tf_op jit(solution)/shard_map/ppermute | solution.py:465
  186.1 2.3 fusion.8
  188.5 14.1 %collective-permute-done.15.refs_0_.refs_1_ = bf16[12,96,384]{2,1,0:T(8,128)(2,1)S(1)} collective-permute-done((bf16[12,96,384]{2,1,0:T(8,128)(2,1)S(1)}, bf16[12,96,384]{2,1,0:T(8,128)(2,1)S(1)}, u32[]{:S(2)}, u32[]{:S(2)}) %collective-permute-start.15) | collective-permute-done | bytes 884768 | tf_op jit(solution)/shard_map/ppermute | solution.py:22
  204.4 2.1 collective-permute-start.27
  210.4 5.8 %collective-permute-done.26 = bf16[32,3144]{1,0:T(8,128)(2,1)} collective-permute-done((bf16[32,3144]{1,0:T(8,128)(2,1)S(1)}, bf16[32,3144]{1,0:T(8,128)(2,1)}, u32[]{:S(2)}, u32[]{:S(2)}) %collective-permute-start.26) | collective-permute-done | bytes 201248 | tf_op jit(solution)/shard_map/ppermute | solution.py:22
  219.7 5.5 %convert_dynamic-update-slice_fusion = (bf16[12576,384]{1,0:T(8,128)(2,1)S(1)}, f32[3144,384]{1,0:T(8,128)}) fusion(bf16[12576,384]{1,0:T(8,128)(2,1)S(1)} %broadcast_in_dim.9, s32[]{:T(128)S(6)} %select_n.176, f32[64,3144]{1,0:T(8,128)S(1)} %copy-done.19, f32[384,64]{0,1:T(8,128)S(1)} %copy-done.21, f32[1,1,3144,384]{3,2,1,0:T(8,128)S(1)} %bitcast.71), kind=kOutput, calls=%fused_computation.13 | convolution fusion | flops 467223552 | bytes 12990468 | tf_op jit(solution)/shard_map/dot_general | solution.py:475
  230.4 2.2 fusion.2
  233.4 9.6 %collective-permute-done.18.refs_1_ = bf16[1608,384]{1,0:T(8,128)(2,1)S(1)} collective-permute-done((bf16[1608,384]{1,0:T(8,128)(2,1)}, bf16[1608,384]{1,0:T(8,128)(2,1)S(1)}, u32[]{:S(2)}, u32[]{:S(2)}) %collective-permute-start.18) | collective-permute-done | bytes 1234976 | tf_op jit(solution)/shard_map/ppermute | solution.py:22
  248.4 13.6 %collective-permute-done.31.refs_0_ = bf16[12,96,384]{2,1,0:T(8,128)(2,1)S(1)} collective-permute-done((bf16[12,96,384]{2,1,0:T(8,128)(2,1)S(1)}, bf16[12,96,384]{2,1,0:T(8,128)(2,1)S(1)}, u32[]{:S(2)}, u32[]{:S(2)}) %collective-permute-start.31) | collective-permute-done | bytes 884768 | tf_op jit(solution)/shard_map/ppermute | solution.py:22
  263.7 11.7 %collective-permute-done.29.refs_0_ = bf16[12,96,384]{2,1,0:T(8,128)(2,1)S(1)} collective-permute-done((bf16[12,96,384]{2,1,0:T(8,128)(2,1)S(1)}, bf16[12,96,384]{2,1,0:T(8,128)(2,1)S(1)}, u32[]{:S(2)}, u32[]{:S(2)}) %collective-permute-start.29) | collective-permute-done | bytes 884768 | tf_op jit(solution)/shard_map/ppermute | solution.py:22
  (129 shorter events, 66.4 us)
Async XLA Ops:
  3.6 35.2 %collective-permute-start.4 = (bf16[1536,384]{1,0:T(8,128)(2,1)}, bf16[1536,384]{1,0:T(8,128)(2,1)}, u32[]{:S(2)}, u32[]{:S(2)}) collective-permute-start(bf16[1536,384]{1,0:T(8,128)(2,1)} %shard_map.170), channel_id=1, source_target_pairs={{8,16},{16,8},{9,17},{17,9},{10,18},{18,10},{11,19},{19,11},{12,20... | collective-permute-start | bytes 3538952 | tf_op jit(solution)/shard_map/ppermute | solution.py:22
  5.3 33.4 %collective-permute-start.3 = (bf16[1536,384]{1,0:T(8,128)(2,1)}, bf16[1536,384]{1,0:T(8,128)(2,1)}, u32[]{:S(2)}, u32[]{:S(2)}) collective-permute-start(bf16[1536,384]{1,0:T(8,128)(2,1)} %shard_map.170), channel_id=1, source_target_pairs={{8,0},{16,24},{9,1},{17,25},{10,2},{18,26},{11,3},{19,27},{12,4},{... | collective-permute-start | bytes 3538952 | tf_op jit(solution)/shard_map/ppermute | solution.py:22
  10.9 27.9 %collective-permute-start.2 = (bf16[12,96,384]{2,1,0:T(8,128)(2,1)S(1)}, bf16[12,96,384]{2,1,0:T(8,128)(2,1)S(1)}, u32[]{:S(2)}, u32[]{:S(2)}) collective-permute-start(bf16[12,96,384]{2,1,0:T(8,128)(2,1)S(1)} %get-tuple-element.39.refs_0_), channel_id=1, source_target_pairs={{0,8},{24,16},{1,9},{25,17},{2,10},{26,18},{3,11},{27,19},{4,12},{... | collective-permute-start | bytes 2654216 | tf_op jit(solution)/shard_map/ppermute | solution.py:22
  18.8 39.1 %collective-permute-start.1 = (bf16[12,96,384]{2,1,0:T(8,128)(2,1)}, bf16[12,96,384]{2,1,0:T(8,128)(2,1)}, u32[]{:S(2)}, u32[]{:S(2)}) collective-permute-start(bf16[12,96,384]{2,1,0:T(8,128)(2,1)} %get-tuple-element.38.refs_0_), channel_id=1, source_target_pairs={{0,8},{24,16},{1,9},{25,17},{2,10},{26,18},{3,11},{27,19},{4,12},{... | collective-permute-start | bytes 2654216 | tf_op jit(solution)/shard_map/ppermute | solution.py:22
  24.0 39.9 %collective-permute-start.6 = (bf16[1608,384]{1,0:T(8,128)(2,1)}, bf16[1608,384]{1,0:T(8,128)(2,1)}, u32[]{:S(2)}, u32[]{:S(2)}) collective-permute-start(bf16[1608,384]{1,0:T(8,128)(2,1)} %shard_map.172.refs_0_), channel_id=1, source_target_pairs={{8,0},{16,24},{9,1},{17,25},{10,2},{18,26},{11,3},{19,27},{12,4},{... | collective-permute-start | bytes 3704840 | tf_op jit(solution)/shard_map/ppermute | solution.py:22
  39.9 25.7 %collective-permute-start.5 = (bf16[12,96,384]{2,1,0:T(8,128)(2,1)}, bf16[12,96,384]{2,1,0:T(8,128)(2,1)}, u32[]{:S(2)}, u32[]{:S(2)}) collective-permute-start(bf16[12,96,384]{2,1,0:T(8,128)(2,1)} %shard_map.171), channel_id=1, source_target_pairs={{8,16},{16,8},{9,17},{17,9},{10,18},{18,10},{11,19},{19,11},{12,20... | collective-permute-start | bytes 2654216 | tf_op jit(solution)/shard_map/ppermute | solution.py:22
  42.7 26.3 %collective-permute-start.19 = (bf16[32,12576]{1,0:T(8,128)(2,1)}, bf16[32,12576]{1,0:T(8,128)(2,1)}, u32[]{:S(2)}, u32[]{:S(2)}) collective-permute-start(bf16[32,12576]{1,0:T(8,128)(2,1)} %get-tuple-element.65), channel_id=1, source_target_pairs={{0,1},{1,0},{2,3},{3,2},{4,5},{5,4},{6,7},{7,6},{8,9},{9,8},{10,11... | collective-permute-start | bytes 2414600 | tf_op jit(solution)/shard_map/ppermute | solution.py:434
  44.2 32.6 %collective-permute-start = (bf16[12,96,384]{2,1,0:T(8,128)(2,1)}, bf16[12,96,384]{2,1,0:T(8,128)(2,1)}, u32[]{:S(2)}, u32[]{:S(2)}) collective-permute-start(bf16[12,96,384]{2,1,0:T(8,128)(2,1)} %get-tuple-element.36.near), channel_id=1, source_target_pairs={{0,8},{24,16},{1,9},{25,17},{2,10},{26,18},{3,11},{27,19},{4,12},{... | collective-permute-start | bytes 2654216 | tf_op jit(solution)/shard_map/ppermute | solution.py:22
  57.8 42.8 %collective-permute-start.11 = (bf16[1536,384]{1,0:T(8,128)(2,1)}, bf16[1536,384]{1,0:T(8,128)(2,1)}, u32[]{:S(2)}, u32[]{:S(2)}) collective-permute-start(bf16[1536,384]{1,0:T(8,128)(2,1)} %shard_map.170), channel_id=1, source_target_pairs={{0,8},{24,16},{1,9},{25,17},{2,10},{26,18},{3,11},{27,19},{4,12},{... | collective-permute-start | bytes 3538952 | tf_op jit(solution)/shard_map/ppermute | solution.py:22
  63.9 41.2 %collective-permute-start.10 = (bf16[1608,384]{1,0:T(8,128)(2,1)S(1)}, bf16[1608,384]{1,0:T(8,128)(2,1)}, u32[]{:S(2)}, u32[]{:S(2)}) collective-permute-start(bf16[1608,384]{1,0:T(8,128)(2,1)S(1)} %copy-done), channel_id=1, source_target_pairs={{8,16},{16,8},{9,17},{17,9},{10,18},{18,10},{11,19},{19,11},{12,20... | collective-permute-start | bytes 3704840 | tf_op jit(solution)/shard_map/ppermute | solution.py:22
  65.6 40.2 %collective-permute-start.9 = (bf16[1536,384]{1,0:T(8,128)(2,1)}, bf16[1536,384]{1,0:T(8,128)(2,1)S(1)}, u32[]{:S(2)}, u32[]{:S(2)}) collective-permute-start(bf16[1536,384]{1,0:T(8,128)(2,1)} %collective-permute-done.4.refs_3_), channel_id=1, source_target_pairs={{8,0},{16,24},{9,1},{17,25},{10,2},{18,26},{11,3},{19,27},{12,4},{... | collective-permute-start | bytes 3538952 | tf_op jit(solution)/shard_map/ppermute | solution.py:22
  69.0 38.1 %collective-permute-start.7 = (bf16[12,96,384]{2,1,0:T(8,128)(2,1)S(1)}, bf16[12,96,384]{2,1,0:T(8,128)(2,1)S(1)}, u32[]{:S(2)}, u32[]{:S(2)}) collective-permute-start(bf16[12,96,384]{2,1,0:T(8,128)(2,1)S(1)} %get-tuple-element.40.refs_2_), channel_id=1, source_target_pairs={{8,16},{16,8},{9,17},{17,9},{10,18},{18,10},{11,19},{19,11},{12,20... | collective-permute-start | bytes 2654216 | tf_op jit(solution)/shard_map/ppermute | solution.py:22
  76.8 38.7 %collective-permute-start.8 = (bf16[12,96,384]{2,1,0:T(8,128)(2,1)S(1)}, bf16[12,96,384]{2,1,0:T(8,128)(2,1)S(1)}, u32[]{:S(2)}, u32[]{:S(2)}) collective-permute-start(bf16[12,96,384]{2,1,0:T(8,128)(2,1)S(1)} %get-tuple-element.41), channel_id=1, source_target_pairs={{8,0},{16,24},{9,1},{17,25},{10,2},{18,26},{11,3},{19,27},{12,4},{... | collective-permute-start | bytes 2654216 | tf_op jit(solution)/shard_map/ppermute | solution.py:22
  100.6 20.5 %collective-permute-start.20 = (bf16[3,32,3144]{2,1,0:T(8,128)(2,1)S(1)}, bf16[3,32,3144]{2,1,0:T(8,128)(2,1)S(1)}, u32[]{:S(2)}, u32[]{:S(2)}) collective-permute-start(bf16[3,32,3144]{2,1,0:T(8,128)(2,1)S(1)} %pad_maximum_fusion), channel_id=1, source_target_pairs={{0,8},{24,16},{1,9},{25,17},{2,10},{26,18},{3,11},{27,19},{4,12},{... | collective-permute-start | bytes 1810952 | tf_op jit(solution)/shard_map/ppermute | solution.py:22
  105.0 40.0 %collective-permute-start.13 = (bf16[1536,384]{1,0:T(8,128)(2,1)}, bf16[1536,384]{1,0:T(8,128)(2,1)S(1)}, u32[]{:S(2)}, u32[]{:S(2)}) collective-permute-start(bf16[1536,384]{1,0:T(8,128)(2,1)} %collective-permute-done.11.refs_2_), channel_id=1, source_target_pairs={{8,16},{16,8},{9,17},{17,9},{10,18},{18,10},{11,19},{19,11},{12,20... | collective-permute-start | bytes 3538952 | tf_op jit(solution)/shard_map/ppermute | solution.py:22
  105.8 40.9 %collective-permute-start.12 = (bf16[1608,384]{1,0:T(8,128)(2,1)}, bf16[1608,384]{1,0:T(8,128)(2,1)}, u32[]{:S(2)}, u32[]{:S(2)}) collective-permute-start(bf16[1608,384]{1,0:T(8,128)(2,1)} %collective-permute-done.10.refs_1_), channel_id=1, source_target_pairs={{8,0},{16,24},{9,1},{17,25},{10,2},{18,26},{11,3},{19,27},{12,4},{... | collective-permute-start | bytes 3704840 | tf_op jit(solution)/shard_map/ppermute | solution.py:22
  118.6 24.8 %collective-permute-start.14 = (bf16[1608,384]{1,0:T(8,128)(2,1)S(1)}, bf16[1608,384]{1,0:T(8,128)(2,1)}, u32[]{:S(2)}, u32[]{:S(2)}) collective-permute-start(bf16[1608,384]{1,0:T(8,128)(2,1)S(1)} %shard_map.176), channel_id=1, source_target_pairs={{0,8},{24,16},{1,9},{25,17},{2,10},{26,18},{3,11},{27,19},{4,12},{... | collective-permute-start | bytes 3704840 | tf_op jit(solution)/shard_map/ppermute | solution.py:22
  121.9 23.2 %all-to-all-start = ((bf16[4,96,1152]{2,1,0:T(8,128)(2,1)}), bf16[4,96,1152]{2,1,0:T(8,128)(2,1)S(1)}, u32[]{:S(2)}, u32[]{:S(2)}) async-start(bf16[4,96,1152]{2,1,0:T(8,128)(2,1)} %shard_map.174.refs_1_.refs_4_), calls=%async_computation | async-start | bytes 1769472 | tf_op jit(solution)/shard_map/all_to_all | solution.py:450
  129.1 26.3 %collective-permute-start.21 = (bf16[2,32,3144]{2,1,0:T(8,128)(2,1)}, bf16[2,32,3144]{2,1,0:T(8,128)(2,1)}, u32[]{:S(2)}, u32[]{:S(2)}) collective-permute-start(bf16[2,32,3144]{2,1,0:T(8,128)(2,1)} %pad_maximum_fusion.2), channel_id=1, source_target_pairs={{8,16},{16,8},{9,17},{17,9},{10,18},{18,10},{11,19},{19,11},{12,20... | collective-permute-start | bytes 1207304 | tf_op jit(solution)/shard_map/ppermute | solution.py:22
  143.4 34.1 %collective-permute-start.17 = (bf16[1608,384]{1,0:T(8,128)(2,1)}, bf16[1608,384]{1,0:T(8,128)(2,1)}, u32[]{:S(2)}, u32[]{:S(2)}) collective-permute-start(bf16[1608,384]{1,0:T(8,128)(2,1)} %collective-permute-done.14.refs_2_), channel_id=1, source_target_pairs={{8,16},{16,8},{9,17},{17,9},{10,18},{18,10},{11,19},{19,11},{12,20... | collective-permute-start | bytes 3704840 | tf_op jit(solution)/shard_map/ppermute | solution.py:22
  145.1 32.4 %collective-permute-start.23 = (bf16[1536,384]{1,0:T(8,128)(2,1)S(1)}, bf16[1536,384]{1,0:T(8,128)(2,1)}, u32[]{:S(2)}, u32[]{:S(2)}) collective-permute-start(bf16[1536,384]{1,0:T(8,128)(2,1)S(1)} %shard_map.175.refs_1_), channel_id=1, source_target_pairs={{8,0},{16,24},{9,1},{17,25},{10,2},{18,26},{11,3},{19,27},{12,4},{... | collective-permute-start | bytes 3538952 | tf_op jit(solution)/shard_map/ppermute | solution.py:22
  151.7 16.3 %all-to-all-start.1 = ((bf16[4,96,1152]{2,1,0:T(8,128)(2,1)}), bf16[4,96,1152]{2,1,0:T(8,128)(2,1)S(1)}, u32[]{:S(2)}, u32[]{:S(2)}) async-start(bf16[4,96,1152]{2,1,0:T(8,128)(2,1)} %get-tuple-element.42.refs_2_), calls=%async_computation.1 | async-start | bytes 1769472 | tf_op jit(solution)/shard_map/all_to_all | solution.py:458
  157.9 19.6 %collective-permute-start.22 = (bf16[32,3144]{1,0:T(8,128)(2,1)}, bf16[32,3144]{1,0:T(8,128)(2,1)}, u32[]{:S(2)}, u32[]{:S(2)}) collective-permute-start(bf16[32,3144]{1,0:T(8,128)(2,1)} %shard_map.182), channel_id=1, source_target_pairs={{8,0},{16,24},{9,1},{17,25},{10,2},{18,26},{11,3},{19,27},{12,4},{... | collective-permute-start | bytes 603656 | tf_op jit(solution)/shard_map/ppermute | solution.py:22
  181.7 20.9 %collective-permute-start.15 = (bf16[12,96,384]{2,1,0:T(8,128)(2,1)S(1)}, bf16[12,96,384]{2,1,0:T(8,128)(2,1)S(1)}, u32[]{:S(2)}, u32[]{:S(2)}) collective-permute-start(bf16[12,96,384]{2,1,0:T(8,128)(2,1)S(1)} %shard_map.178.refs_4_.refs_0_.refs_1_), channel_id=1, source_target_pairs={{0,8},{24,16},{8,0},{16,24},{1,9},{25,17},{9,1},{17,25},{2,10},{26... | collective-permute-start | bytes 2654216 | tf_op jit(solution)/shard_map/ppermute | solution.py:22
  202.7 13.5 %collective-permute-start.26 = (bf16[32,3144]{1,0:T(8,128)(2,1)S(1)}, bf16[32,3144]{1,0:T(8,128)(2,1)}, u32[]{:S(2)}, u32[]{:S(2)}) collective-permute-start(bf16[32,3144]{1,0:T(8,128)(2,1)S(1)} %shard_map.184), channel_id=1, source_target_pairs={{0,16},{8,24},{16,0},{24,8},{1,17},{9,25},{17,1},{25,9},{2,18},{10... | collective-permute-start | bytes 603656 | tf_op jit(solution)/shard_map/ppermute | solution.py:22
  204.4 12.3 %collective-permute-start.27 = (bf16[32,3144]{1,0:T(8,128)(2,1)S(1)}, bf16[32,3144]{1,0:T(8,128)(2,1)}, u32[]{:S(2)}, u32[]{:S(2)}) collective-permute-start(bf16[32,3144]{1,0:T(8,128)(2,1)S(1)} %shard_map.184), channel_id=1, source_target_pairs={{0,24},{8,0},{16,8},{24,16},{1,25},{9,1},{17,9},{25,17},{2,26},{10... | collective-permute-start | bytes 603656 | tf_op jit(solution)/shard_map/ppermute | solution.py:22
  207.4 18.5 %collective-permute-start.30 = (bf16[12,96,384]{2,1,0:T(8,128)(2,1)S(1)}, bf16[12,96,384]{2,1,0:T(8,128)(2,1)S(1)}, u32[]{:S(2)}, u32[]{:S(2)}) collective-permute-start(bf16[12,96,384]{2,1,0:T(8,128)(2,1)S(1)} %shard_map.178.refs_4_.refs_0_.refs_1_), channel_id=1, source_target_pairs={{8,16},{16,8},{9,17},{17,9},{10,18},{18,10},{11,19},{19,11},{12,20... | collective-permute-start | bytes 2654216 | tf_op jit(solution)/shard_map/ppermute | solution.py:22
  208.1 34.9 %collective-permute-start.18 = (bf16[1608,384]{1,0:T(8,128)(2,1)}, bf16[1608,384]{1,0:T(8,128)(2,1)S(1)}, u32[]{:S(2)}, u32[]{:S(2)}) collective-permute-start(bf16[1608,384]{1,0:T(8,128)(2,1)} %collective-permute-done.17.refs_6_), channel_id=1, source_target_pairs={{8,0},{16,24},{9,1},{17,25},{10,2},{18,26},{11,3},{19,27},{12,4},{... | collective-permute-start | bytes 3704840 | tf_op jit(solution)/shard_map/ppermute | solution.py:22
  218.0 10.2 %collective-permute-start.28 = (bf16[3,32,3144]{2,1,0:T(8,128)(2,1)S(1)}, bf16[3,32,3144]{2,1,0:T(8,128)(2,1)S(1)}, u32[]{:S(2)}, u32[]{:S(2)}) collective-permute-start(bf16[3,32,3144]{2,1,0:T(8,128)(2,1)S(1)} %pad_maximum_fusion.1), channel_id=1, source_target_pairs={{0,1},{1,0},{2,3},{3,2},{4,5},{5,4},{6,7},{7,6},{8,9},{9,8},{10,11... | collective-permute-start | bytes 1810952 | tf_op jit(solution)/shard_map/ppermute | solution.py:485
  225.2 8.2 %collective-permute-start.16 = (bf16[12,96,384]{2,1,0:T(8,128)(2,1)S(1)}, bf16[12,96,384]{2,1,0:T(8,128)(2,1)S(1)}, u32[]{:S(2)}, u32[]{:S(2)}) collective-permute-start(bf16[12,96,384]{2,1,0:T(8,128)(2,1)S(1)} %collective-permute-done.15.refs_0_.refs_1_), channel_id=1, source_target_pairs={{8,16},{16,8},{9,17},{17,9},{10,18},{18,10},{11,19},{19,11},{12,20... | collective-permute-start | bytes 2654216 | tf_op jit(solution)/shard_map/ppermute | solution.py:22
  225.9 36.1 %collective-permute-start.31 = (bf16[12,96,384]{2,1,0:T(8,128)(2,1)S(1)}, bf16[12,96,384]{2,1,0:T(8,128)(2,1)S(1)}, u32[]{:S(2)}, u32[]{:S(2)}) collective-permute-start(bf16[12,96,384]{2,1,0:T(8,128)(2,1)S(1)} %collective-permute-done.30.refs_1_), channel_id=1, source_target_pairs={{8,0},{16,24},{9,1},{17,25},{10,2},{18,26},{11,3},{19,27},{12,4},{... | collective-permute-start | bytes 2654216 | tf_op jit(solution)/shard_map/ppermute | solution.py:22
  243.1 32.4 %collective-permute-start.29 = (bf16[12,96,384]{2,1,0:T(8,128)(2,1)S(1)}, bf16[12,96,384]{2,1,0:T(8,128)(2,1)S(1)}, u32[]{:S(2)}, u32[]{:S(2)}) collective-permute-start(bf16[12,96,384]{2,1,0:T(8,128)(2,1)S(1)} %shard_map.185.refs_1_), channel_id=1, source_target_pairs={{8,0},{16,24},{9,1},{17,25},{10,2},{18,26},{11,3},{19,27},{12,4},{... | collective-permute-start | bytes 2654216 | tf_op jit(solution)/shard_map/ppermute | solution.py:22
  (26 other events, 197.7 us)
